TPU v7x, 256 devices: a whole 4x4x8 slice. The times are simulated.
256 devices in a mesh: dp: 2 (over x_lo), mp: 128 (over x_hi, z, y, core).
Axes of the slice: x: 4 (x_hi: 2, x_lo: 2; x = x_hi * 2 + x_lo), y: 4, z: 8, core: 2. Of those that a mesh axis runs over, the one named last changes fastest.
Arguments:
- inputs: bfloat16 [1024, 8192], P('dp', 'mp'), may hold values from -6 to 6
- cotangent: bfloat16 [1024, 8192], P('dp', 'mp'), may hold values from -6 to 6
- up_blocks: bfloat16 [128, 6, 256, 256], P('mp'), may hold values from -0.15625 to 0.15625
- down_blocks: bfloat16 [128, 6, 256, 256], P('mp'), may hold values from -0.078125 to 0.078125
- up_left: bfloat16 [8192, 256], P('mp'), may hold values from -0.0625 to 0.0625
- up_right: bfloat16 [256, 32768], P(None, 'mp'), may hold values from -0.375 to 0.375
- down_left: bfloat16 [32768, 256], P('mp'), may hold values from -0.03125 to 0.03125
- down_right: bfloat16 [256, 8192], P(None, 'mp'), may hold values from -0.375 to 0.375
Outputs:
- outputs: bfloat16 [1024, 8192], P('dp', 'mp')
- grad_inputs: bfloat16 [1024, 8192], P('dp', 'mp')
- grad_up_blocks: bfloat16 [128, 6, 256, 256], P('mp')
- grad_down_blocks: bfloat16 [128, 6, 256, 256], P('mp')
- grad_up_left: bfloat16 [8192, 256], P('mp')
- grad_up_right: bfloat16 [256, 32768], P(None, 'mp')
- grad_down_left: bfloat16 [32768, 256], P('mp')
- grad_down_right: bfloat16 [256, 8192], P(None, 'mp')
All inputs are finite; a program needn't handle non-finite values.
Results may differ from a plain program's by a relative error of at most 0.013.
Values may be sent and summed in bfloat16 or wider, within the bound.
No kernel may reach another device: no remote copies, remote signals or barrier semaphores. Data moves between devices by JAX's collectives and lax.ppermute only.
A program may use at most 64 MiB of HBM per device.

v0:
```python
from functools import partial

import jax
import jax.numpy as jnp
from jax import lax
from jax.sharding import PartitionSpec as P


def swapped(block, axis, bit):
    count = lax.axis_size(axis)
    route = []
    for low in range(count):
        high = low | 1 << bit
        if high != low and high < count:
            route += [(low, high), (high, low)]
    return lax.ppermute(block, axis, route)


def bit_value(which_bit):
    return lax.axis_index("mp") >> which_bit & 1


def flip_on(array, axis, stride):
    shape = array.shape
    count = shape[axis]
    paired = array.reshape(shape[:axis] + (count // (2 * stride), 2, stride) + shape[axis + 1 :])
    return jnp.flip(paired, axis=axis + 1).reshape(shape)


def route_rows(blocks, height):
    local_count = blocks.shape[1]
    return swapped(blocks, "mp", height - (local_count.bit_length() - 1))


def route_terms(blocks, height):
    local_count = blocks.shape[1]
    if 1 << height < local_count:
        return flip_on(blocks, 1, 1 << height)
    return swapped(
        blocks.astype(jnp.bfloat16), "mp", height - (local_count.bit_length() - 1)
    ).astype(blocks.dtype)


def partners(blocks, height_count):
    return [blocks] + [route_rows(blocks, height) for height in range(height_count)]


def routed_sum(activation, weights, form, term_count, shape):
    accumulated = jnp.zeros(shape, jnp.float32)
    for member in range(term_count):
        if member == 0:
            accumulated = accumulated + jnp.einsum(
                form, activation, weights[:, 0], preferred_element_type=jnp.float32
            )
        else:
            contribution = jnp.einsum(
                form, activation, weights[:, member], preferred_element_type=jnp.float32
            )
            accumulated = accumulated + route_terms(contribution, member - 1)
    return accumulated


def assemble(local_piece, block_width):
    top_bit = lax.axis_size("mp").bit_length() - 1
    joined = local_piece
    for which_bit in (top_bit - 2, top_bit - 1):
        partner = swapped(joined, "mp", which_bit)
        low_half = bit_value(which_bit) == 0
        joined = jnp.where(
            low_half, jnp.stack([joined, partner], axis=1), jnp.stack([partner, joined], axis=1)
        )
    row_count = local_piece.shape[0]
    local_count = local_piece.shape[1] * 4 // block_width
    joined = joined.reshape(row_count, 4, local_count, block_width // 4)
    return joined.transpose(0, 2, 1, 3).reshape(row_count, local_count, block_width)


def reduce_quarters(sums):
    row_count, local_count, block_width = sums.shape
    halves = sums.reshape(row_count, local_count, 4, block_width // 4).transpose(0, 2, 1, 3)
    halves = halves.reshape(row_count, 2, 2, local_count * block_width // 4)
    top_bit = lax.axis_size("mp").bit_length() - 1
    for which_bit in (top_bit - 1, top_bit - 2):
        low_half = bit_value(which_bit) == 0
        keeping = jnp.where(low_half, halves[:, 0], halves[:, 1])
        sending = jnp.where(low_half, halves[:, 1], halves[:, 0])
        halves = keeping + swapped(sending.astype(jnp.bfloat16), "mp", which_bit).astype(
            sending.dtype
        )
    return halves


def shards(inputs, cotangent, up_blocks, down_blocks, up_left, up_right, down_left, down_right):
    row_count = inputs.shape[0]
    local_count = up_blocks.shape[0]
    term_count = up_blocks.shape[1]
    block_width = up_blocks.shape[2]
    height_count = term_count - 1
    block_shape = (row_count, local_count, block_width)
    gelu_tanh = partial(jax.nn.gelu, approximate=True)
    input_rows = partners(assemble(inputs, block_width), height_count)
    input_rank = lax.psum(
        jnp.dot(inputs, up_left, preferred_element_type=jnp.float32), "mp"
    ).astype(jnp.bfloat16)
    result = jnp.dot(input_rank, up_right, preferred_element_type=jnp.float32).reshape(block_shape)
    for preact_member in range(term_count):
        result = result + jnp.einsum(
            "tkc,kcd->tkd",
            input_rows[preact_member],
            up_blocks[:, preact_member],
            preferred_element_type=jnp.float32,
        )
    hidden = gelu_tanh(result).astype(jnp.bfloat16)
    flat_hidden = hidden.reshape(row_count, -1)
    hidden_rank = lax.psum(
        jnp.dot(flat_hidden, down_left, preferred_element_type=jnp.float32), "mp"
    ).astype(jnp.bfloat16)
    accumulated = routed_sum(hidden, down_blocks, "tkc,kcd->tkd", term_count, block_shape)
    outputs = (
        reduce_quarters(accumulated)
        + jnp.dot(hidden_rank, down_right, preferred_element_type=jnp.float32)
    ).astype(jnp.bfloat16)
    cot_rows = partners(assemble(cotangent, block_width), height_count)
    cot_rank = lax.psum(
        jnp.dot(cotangent, down_right.T, preferred_element_type=jnp.float32), "mp"
    ).astype(jnp.bfloat16)
    grad_hidden = jnp.dot(cot_rank, down_left.T, preferred_element_type=jnp.float32).reshape(
        block_shape
    )
    weight_down = []
    for member in range(term_count):
        grad_hidden = grad_hidden + jnp.einsum(
            "tkd,kcd->tkc",
            cot_rows[member],
            down_blocks[:, member],
            preferred_element_type=jnp.float32,
        )
        weight_down.append(
            jnp.einsum("tkc,tkd->kcd", hidden, cot_rows[member], preferred_element_type=jnp.float32)
        )
    grad_preact = jax.vjp(gelu_tanh, result)[1](grad_hidden)[0].astype(jnp.bfloat16)
    flat_grad = grad_preact.reshape(row_count, -1)
    back_rank = lax.psum(
        jnp.dot(flat_grad, up_right.T, preferred_element_type=jnp.float32), "mp"
    ).astype(jnp.bfloat16)
    accumulated = routed_sum(grad_preact, up_blocks, "tkd,kcd->tkc", term_count, block_shape)
    weight_up = []
    for member in range(term_count):
        weight_up.append(
            jnp.einsum(
                "tkc,tkd->kcd", input_rows[member], grad_preact, preferred_element_type=jnp.float32
            )
        )
    grad_inputs = (
        reduce_quarters(accumulated)
        + jnp.dot(back_rank, up_left.T, preferred_element_type=jnp.float32)
    ).astype(jnp.bfloat16)
    summed = (
        lax.psum(jnp.stack(weight_up, axis=1).astype(jnp.bfloat16), "dp").astype(jnp.float32),
        lax.psum(jnp.stack(weight_down, axis=1).astype(jnp.bfloat16), "dp").astype(jnp.float32),
        lax.psum(
            jnp.dot(inputs.T, back_rank, preferred_element_type=jnp.float32).astype(jnp.bfloat16),
            "dp",
        ).astype(jnp.float32),
        lax.psum(
            jnp.dot(input_rank.T, flat_grad, preferred_element_type=jnp.float32).astype(
                jnp.bfloat16
            ),
            "dp",
        ).astype(jnp.float32),
        lax.psum(
            jnp.dot(flat_hidden.T, cot_rank, preferred_element_type=jnp.float32).astype(
                jnp.bfloat16
            ),
            "dp",
        ).astype(jnp.float32),
        lax.psum(
            jnp.dot(hidden_rank.T, cotangent, preferred_element_type=jnp.float32).astype(
                jnp.bfloat16
            ),
            "dp",
        ).astype(jnp.float32),
    )
    return (outputs, grad_inputs) + tuple((gradient.astype(jnp.bfloat16) for gradient in summed))


def solution(mesh):
    placed = (
        P("dp", "mp"),
        P("dp", "mp"),
        P("mp", None, None, None),
        P("mp", None, None, None),
        P("mp", None),
        P(None, "mp"),
        P("mp", None),
        P(None, "mp"),
    )
    return jax.shard_map(
        shards,
        mesh=mesh,
        in_specs=placed,
        out_specs=(
            P("dp", "mp"),
            P("dp", "mp"),
            P("mp", None, None, None),
            P("mp", None, None, None),
            P("mp", None),
            P(None, "mp"),
            P("mp", None),
            P(None, "mp"),
        ),
        check_vma=False,
    )
```

profile of v0, /device:TPU:32, one launch (start us, length us, event | category | flops | bytes accessed | tf_op | source)
XLA Modules:
  0.0 1509.5 jit_solution(9112240839596329677)
XLA Ops:
  7.3 6.4 collective-permute-start
  15.1 631.8 %all-reduce.12 = (bf16[512,256]{1,0:T(8,128)(2,1)S(1)}, bf16[512,256]{1,0:T(8,128)(2,1)S(1)}) all-reduce(f32[512,256]{1,0:T(8,128)S(1)} %fusion.160, f32[512,256]{1,0:T(8,128)S(1)} %fusion.161), channel_id=1, replica_groups=mesh['dp'=2,'mp'=128] {'mp'}, use_global_device_ids=true, to_apply=%region_0.1 | all-reduce | flops 262144 | bytes 1572864 | tf_op jit(solution)/shard_map/psum | solution.py:102
  647.6 3.1 collective-permute-start.15
  650.8 2.8 collective-permute-done.1
  653.6 28.2 %collective-permute-start.5 = (bf16[512,1,256]{0,2,1:T(8,128)(2,1)S(1)}, bf16[512,1,256]{0,2,1:T(8,128)(2,1)S(1)}, u32[]{:S(2)}, u32[]{:S(2)}) collective-permute-start(bf16[512,1,256]{0,2,1:T(8,128)(2,1)S(1)} %bitcast.461), channel_id=1, source_target_pairs={{0,8},{8,0},{1,9},{9,1},{2,10},{10,2},{3,11},{11,3},{4,12},{12,4},... | collective-permute-start | bytes 786440 | tf_op jit(solution)/shard_map/ppermute | solution.py:16
  684.5 2.4 collective-permute-done.5
  687.1 2.5 collective-permute-done.4
  691.1 8.7 collective-permute-done.20
  699.8 3.1 collective-permute-start.18
  705.1 5.4 collective-permute-done.18
  711.2 4.9 collective-permute-done.17
  727.9 627.9 %all-reduce.13 = (bf16[512,256]{1,0:T(8,128)(2,1)}, bf16[512,256]{1,0:T(8,128)(2,1)}) all-reduce(f32[512,256]{1,0:T(8,128)S(1)} %fusion.72, f32[512,256]{1,0:T(8,128)S(1)} %fusion.162), channel_id=1, replica_groups=mesh['dp'=2,'mp'=128] {'mp'}, use_global_device_ids=true, to_apply=%region_1.2 | all-reduce | flops 262144 | bytes 1572864 | tf_op jit(solution)/shard_map/psum | solution.py:115
  1355.9 1.8 fusion.46
  1362.6 28.1 %collective-permute-start.24 = (bf16[512,1,256]{0,2,1:T(8,128)(2,1)}, bf16[512,1,256]{0,2,1:T(8,128)(2,1)}, u32[]{:S(2)}, u32[]{:S(2)}) collective-permute-start(bf16[512,1,256]{0,2,1:T(8,128)(2,1)} %fusion.20), channel_id=1, source_target_pairs={{0,8},{8,0},{1,9},{9,1},{2,10},{10,2},{3,11},{11,3},{4,12},{12,4},... | collective-permute-start | bytes 786440 | tf_op jit(solution)/shard_map/ppermute | solution.py:16
  1401.3 2.9 collective-permute-start.11
  1404.2 2.0 collective-permute-start.8
  1406.3 4.1 collective-permute-start.9
  1412.0 3.0 collective-permute-done.10
  1416.5 6.1 collective-permute-done.9
  1423.9 5.7 collective-permute-done.12
  1430.0 2.8 collective-permute-done.27
  1433.5 4.6 collective-permute-done.13
  1438.7 58.0 %all-reduce.11.cloned.1.call-done = (bf16[1,6,256,256]{3,2,1,0:T(8,128)(2,1)}, bf16[1,6,256,256]{3,2,1,0:T(8,128)(2,1)}, bf16[256,256]{1,0:T(8,128)(2,1)}, bf16[256,256]{1,0:T(8,128)(2,1)}) async-done(((bf16[1,6,256,256]{3,2,1,0:T(8,128)(2,1)}, bf16[1,6,256,256]{3,2,1,0:T(8,128)(2,1)}, bf16[256,256]{1,0:T(8,128)(2,1)}, bf16[256,256]{1,0:T(8,128)(2,1)}), (bf16[1,6,256,256]{3,2,1,0:T(8,128)(2,1)}, ...) | async-done | bytes 1835024 | tf_op jit(solution)/shard_map/psum | solution.py:159
  1496.7 2.1 copy.60
  (186 shorter events, 46.5 us)
Async XLA Ops:
  7.2 1431.5 %all-reduce.9.cloned.1.call-start = ((), (), s32[]{:S(2)}) async-start(), calls=%async_computation | async-start | bytes 131072 | tf_op jit(solution)/shard_map/psum | solution.py:161
  7.3 639.7 %collective-permute-start = (bf16[512,64]{0,1:T(8,128)(2,1)}, bf16[512,64]{0,1:T(8,128)(2,1)S(1)}, u32[]{:S(2)}, u32[]{:S(2)}) collective-permute-start(bf16[512,64]{0,1:T(8,128)(2,1)} %param.8), channel_id=1, source_target_pairs={{0,32},{32,0},{1,33},{33,1},{2,34},{34,2},{3,35},{35,3},{4,36},{36... | collective-permute-start | bytes 196616 | tf_op jit(solution)/shard_map/ppermute | solution.py:16
  13.6 634.0 %collective-permute-start.14 = (bf16[512,64]{0,1:T(8,128)(2,1)}, bf16[512,64]{0,1:T(8,128)(2,1)S(1)}, u32[]{:S(2)}, u32[]{:S(2)}) collective-permute-start(bf16[512,64]{0,1:T(8,128)(2,1)} %param.9), channel_id=1, source_target_pairs={{0,32},{32,0},{1,33},{33,1},{2,34},{34,2},{3,35},{35,3},{4,36},{36... | collective-permute-start | bytes 196616 | tf_op jit(solution)/shard_map/ppermute | solution.py:16
  647.6 34.4 %collective-permute-start.15 = (bf16[512,2,64]{0,2,1:T(8,128)(2,1)S(1)}, bf16[512,2,64]{0,2,1:T(8,128)(2,1)S(1)}, u32[]{:S(2)}, u32[]{:S(2)}) collective-permute-start(bf16[512,2,64]{0,2,1:T(8,128)(2,1)S(1)} %maximum_select_fusion.5), channel_id=1, source_target_pairs={{0,64},{64,0},{1,65},{65,1},{2,66},{66,2},{3,67},{67,3},{4,68},{68... | collective-permute-start | bytes 393224 | tf_op jit(solution)/shard_map/ppermute | solution.py:16
  653.6 33.3 %collective-permute-start.5 = (bf16[512,1,256]{0,2,1:T(8,128)(2,1)S(1)}, bf16[512,1,256]{0,2,1:T(8,128)(2,1)S(1)}, u32[]{:S(2)}, u32[]{:S(2)}) collective-permute-start(bf16[512,1,256]{0,2,1:T(8,128)(2,1)S(1)} %bitcast.461), channel_id=1, source_target_pairs={{0,8},{8,0},{1,9},{9,1},{2,10},{10,2},{3,11},{11,3},{4,12},{12,4},... | collective-permute-start | bytes 786440 | tf_op jit(solution)/shard_map/ppermute | solution.py:16
  681.8 35.0 %collective-permute-start.6 = (bf16[512,1,256]{0,2,1:T(8,128)(2,1)S(1)}, bf16[512,1,256]{0,2,1:T(8,128)(2,1)S(1)}, u32[]{:S(2)}, u32[]{:S(2)}) collective-permute-start(bf16[512,1,256]{0,2,1:T(8,128)(2,1)S(1)} %bitcast.464), channel_id=1, source_target_pairs={{0,16},{16,0},{1,17},{17,1},{2,18},{18,2},{3,19},{19,3},{4,20},{20... | collective-permute-start | bytes 786440 | tf_op jit(solution)/shard_map/ppermute | solution.py:16
  682.1 35.4 %collective-permute-start.2 = (bf16[512,1,256]{0,2,1:T(8,128)(2,1)S(1)}, bf16[512,1,256]{0,2,1:T(8,128)(2,1)S(1)}, u32[]{:S(2)}, u32[]{:S(2)}) collective-permute-start(bf16[512,1,256]{0,2,1:T(8,128)(2,1)S(1)} %bitcast.466), channel_id=1, source_target_pairs={{0,1},{1,0},{2,3},{3,2},{4,5},{5,4},{6,7},{7,6},{8,9},{9,8},{10,11... | collective-permute-start | bytes 786440 | tf_op jit(solution)/shard_map/ppermute | solution.py:16
  686.9 31.3 %collective-permute-start.16 = (bf16[512,1,256]{0,2,1:T(8,128)(2,1)S(1)}, bf16[512,1,256]{0,2,1:T(8,128)(2,1)S(1)}, u32[]{:S(2)}, u32[]{:S(2)}) collective-permute-start(bf16[512,1,256]{0,2,1:T(8,128)(2,1)S(1)} %bitcast.469), channel_id=1, source_target_pairs={{0,1},{1,0},{2,3},{3,2},{4,5},{5,4},{6,7},{7,6},{8,9},{9,8},{10,11... | collective-permute-start | bytes 786440 | tf_op jit(solution)/shard_map/ppermute | solution.py:16
  689.6 10.1 collective-permute-start.20
  690.3 12.8 collective-permute-start.19
  699.8 10.7 collective-permute-start.18
  703.1 12.9 collective-permute-start.17
  1362.6 38.5 %collective-permute-start.21 = (bf16[512,1,256]{0,2,1:T(8,128)(2,1)}, bf16[512,1,256]{0,2,1:T(8,128)(2,1)}, u32[]{:S(2)}, u32[]{:S(2)}) collective-permute-start(bf16[512,1,256]{0,2,1:T(8,128)(2,1)} %fusion.17), channel_id=1, source_target_pairs={{0,1},{1,0},{2,3},{3,2},{4,5},{5,4},{6,7},{7,6},{8,9},{9,8},{10,11... | collective-permute-start | bytes 786440 | tf_op jit(solution)/shard_map/ppermute | solution.py:16
  1362.6 38.7 %collective-permute-start.22 = (bf16[512,1,256]{0,2,1:T(8,128)(2,1)}, bf16[512,1,256]{0,2,1:T(8,128)(2,1)}, u32[]{:S(2)}, u32[]{:S(2)}) collective-permute-start(bf16[512,1,256]{0,2,1:T(8,128)(2,1)} %fusion.18), channel_id=1, source_target_pairs={{0,2},{2,0},{1,3},{3,1},{4,6},{6,4},{5,7},{7,5},{8,10},{10,8},{9,1... | collective-permute-start | bytes 786440 | tf_op jit(solution)/shard_map/ppermute | solution.py:16
  1362.6 41.6 %collective-permute-start.23 = (bf16[512,1,256]{0,2,1:T(8,128)(2,1)}, bf16[512,1,256]{0,2,1:T(8,128)(2,1)}, u32[]{:S(2)}, u32[]{:S(2)}) collective-permute-start(bf16[512,1,256]{0,2,1:T(8,128)(2,1)} %fusion.19), channel_id=1, source_target_pairs={{0,4},{4,0},{1,5},{5,1},{2,6},{6,2},{3,7},{7,3},{8,12},{12,8},{9,1... | collective-permute-start | bytes 786440 | tf_op jit(solution)/shard_map/ppermute | solution.py:16
  1362.6 41.6 %collective-permute-start.24 = (bf16[512,1,256]{0,2,1:T(8,128)(2,1)}, bf16[512,1,256]{0,2,1:T(8,128)(2,1)}, u32[]{:S(2)}, u32[]{:S(2)}) collective-permute-start(bf16[512,1,256]{0,2,1:T(8,128)(2,1)} %fusion.20), channel_id=1, source_target_pairs={{0,8},{8,0},{1,9},{9,1},{2,10},{10,2},{3,11},{11,3},{4,12},{12,4},... | collective-permute-start | bytes 786440 | tf_op jit(solution)/shard_map/ppermute | solution.py:16
  1390.7 15.5 %collective-permute-start.25 = (bf16[512,1,256]{0,2,1:T(8,128)(2,1)}, bf16[512,1,256]{0,2,1:T(8,128)(2,1)}, u32[]{:S(2)}, u32[]{:S(2)}) collective-permute-start(bf16[512,1,256]{0,2,1:T(8,128)(2,1)} %fusion.21), channel_id=1, source_target_pairs={{0,16},{16,0},{1,17},{17,1},{2,18},{18,2},{3,19},{19,3},{4,20},{20... | collective-permute-start | bytes 786440 | tf_op jit(solution)/shard_map/ppermute | solution.py:16
  1390.8 105.9 %all-reduce.11.cloned.1.call-start = ((), (), s32[]{:S(2)}) async-start(), calls=%async_computation.1 | async-start | bytes 3670016 | tf_op jit(solution)/shard_map/psum | solution.py:159
  1401.1 13.9 collective-permute-start.10
  1401.3 15.2 %collective-permute-start.11 = (bf16[512,1,256]{0,2,1:T(8,128)(2,1)}, bf16[512,1,256]{0,2,1:T(8,128)(2,1)S(1)}, u32[]{:S(2)}, u32[]{:S(2)}) collective-permute-start(bf16[512,1,256]{0,2,1:T(8,128)(2,1)} %fusion.16), channel_id=1, source_target_pairs={{0,16},{16,0},{1,17},{17,1},{2,18},{18,2},{3,19},{19,3},{4,20},{20... | collective-permute-start | bytes 786440 | tf_op jit(solution)/shard_map/ppermute | solution.py:16
  1404.2 12.3 collective-permute-start.7
  1404.2 12.2 collective-permute-start.8
  1406.3 16.4 %collective-permute-start.9 = (bf16[512,1,256]{0,2,1:T(8,128)(2,1)}, bf16[512,1,256]{0,2,1:T(8,128)(2,1)S(1)}, u32[]{:S(2)}, u32[]{:S(2)}) collective-permute-start(bf16[512,1,256]{0,2,1:T(8,128)(2,1)} %fusion.14), channel_id=1, source_target_pairs={{0,4},{4,0},{1,5},{5,1},{2,6},{6,2},{3,7},{7,3},{8,12},{12,8},{9,1... | collective-permute-start | bytes 786440 | tf_op jit(solution)/shard_map/ppermute | solution.py:16
  1423.8 9.0 collective-permute-start.27
  (45 other events, 1473.6 us)
Sparse Core Ops, SparseCore 0:
  1390.9 31.9 all-reduce.8
  1426.2 70.4 all-reduce.10
where the time goes:
time: 1510 us
  blocking collectives  1260 us (83%)
  waiting for transfers between devices  108 us (7%)
  starting transfers between devices  82.4 us (5%)
  matrix products  30.1 us (2%)
    psum x1, blocking collectives, shards(): lax.psum(jnp.dot(inputs, up_left, preferred_element_type=jnp.float32), 'mp')  632 us
    psum x1, blocking collectives, shards(): lax.psum(jnp.dot(flat_hidden, down_left, preferred_element_type=jnp.float...  628 us
    ppermute x28, starting transfers between devices, swapped(): return lax.ppermute(block, axis, route)  82.3 us
    psum x1, waiting for transfers between devices, shards(): lax.psum(jnp.stack(weight_up, axis=1).astype(jnp.bfloat16), 'dp')  58 us
    ppermute x28, waiting for transfers between devices, swapped(): return lax.ppermute(block, axis, route)  49.8 us
  transfers between devices with their start and end apart: 30, of which 13 were waited for; matrix products, arithmetic and copies ran while one was open for 1% of the time, Pallas kernels for 0%

commit v1 on v0

v1 whole, which is shorter than its diff:
```python
from functools import partial

import jax
import jax.numpy as jnp
from jax import lax
from jax.sharding import PartitionSpec as P

BF = jnp.bfloat16
F32 = jnp.float32

Z_NEAR = (7, 2, 1, 4, 3, 6, 5, 0)
Z_FAR = (3, 6, 5, 0, 7, 2, 1, 4)


def by_mask(mask):
    return [(i, i ^ mask) for i in range(128)]


def by_z(table):
    return [(i, (i & 0b1000111) | table[i >> 3 & 7] << 3) for i in range(128)]


def send(value, route):
    return lax.ppermute(value, "mp", route)


def swapped_dp(value):
    return lax.ppermute(value, "dp", [(0, 1), (1, 0)])


def dp_sum(value):
    mine = value.astype(BF)
    return (mine.astype(F32) + swapped_dp(mine).astype(F32)).astype(BF)


def mp_sum(partial_sums):
    index = lax.axis_index("mp")
    core, y0, y1 = index & 1, index >> 1 & 1, index >> 2 & 1
    halving = ((1, core), (2, y0 ^ y1), (6, y1))
    value = partial_sums
    for mask, side in halving:
        half = value.shape[0] // 2
        low, high = value[:half], value[half:]
        keep = jnp.where(side == 0, low, high)
        give = jnp.where(side == 0, high, low)
        value = keep + send(give.astype(BF), by_mask(mask)).astype(F32)
    for route in (by_mask(8), by_z(Z_NEAR), by_z(Z_FAR), by_mask(64)):
        value = value + send(value.astype(BF), route).astype(F32)
    value = value.astype(BF)
    for mask, side in halving[::-1]:
        other = send(value, by_mask(mask))
        value = jnp.where(
            side == 0,
            jnp.concatenate([value, other], axis=0),
            jnp.concatenate([other, value], axis=0),
        )
    return value


def bit_value(which_bit):
    return lax.axis_index("mp") >> which_bit & 1


def assemble(piece):
    joined = piece
    for which_bit in (5, 6):
        partner = send(joined, by_mask(1 << which_bit))
        joined = jnp.where(
            bit_value(which_bit) == 0,
            jnp.concatenate([joined, partner], axis=2),
            jnp.concatenate([partner, joined], axis=2),
        )
    return joined


def reduce_quarters(sums):
    value = sums
    for which_bit in (6, 5):
        half = value.shape[2] // 2
        low, high = value[:, :, :half], value[:, :, half:]
        first = bit_value(which_bit) == 0
        keep = jnp.where(first, low, high)
        give = jnp.where(first, high, low)
        value = keep + send(give.astype(BF), by_mask(1 << which_bit)).astype(F32)
    return value


def mm(a, b, dims):
    return lax.dot_general(a, b, (dims, ((), ())), preferred_element_type=F32)


NN = ((1,), (0,))
NT = ((1,), (1,))
TN = ((0,), (0,))


def shards(inputs, cotangent, up_blocks, down_blocks, up_left, up_right, down_left, down_right):
    up, down = up_blocks[0], down_blocks[0]
    terms = up.shape[0]
    masks = [1 << t for t in range(terms - 1)]
    gelu = partial(jax.nn.gelu, approximate=True)

    first = jnp.concatenate([mm(inputs, up_left, NN), mm(cotangent, down_right, NT)], axis=1)
    ranks = mp_sum(first)
    input_rank, cot_rank = ranks[:, :256], ranks[:, 256:]
    own = assemble(jnp.stack([inputs, cotangent]))
    rows = [own] + [send(own, by_mask(mask)) for mask in masks]

    preact = mm(input_rank, up_right, NN)
    grad_hidden = mm(cot_rank, down_left, NT)
    for t in range(terms):
        preact = preact + mm(rows[t][0], up[t], NN)
        grad_hidden = grad_hidden + mm(rows[t][1], down[t], NT)
    hidden_wide, pull = jax.vjp(gelu, preact)
    hidden = hidden_wide.astype(BF)
    grad_preact = pull(grad_hidden)[0].astype(BF)

    second = jnp.concatenate([mm(hidden, down_left, NN), mm(grad_preact, up_right, NT)], axis=1)
    back = mp_sum(second)
    hidden_rank, back_rank = back[:, :256], back[:, 256:]

    sums = jnp.stack([mm(hidden, down[0], NN), mm(grad_preact, up[0], NT)])
    for t in range(1, terms):
        term = jnp.stack([mm(hidden, down[t], NN).astype(BF), mm(grad_preact, up[t], NT).astype(BF)])
        sums = sums + send(term, by_mask(masks[t - 1])).astype(F32)

    weight_down = [mm(hidden, rows[t][1], TN) for t in range(terms)] + [mm(hidden, cot_rank, TN)]
    weight_up = [mm(rows[t][0], grad_preact, TN) for t in range(terms)] + [mm(input_rank, grad_preact, TN)]
    weights = dp_sum(jnp.stack([w.astype(BF) for w in weight_down + weight_up]))
    grad_down_blocks, grad_down_left = weights[:terms], weights[terms]
    grad_up_blocks, grad_up_right = weights[terms + 1 : 2 * terms + 1], weights[2 * terms + 1]

    mine = reduce_quarters(sums)
    outputs = (mine[0] + mm(hidden_rank, down_right, NN)).astype(BF)
    grad_inputs = (mine[1] + mm(back_rank, up_left, NT)).astype(BF)
    narrow = dp_sum(jnp.stack([mm(inputs, back_rank, TN), mm(cotangent, hidden_rank, TN)]))
    return (
        outputs,
        grad_inputs,
        grad_up_blocks[None],
        grad_down_blocks[None],
        narrow[0],
        grad_up_right,
        grad_down_left,
        narrow[1].T,
    )


def solution(mesh):
    placed = (
        P("dp", "mp"),
        P("dp", "mp"),
        P("mp", None, None, None),
        P("mp", None, None, None),
        P("mp", None),
        P(None, "mp"),
        P("mp", None),
        P(None, "mp"),
    )
    return jax.shard_map(shards, mesh=mesh, in_specs=placed, out_specs=placed, check_vma=False)
```

time: 1510 us -> 204 us (0.14)
  blocking collectives: 1260 us -> 0 us
  starting transfers between devices: 82.4 us -> 59.5 us
  matrix products: 30.1 us -> 15 us
    psum x2 -> x0, blocking collectives: 1260 us -> none  [the longest x1 632 us: shards(): lax.psum(jnp.dot(inputs, up_left, preferred_element_type=jnp.float32), 'mp')]
    ppermute x28 -> x36, waiting for transfers between devices: 49.8 us -> 122 us  [the longest x34 101 us: send(): return lax.ppermute(value, 'mp', route)]
    psum x2 -> x0, waiting for transfers between devices: 58 us -> none  [the longest x1 58 us: shards(): lax.psum(jnp.stack(weight_up, axis=1).astype(jnp.bfloat16), 'dp')]
    ppermute x28 -> x36, starting transfers between devices: 82.3 us -> 59.5 us  [the longest x34 57.9 us: send(): return lax.ppermute(value, 'mp', route)]
    dot_general x48, matrix products: 30.1 us -> 15 us  [mm(): return lax.dot_general(a, b, (dims, ((), ())), preferred_element_type=F32)]
  transfers between devices with their start and end apart: 30 -> 36, of which waited for: 13 -> 20; matrix products, arithmetic and copies ran while one was open for 1% -> 6% of each run, Pallas kernels for 0% -> 0%
where the time goes in v1:
time: 204 us
  waiting for transfers between devices  122 us (60%)
  starting transfers between devices  59.5 us (29%)
  matrix products  15 us (7%)
  other arithmetic  3.87 us (2%)
  local copies, waits for them, and re-layouts  2.64 us (1%)
    ppermute x34, waiting for transfers between devices, send(): return lax.ppermute(value, 'mp', route)  101 us
    ppermute x34, starting transfers between devices, send(): return lax.ppermute(value, 'mp', route)  57.9 us
    ppermute x2, waiting for transfers between devices, swapped_dp(): return lax.ppermute(value, 'dp', [(0, 1), (1, 0)])  20.2 us
    dot_general x48, matrix products, mm(): return lax.dot_general(a, b, (dims, ((), ())), preferred_element_type=F32)  15 us
  transfers between devices with their start and end apart: 36, of which 20 were waited for; matrix products, arithmetic and copies ran while one was open for 6% of the time, Pallas kernels for 0%

profile of v1, /device:TPU:32, one launch (start us, length us, event | category | flops | bytes accessed | tf_op | source)
XLA Modules:
  0.0 204.0 jit_solution(7645633156728556688)
XLA Ops:
  6.4 4.0 %collective-permute-done.1 = bf16[128,512]{0,1:T(8,128)(2,1)S(1)} collective-permute-done((bf16[128,512]{0,1:T(8,128)(2,1)S(1)}, bf16[128,512]{0,1:T(8,128)(2,1)S(1)}, u32[]{:S(2)}, u32[]{:S(2)}) %collective-permute-start.1) | collective-permute-done | bytes 131104 | tf_op jit(solution)/shard_map/ppermute | solution.py:24
  10.5 3.1 %collective-permute-start.2 = (bf16[64,512]{0,1:T(8,128)(2,1)S(1)}, bf16[64,512]{0,1:T(8,128)(2,1)S(1)}, u32[]{:S(2)}, u32[]{:S(2)}) collective-permute-start(bf16[64,512]{0,1:T(8,128)(2,1)S(1)} %select_convert_fusion.6), channel_id=1, source_target_pairs={{0,6},{1,7},{2,4},{3,5},{4,2},{5,3},{6,0},{7,1},{8,14},{9,15},{10,... | collective-permute-start | bytes 196616 | tf_op jit(solution)/shard_map/ppermute | solution.py:24
  13.6 3.2 %collective-permute-done.2 = bf16[64,512]{0,1:T(8,128)(2,1)S(1)} collective-permute-done((bf16[64,512]{0,1:T(8,128)(2,1)S(1)}, bf16[64,512]{0,1:T(8,128)(2,1)S(1)}, u32[]{:S(2)}, u32[]{:S(2)}) %collective-permute-start.2) | collective-permute-done | bytes 65568 | tf_op jit(solution)/shard_map/ppermute | solution.py:24
  18.9 3.1 %collective-permute-done.3 = bf16[64,512]{0,1:T(8,128)(2,1)S(1)} collective-permute-done((bf16[64,512]{0,1:T(8,128)(2,1)S(1)}, bf16[64,512]{0,1:T(8,128)(2,1)S(1)}, u32[]{:S(2)}, u32[]{:S(2)}) %collective-permute-start.3) | collective-permute-done | bytes 65568 | tf_op jit(solution)/shard_map/ppermute | solution.py:24
  24.1 5.5 %collective-permute-start.10 = (bf16[2,512,64]{1,2,0:T(8,128)(2,1)S(1)}, bf16[2,512,64]{1,2,0:T(8,128)(2,1)S(1)}, u32[]{:S(2)}, u32[]{:S(2)}) collective-permute-start(bf16[2,512,64]{1,2,0:T(8,128)(2,1)S(1)} %pad_maximum_fusion.7), channel_id=1, source_target_pairs={{0,32},{1,33},{2,34},{3,35},{4,36},{5,37},{6,38},{7,39},{8,40},{9,... | collective-permute-start | bytes 393224 | tf_op jit(solution)/shard_map/ppermute | solution.py:24
  32.0 7.3 %collective-permute-start.5 = (bf16[64,512]{0,1:T(8,128)(2,1)S(1)}, bf16[64,512]{0,1:T(8,128)(2,1)S(1)}, u32[]{:S(2)}, u32[]{:S(2)}) collective-permute-start(bf16[64,512]{0,1:T(8,128)(2,1)S(1)} %fusion.137), channel_id=1, source_target_pairs={{0,24},{1,25},{2,26},{3,27},{4,28},{5,29},{6,30},{7,31},{8,48},{9,... | collective-permute-start | bytes 196616 | tf_op jit(solution)/shard_map/ppermute | solution.py:24
  39.5 3.1 %collective-permute-start.11 = (bf16[2,512,128]{1,2,0:T(8,128)(2,1)S(1)}, bf16[2,512,128]{1,2,0:T(8,128)(2,1)S(1)}, u32[]{:S(2)}, u32[]{:S(2)}) collective-permute-start(bf16[2,512,128]{1,2,0:T(8,128)(2,1)S(1)} %maximum_select_fusion.4), channel_id=1, source_target_pairs={{0,64},{1,65},{2,66},{3,67},{4,68},{5,69},{6,70},{7,71},{8,72},{9,... | collective-permute-start | bytes 786440 | tf_op jit(solution)/shard_map/ppermute | solution.py:24
  43.2 3.1 %collective-permute-start.6 = (bf16[64,512]{0,1:T(8,128)(2,1)S(1)}, bf16[64,512]{0,1:T(8,128)(2,1)S(1)}, u32[]{:S(2)}, u32[]{:S(2)}) collective-permute-start(bf16[64,512]{0,1:T(8,128)(2,1)S(1)} %fusion.82), channel_id=1, source_target_pairs={{0,64},{1,65},{2,66},{3,67},{4,68},{5,69},{6,70},{7,71},{8,72},{9,... | collective-permute-start | bytes 196616 | tf_op jit(solution)/shard_map/ppermute | solution.py:24
  48.0 4.1 %collective-permute-start.14 = (bf16[2,512,256]{1,2,0:T(8,128)(2,1)S(1)}, bf16[2,512,256]{1,2,0:T(8,128)(2,1)S(1)}, u32[]{:S(2)}, u32[]{:S(2)}) collective-permute-start(bf16[2,512,256]{1,2,0:T(8,128)(2,1)S(1)} %maximum_select_fusion.1), channel_id=1, source_target_pairs={{0,4},{1,5},{2,6},{3,7},{4,0},{5,1},{6,2},{7,3},{8,12},{9,13},{10,... | collective-permute-start | bytes 1572872 | tf_op jit(solution)/shard_map/ppermute | solution.py:24
  55.3 6.2 %collective-permute-done.7 = bf16[64,512]{0,1:T(8,128)(2,1)S(1)} collective-permute-done((bf16[64,512]{0,1:T(8,128)(2,1)S(1)}, bf16[64,512]{0,1:T(8,128)(2,1)S(1)}, u32[]{:S(2)}, u32[]{:S(2)}) %collective-permute-start.7) | collective-permute-done | bytes 65568 | tf_op jit(solution)/shard_map/ppermute | solution.py:24
  62.1 6.7 %collective-permute-done.8 = bf16[128,512]{0,1:T(8,128)(2,1)S(1)} collective-permute-done((bf16[128,512]{0,1:T(8,128)(2,1)S(1)}, bf16[128,512]{0,1:T(8,128)(2,1)S(1)}, u32[]{:S(2)}, u32[]{:S(2)}) %collective-permute-start.8) | collective-permute-done | bytes 131104 | tf_op jit(solution)/shard_map/ppermute | solution.py:24
  80.2 4.2 %collective-permute-start.19 = (bf16[2,512,256]{1,2,0:T(8,128)(2,1)S(1)}, bf16[2,512,256]{1,2,0:T(8,128)(2,1)S(1)}, u32[]{:S(2)}, u32[]{:S(2)}) collective-permute-start(bf16[2,512,256]{1,2,0:T(8,128)(2,1)S(1)} %pad_maximum_fusion.4), channel_id=1, source_target_pairs={{0,4},{1,5},{2,6},{3,7},{4,0},{5,1},{6,2},{7,3},{8,12},{9,13},{10,... | collective-permute-start | bytes 1572872 | tf_op jit(solution)/shard_map/ppermute | solution.py:24
  86.4 21.3 %collective-permute-done.25 = bf16[128,512]{0,1:T(8,128)(2,1)S(1)} collective-permute-done((bf16[128,512]{0,1:T(8,128)(2,1)S(1)}, bf16[128,512]{0,1:T(8,128)(2,1)S(1)}, u32[]{:S(2)}, u32[]{:S(2)}) %collective-permute-start.25) | collective-permute-done | bytes 131104 | tf_op jit(solution)/shard_map/ppermute | solution.py:24
  107.9 3.1 %collective-permute-start.26 = (bf16[64,512]{0,1:T(8,128)(2,1)S(1)}, bf16[64,512]{0,1:T(8,128)(2,1)S(1)}, u32[]{:S(2)}, u32[]{:S(2)}) collective-permute-start(bf16[64,512]{0,1:T(8,128)(2,1)S(1)} %select_convert_fusion.3), channel_id=1, source_target_pairs={{0,6},{1,7},{2,4},{3,5},{4,2},{5,3},{6,0},{7,1},{8,14},{9,15},{10,... | collective-permute-start | bytes 196616 | tf_op jit(solution)/shard_map/ppermute | solution.py:24
  111.2 2.9 %collective-permute-done.26 = bf16[64,512]{0,1:T(8,128)(2,1)S(1)} collective-permute-done((bf16[64,512]{0,1:T(8,128)(2,1)S(1)}, bf16[64,512]{0,1:T(8,128)(2,1)S(1)}, u32[]{:S(2)}, u32[]{:S(2)}) %collective-permute-start.26) | collective-permute-done | bytes 65568 | tf_op jit(solution)/shard_map/ppermute | solution.py:24
  115.6 3.7 %collective-permute-done.27 = bf16[64,512]{0,1:T(8,128)(2,1)S(1)} collective-permute-done((bf16[64,512]{0,1:T(8,128)(2,1)S(1)}, bf16[64,512]{0,1:T(8,128)(2,1)S(1)}, u32[]{:S(2)}, u32[]{:S(2)}) %collective-permute-start.27) | collective-permute-done | bytes 65568 | tf_op jit(solution)/shard_map/ppermute | solution.py:24
  122.9 18.1 %collective-permute-done.21 = bf16[2,512,256]{1,2,0:T(8,128)(2,1)S(1)} collective-permute-done((bf16[2,512,256]{1,2,0:T(8,128)(2,1)S(1)}, bf16[2,512,256]{1,2,0:T(8,128)(2,1)S(1)}, u32[]{:S(2)}, u32[]{:S(2)}) %collective-permute-start.21) | collective-permute-done | bytes 524320 | tf_op jit(solution)/shard_map/ppermute | solution.py:24
  141.4 3.3 %collective-permute-done.28 = bf16[64,512]{0,1:T(8,128)(2,1)S(1)} collective-permute-done((bf16[64,512]{0,1:T(8,128)(2,1)S(1)}, bf16[64,512]{0,1:T(8,128)(2,1)S(1)}, u32[]{:S(2)}, u32[]{:S(2)}) %collective-permute-start.28) | collective-permute-done | bytes 65568 | tf_op jit(solution)/shard_map/ppermute | solution.py:24
  148.6 5.7 %collective-permute-done.29 = bf16[64,512]{0,1:T(8,128)(2,1)S(1)} collective-permute-done((bf16[64,512]{0,1:T(8,128)(2,1)S(1)}, bf16[64,512]{0,1:T(8,128)(2,1)S(1)}, u32[]{:S(2)}, u32[]{:S(2)}) %collective-permute-start.29) | collective-permute-done | bytes 65568 | tf_op jit(solution)/shard_map/ppermute | solution.py:24
  157.2 5.1 %collective-permute-done.30 = bf16[64,512]{0,1:T(8,128)(2,1)S(1)} collective-permute-done((bf16[64,512]{0,1:T(8,128)(2,1)S(1)}, bf16[64,512]{0,1:T(8,128)(2,1)S(1)}, u32[]{:S(2)}, u32[]{:S(2)}) %collective-permute-start.30) | collective-permute-done | bytes 65568 | tf_op jit(solution)/shard_map/ppermute | solution.py:24
  162.9 5.8 %collective-permute-done.31 = bf16[64,512]{0,1:T(8,128)(2,1)S(1)} collective-permute-done((bf16[64,512]{0,1:T(8,128)(2,1)S(1)}, bf16[64,512]{0,1:T(8,128)(2,1)S(1)}, u32[]{:S(2)}, u32[]{:S(2)}) %collective-permute-start.31) | collective-permute-done | bytes 65568 | tf_op jit(solution)/shard_map/ppermute | solution.py:24
  169.0 3.0 %collective-permute-start.23 = (bf16[2,512,64]{1,2,0:T(8,128)(2,1)S(1)}, bf16[2,512,64]{1,2,0:T(8,128)(2,1)S(1)}, u32[]{:S(2)}, u32[]{:S(2)}) collective-permute-start(bf16[2,512,64]{1,2,0:T(8,128)(2,1)S(1)} %select_convert_fusion.5), channel_id=1, source_target_pairs={{0,32},{1,33},{2,34},{3,35},{4,36},{5,37},{6,38},{7,39},{8,40},{9,... | collective-permute-start | bytes 393224 | tf_op jit(solution)/shard_map/ppermute | solution.py:24
  174.1 4.7 %collective-permute-done.23 = bf16[2,512,64]{1,2,0:T(8,128)(2,1)S(1)} collective-permute-done((bf16[2,512,64]{1,2,0:T(8,128)(2,1)S(1)}, bf16[2,512,64]{1,2,0:T(8,128)(2,1)S(1)}, u32[]{:S(2)}, u32[]{:S(2)}) %collective-permute-start.23) | collective-permute-done | bytes 131104 | tf_op jit(solution)/shard_map/ppermute | solution.py:24
  180.6 20.2 %collective-permute-done.35 = bf16[2,64,256]{2,1,0:T(8,128)(2,1)S(1)} collective-permute-done((bf16[2,64,256]{2,1,0:T(8,128)(2,1)S(1)}, bf16[2,64,256]{2,1,0:T(8,128)(2,1)S(1)}, u32[]{:S(2)}, u32[]{:S(2)}) %collective-permute-start.35) | collective-permute-done | bytes 65568 | tf_op jit(solution)/shard_map/ppermute | solution.py:28
  (157 shorter events, 51.9 us)
Async XLA Ops:
  22.0 10.0 %collective-permute-start.4 = (bf16[64,512]{0,1:T(8,128)(2,1)S(1)}, bf16[64,512]{0,1:T(8,128)(2,1)S(1)}, u32[]{:S(2)}, u32[]{:S(2)}) collective-permute-start(bf16[64,512]{0,1:T(8,128)(2,1)S(1)} %fusion.81), channel_id=1, source_target_pairs={{0,56},{1,57},{2,58},{3,59},{4,60},{5,61},{6,62},{7,63},{8,16},{9,... | collective-permute-start | bytes 196616 | tf_op jit(solution)/shard_map/ppermute | solution.py:24
  24.1 15.3 %collective-permute-start.10 = (bf16[2,512,64]{1,2,0:T(8,128)(2,1)S(1)}, bf16[2,512,64]{1,2,0:T(8,128)(2,1)S(1)}, u32[]{:S(2)}, u32[]{:S(2)}) collective-permute-start(bf16[2,512,64]{1,2,0:T(8,128)(2,1)S(1)} %pad_maximum_fusion.7), channel_id=1, source_target_pairs={{0,32},{1,33},{2,34},{3,35},{4,36},{5,37},{6,38},{7,39},{8,40},{9,... | collective-permute-start | bytes 393224 | tf_op jit(solution)/shard_map/ppermute | solution.py:24
  32.0 11.0 %collective-permute-start.5 = (bf16[64,512]{0,1:T(8,128)(2,1)S(1)}, bf16[64,512]{0,1:T(8,128)(2,1)S(1)}, u32[]{:S(2)}, u32[]{:S(2)}) collective-permute-start(bf16[64,512]{0,1:T(8,128)(2,1)S(1)} %fusion.137), channel_id=1, source_target_pairs={{0,24},{1,25},{2,26},{3,27},{4,28},{5,29},{6,30},{7,31},{8,48},{9,... | collective-permute-start | bytes 196616 | tf_op jit(solution)/shard_map/ppermute | solution.py:24
  39.5 8.0 %collective-permute-start.11 = (bf16[2,512,128]{1,2,0:T(8,128)(2,1)S(1)}, bf16[2,512,128]{1,2,0:T(8,128)(2,1)S(1)}, u32[]{:S(2)}, u32[]{:S(2)}) collective-permute-start(bf16[2,512,128]{1,2,0:T(8,128)(2,1)S(1)} %maximum_select_fusion.4), channel_id=1, source_target_pairs={{0,64},{1,65},{2,66},{3,67},{4,68},{5,69},{6,70},{7,71},{8,72},{9,... | collective-permute-start | bytes 786440 | tf_op jit(solution)/shard_map/ppermute | solution.py:24
  43.2 11.4 %collective-permute-start.6 = (bf16[64,512]{0,1:T(8,128)(2,1)S(1)}, bf16[64,512]{0,1:T(8,128)(2,1)S(1)}, u32[]{:S(2)}, u32[]{:S(2)}) collective-permute-start(bf16[64,512]{0,1:T(8,128)(2,1)S(1)} %fusion.82), channel_id=1, source_target_pairs={{0,64},{1,65},{2,66},{3,67},{4,68},{5,69},{6,70},{7,71},{8,72},{9,... | collective-permute-start | bytes 196616 | tf_op jit(solution)/shard_map/ppermute | solution.py:24
  47.6 21.3 %collective-permute-start.13 = (bf16[2,512,256]{1,2,0:T(8,128)(2,1)S(1)}, bf16[2,512,256]{1,2,0:T(8,128)(2,1)S(1)}, u32[]{:S(2)}, u32[]{:S(2)}) collective-permute-start(bf16[2,512,256]{1,2,0:T(8,128)(2,1)S(1)} %maximum_select_fusion.1), channel_id=1, source_target_pairs={{0,2},{1,3},{2,0},{3,1},{4,6},{5,7},{6,4},{7,5},{8,10},{9,11},{10,... | collective-permute-start | bytes 1572872 | tf_op jit(solution)/shard_map/ppermute | solution.py:24
  48.0 22.3 %collective-permute-start.14 = (bf16[2,512,256]{1,2,0:T(8,128)(2,1)S(1)}, bf16[2,512,256]{1,2,0:T(8,128)(2,1)S(1)}, u32[]{:S(2)}, u32[]{:S(2)}) collective-permute-start(bf16[2,512,256]{1,2,0:T(8,128)(2,1)S(1)} %maximum_select_fusion.1), channel_id=1, source_target_pairs={{0,4},{1,5},{2,6},{3,7},{4,0},{5,1},{6,2},{7,3},{8,12},{9,13},{10,... | collective-permute-start | bytes 1572872 | tf_op jit(solution)/shard_map/ppermute | solution.py:24
  52.1 18.7 %collective-permute-start.15 = (bf16[2,512,256]{1,2,0:T(8,128)(2,1)S(1)}, bf16[2,512,256]{1,2,0:T(8,128)(2,1)S(1)}, u32[]{:S(2)}, u32[]{:S(2)}) collective-permute-start(bf16[2,512,256]{1,2,0:T(8,128)(2,1)S(1)} %maximum_select_fusion.1), channel_id=1, source_target_pairs={{0,8},{1,9},{2,10},{3,11},{4,12},{5,13},{6,14},{7,15},{8,0},{9,1},... | collective-permute-start | bytes 1572872 | tf_op jit(solution)/shard_map/ppermute | solution.py:24
  52.1 19.3 %collective-permute-start.16 = (bf16[2,512,256]{1,2,0:T(8,128)(2,1)S(1)}, bf16[2,512,256]{1,2,0:T(8,128)(2,1)S(1)}, u32[]{:S(2)}, u32[]{:S(2)}) collective-permute-start(bf16[2,512,256]{1,2,0:T(8,128)(2,1)S(1)} %maximum_select_fusion.1), channel_id=1, source_target_pairs={{0,16},{1,17},{2,18},{3,19},{4,20},{5,21},{6,22},{7,23},{8,24},{9,... | collective-permute-start | bytes 1572872 | tf_op jit(solution)/shard_map/ppermute | solution.py:24
  61.7 7.1 %collective-permute-start.8 = (bf16[128,512]{0,1:T(8,128)(2,1)S(1)}, bf16[128,512]{0,1:T(8,128)(2,1)S(1)}, u32[]{:S(2)}, u32[]{:S(2)}) collective-permute-start(bf16[128,512]{0,1:T(8,128)(2,1)S(1)} %maximum_select_fusion.6), channel_id=1, source_target_pairs={{0,2},{1,3},{2,0},{3,1},{4,6},{5,7},{6,4},{7,5},{8,10},{9,11},{10,... | collective-permute-start | bytes 393224 | tf_op jit(solution)/shard_map/ppermute | solution.py:24
  77.0 8.8 %collective-permute-start.24 = (bf16[256,512]{0,1:T(8,128)(2,1)S(1)}, bf16[256,512]{0,1:T(8,128)(2,1)S(1)}, u32[]{:S(2)}, u32[]{:S(2)}) collective-permute-start(bf16[256,512]{0,1:T(8,128)(2,1)S(1)} %select_convert_fusion), channel_id=1, source_target_pairs={{0,1},{1,0},{2,3},{3,2},{4,5},{5,4},{6,7},{7,6},{8,9},{9,8},{10,11... | collective-permute-start | bytes 786440 | tf_op jit(solution)/shard_map/ppermute | solution.py:24
  79.1 42.6 %collective-permute-start.17 = (bf16[2,512,256]{1,2,0:T(8,128)(2,1)S(1)}, bf16[2,512,256]{1,2,0:T(8,128)(2,1)S(1)}, u32[]{:S(2)}, u32[]{:S(2)}) collective-permute-start(bf16[2,512,256]{1,2,0:T(8,128)(2,1)S(1)} %pad_maximum_fusion.2), channel_id=1, source_target_pairs={{0,1},{1,0},{2,3},{3,2},{4,5},{5,4},{6,7},{7,6},{8,9},{9,8},{10,11... | collective-permute-start | bytes 1572872 | tf_op jit(solution)/shard_map/ppermute | solution.py:24
  79.7 43.2 %collective-permute-start.18 = (bf16[2,512,256]{1,2,0:T(8,128)(2,1)S(1)}, bf16[2,512,256]{1,2,0:T(8,128)(2,1)S(1)}, u32[]{:S(2)}, u32[]{:S(2)}) collective-permute-start(bf16[2,512,256]{1,2,0:T(8,128)(2,1)S(1)} %pad_maximum_fusion.3), channel_id=1, source_target_pairs={{0,2},{1,3},{2,0},{3,1},{4,6},{5,7},{6,4},{7,5},{8,10},{9,11},{10,... | collective-permute-start | bytes 1572872 | tf_op jit(solution)/shard_map/ppermute | solution.py:24
  80.2 42.7 %collective-permute-start.19 = (bf16[2,512,256]{1,2,0:T(8,128)(2,1)S(1)}, bf16[2,512,256]{1,2,0:T(8,128)(2,1)S(1)}, u32[]{:S(2)}, u32[]{:S(2)}) collective-permute-start(bf16[2,512,256]{1,2,0:T(8,128)(2,1)S(1)} %pad_maximum_fusion.4), channel_id=1, source_target_pairs={{0,4},{1,5},{2,6},{3,7},{4,0},{5,1},{6,2},{7,3},{8,12},{9,13},{10,... | collective-permute-start | bytes 1572872 | tf_op jit(solution)/shard_map/ppermute | solution.py:24
  84.4 38.4 %collective-permute-start.20 = (bf16[2,512,256]{1,2,0:T(8,128)(2,1)S(1)}, bf16[2,512,256]{1,2,0:T(8,128)(2,1)S(1)}, u32[]{:S(2)}, u32[]{:S(2)}) collective-permute-start(bf16[2,512,256]{1,2,0:T(8,128)(2,1)S(1)} %pad_maximum_fusion.5), channel_id=1, source_target_pairs={{0,8},{1,9},{2,10},{3,11},{4,12},{5,13},{6,14},{7,15},{8,0},{9,1},... | collective-permute-start | bytes 1572872 | tf_op jit(solution)/shard_map/ppermute | solution.py:24
  86.0 21.7 %collective-permute-start.25 = (bf16[128,512]{0,1:T(8,128)(2,1)S(1)}, bf16[128,512]{0,1:T(8,128)(2,1)S(1)}, u32[]{:S(2)}, u32[]{:S(2)}) collective-permute-start(bf16[128,512]{0,1:T(8,128)(2,1)S(1)} %select_convert_fusion.4), channel_id=1, source_target_pairs={{0,2},{1,3},{2,0},{3,1},{4,6},{5,7},{6,4},{7,5},{8,10},{9,11},{10,... | collective-permute-start | bytes 393224 | tf_op jit(solution)/shard_map/ppermute | solution.py:24
  119.3 21.7 %collective-permute-start.21 = (bf16[2,512,256]{1,2,0:T(8,128)(2,1)S(1)}, bf16[2,512,256]{1,2,0:T(8,128)(2,1)S(1)}, u32[]{:S(2)}, u32[]{:S(2)}) collective-permute-start(bf16[2,512,256]{1,2,0:T(8,128)(2,1)S(1)} %pad_maximum_fusion.6), channel_id=1, source_target_pairs={{0,16},{1,17},{2,18},{3,19},{4,20},{5,21},{6,22},{7,23},{8,24},{9,... | collective-permute-start | bytes 1572872 | tf_op jit(solution)/shard_map/ppermute | solution.py:24
  121.7 23.0 %collective-permute-start.28 = (bf16[64,512]{0,1:T(8,128)(2,1)S(1)}, bf16[64,512]{0,1:T(8,128)(2,1)S(1)}, u32[]{:S(2)}, u32[]{:S(2)}) collective-permute-start(bf16[64,512]{0,1:T(8,128)(2,1)S(1)} %fusion.83), channel_id=1, source_target_pairs={{0,56},{1,57},{2,58},{3,59},{4,60},{5,61},{6,62},{7,63},{8,16},{9,... | collective-permute-start | bytes 196616 | tf_op jit(solution)/shard_map/ppermute | solution.py:24
  144.8 9.6 %collective-permute-start.29 = (bf16[64,512]{0,1:T(8,128)(2,1)S(1)}, bf16[64,512]{0,1:T(8,128)(2,1)S(1)}, u32[]{:S(2)}, u32[]{:S(2)}) collective-permute-start(bf16[64,512]{0,1:T(8,128)(2,1)S(1)} %fusion.138), channel_id=1, source_target_pairs={{0,24},{1,25},{2,26},{3,27},{4,28},{5,29},{6,30},{7,31},{8,48},{9,... | collective-permute-start | bytes 196616 | tf_op jit(solution)/shard_map/ppermute | solution.py:24
  147.7 15.0 %collective-permute-start.22 = (bf16[2,512,128]{1,2,0:T(8,128)(2,1)S(1)}, bf16[2,512,128]{1,2,0:T(8,128)(2,1)S(1)}, u32[]{:S(2)}, u32[]{:S(2)}) collective-permute-start(bf16[2,512,128]{1,2,0:T(8,128)(2,1)S(1)} %select_convert_fusion.1), channel_id=1, source_target_pairs={{0,64},{1,65},{2,66},{3,67},{4,68},{5,69},{6,70},{7,71},{8,72},{9,... | collective-permute-start | bytes 786440 | tf_op jit(solution)/shard_map/ppermute | solution.py:24
  154.5 7.9 %collective-permute-start.30 = (bf16[64,512]{0,1:T(8,128)(2,1)S(1)}, bf16[64,512]{0,1:T(8,128)(2,1)S(1)}, u32[]{:S(2)}, u32[]{:S(2)}) collective-permute-start(bf16[64,512]{0,1:T(8,128)(2,1)S(1)} %fusion.84), channel_id=1, source_target_pairs={{0,64},{1,65},{2,66},{3,67},{4,68},{5,69},{6,70},{7,71},{8,72},{9,... | collective-permute-start | bytes 196616 | tf_op jit(solution)/shard_map/ppermute | solution.py:24
  155.9 45.6 %collective-permute-start.34 = (bf16[14,256,256]{2,1,0:T(8,128)(2,1)S(1)}, bf16[14,256,256]{2,1,0:T(8,128)(2,1)S(1)}, u32[]{:S(2)}, u32[]{:S(2)}) collective-permute-start(bf16[14,256,256]{2,1,0:T(8,128)(2,1)S(1)} %fusion.45), channel_id=1, source_target_pairs={{0,128},{128,0},{1,129},{129,1},{2,130},{130,2},{3,131},{131,3},{4... | collective-permute-start | bytes 5505032 | tf_op jit(solution)/shard_map/ppermute | solution.py:28
  169.0 9.8 %collective-permute-start.23 = (bf16[2,512,64]{1,2,0:T(8,128)(2,1)S(1)}, bf16[2,512,64]{1,2,0:T(8,128)(2,1)S(1)}, u32[]{:S(2)}, u32[]{:S(2)}) collective-permute-start(bf16[2,512,64]{1,2,0:T(8,128)(2,1)S(1)} %select_convert_fusion.5), channel_id=1, source_target_pairs={{0,32},{1,33},{2,34},{3,35},{4,36},{5,37},{6,38},{7,39},{8,40},{9,... | collective-permute-start | bytes 393224 | tf_op jit(solution)/shard_map/ppermute | solution.py:24
  179.4 21.5 %collective-permute-start.35 = (bf16[2,64,256]{2,1,0:T(8,128)(2,1)S(1)}, bf16[2,64,256]{2,1,0:T(8,128)(2,1)S(1)}, u32[]{:S(2)}, u32[]{:S(2)}) collective-permute-start(bf16[2,64,256]{2,1,0:T(8,128)(2,1)S(1)} %pad_maximum_fusion.8), channel_id=1, source_target_pairs={{0,128},{128,0},{1,129},{129,1},{2,130},{130,2},{3,131},{131,3},{4... | collective-permute-start | bytes 196616 | tf_op jit(solution)/shard_map/ppermute | solution.py:28
  (20 other events, 237.3 us)

commit v2 on v1

v2 whole, which is shorter than its diff:
```python
from functools import partial

import jax
import jax.numpy as jnp
from jax import lax
from jax.sharding import PartitionSpec as P

BF = jnp.bfloat16
F32 = jnp.float32

Z_NEAR = (7, 2, 1, 4, 3, 6, 5, 0)
Z_FAR = (3, 6, 5, 0, 7, 2, 1, 4)
Z_TWO = (6, 3, 0, 5, 2, 7, 4, 1)
Z_THREE = (5, 4, 7, 6, 1, 0, 3, 2)

STEPS_A = ['h:core', 'y:halve', 'a:z1', 'z:all', 'a:x2', 'y:join', 'j:core']
STARTS_A = {'z2a': 2, 'z2b': 2, 'core': 'y2'}
ENDS_A = {'q1': 2, 'z1h': 2, 'q2': 3, 'fx': 5, 'y2': 5, 'y1': 5}
FAR = ('z1',)
FXG = {'fx': ('z1',)}
SPLIT = ('z2',)
NTIE = False
STEPS_C = ['h:core', 'y:halve', 'a:x2', 'a:z1', 'a:zn', 'a:zf', 'y:join', 'j:core']
STARTS_C = {'y1': 0, 'y2': 0, 'd0': 2, 'd1': 'q2'}
ENDS_C = {'core': 1, 'z1': 3, 'z2': 3, 'y2': 6, 'y1': 6, 'd0': 6}
PARTS = 2
WAITS = (1, 1)
DMODE = 'swap'
TERMS_C = {'y1': 0, 'y2': 0}


def by_mask(mask):
    return [(i, i ^ mask) for i in range(128)]


def by_z(table):
    return [(i, (i & 0b1000111) | table[i >> 3 & 7] << 3) for i in range(128)]


ROUTES = {
    "core": by_mask(1),
    "y1": by_mask(2),
    "y2": by_mask(4),
    "y3": by_mask(6),
    "z1": by_mask(8),
    "z2": by_mask(16),
    "z4": by_mask(32),
    "z6": by_mask(48),
    "x2": by_mask(64),
    "zn": by_z(Z_NEAR),
    "zf": by_z(Z_FAR),
    "zp": by_z(Z_TWO),
    "zq": by_z(Z_THREE),
}


def send(value, route):
    return lax.ppermute(value, "mp", ROUTES[route])


def swapped_dp(value):
    return lax.ppermute(value, "dp", [(0, 1), (1, 0)])


def after(value, *others):
    return lax.optimization_barrier((value,) + others)[0]


def bit_value(which_bit):
    return lax.axis_index("mp") >> which_bit & 1


def pick(side, low, high):
    return jnp.where(side == 0, low, high)


class Tree:
    def __init__(self, partial_sums, steps, starts, ends):
        self.value = partial_sums
        self.steps, self.starts, self.ends = steps, starts, ends
        self.ops = {}
        self.got = {}

    def side(self, route):
        return {
            "core": lambda: bit_value(0),
            "y1": lambda: bit_value(1) ^ bit_value(2),
            "y3": lambda: bit_value(2),
            "z1": lambda: bit_value(3) ^ bit_value(4),
            "x2": lambda: bit_value(6),
        }[route]()

    def result(self, name):
        if name not in self.got:
            self.got[name] = self.ops[name]()
        return self.got[name]

    def big(self, name, make, go):
        self.ops[name] = lambda: go(make())

    def tied(self, name, value):
        step = self.starts.get(name)
        if step is None:
            return value
        return after(value, self.result(step) if isinstance(step, str) else self.history[step])

    def direct(self, way, first):
        mine = bit_value(1) + 2 * bit_value(2)
        if way == "halve":
            parts = self.value.reshape((4, -1) + self.value.shape[1:])
            take = lambda k: lax.dynamic_index_in_dim(parts, mine ^ k, 0, False)
            gives = after(tuple(take(k).astype(BF) for k in (1, 3, 2)), *first)
            self.value = take(0)
            for give, route in zip(gives, ("y1", "y3", "y2")):
                self.value = self.value + send(give, route).astype(F32)
        else:
            own = after(self.value.astype(BF), *first)
            got = {1: send(own, "y1"), 3: send(own, "y3"), 2: send(own, "y2")}
            stack = jnp.stack([own, got[1], got[2], got[3]])
            self.value = jnp.concatenate(
                [lax.dynamic_index_in_dim(stack, mine ^ k, 0, False) for k in range(4)], axis=0
            )

    def run(self):
        self.history = {}
        for index, step in enumerate(self.steps):
            kind, route = step.split(":")
            first = [self.result(name) for name, at in self.ends.items() if at == index]
            if kind == "y":
                self.direct(route, first)
            elif kind == "z":
                give = after(self.value.astype(BF), *first)
                got = [send(give, r) for r in (("zn", "zp", "zq") if route == "all" else route.split(","))]
                for one in got:
                    self.value = self.value + one.astype(F32)
            elif kind == "h":
                side = self.side(route)
                half = self.value.shape[0] // 2
                low, high = self.value[:half], self.value[half:]
                give = after(pick(side, high, low).astype(BF), *first)
                self.value = pick(side, low, high) + send(give, route).astype(F32)
            elif kind == "a":
                give = after(self.value.astype(BF), *first)
                self.value = self.value + send(give, route).astype(F32)
            else:
                side = self.side(route)
                mine = self.value.astype(BF)
                other = send(after(mine, *first), route)
                self.value = pick(
                    side,
                    jnp.concatenate([mine, other], axis=0),
                    jnp.concatenate([other, mine], axis=0),
                )
            self.history[index] = self.value[:8, :128]
        return self.value


def mm(a, b, dims):
    return lax.dot_general(a, b, (dims, ((), ())), preferred_element_type=F32)


NN = ((1,), (0,))
NT = ((1,), (1,))
TN = ((0,), (0,))


def joined(which_bit, mine, other):
    return pick(
        bit_value(which_bit),
        jnp.concatenate([mine, other], axis=2),
        jnp.concatenate([other, mine], axis=2),
    )


def shards(inputs, cotangent, up_blocks, down_blocks, up_left, up_right, down_left, down_right):
    up, down = up_blocks[0], down_blocks[0]
    terms = up.shape[0]
    gelu = partial(jax.nn.gelu, approximate=True)
    names = ("core", "y1", "y2", "z1", "z2")

    pair = jnp.stack([inputs, cotangent])
    partial_ranks = jnp.concatenate([mm(inputs, up_left, NN), mm(cotangent, down_right, NT)], axis=1)
    tree = Tree(partial_ranks, STEPS_A, STARTS_A, ENDS_A)
    tree.big("q1", lambda: tree.tied("q1", pair), lambda v: send(v, "z4"))
    half = lambda: joined(5, pair, tree.result("q1"))
    tree.big("q2", lambda: tree.tied("q2", half()), lambda v: send(v, "x2"))
    own = lambda: joined(6, half(), tree.result("q2"))
    for name in names:
        if name in FAR:
            tree.big(name + "h", lambda: half(), lambda v, name=name: send(v, name))
        elif name in SPLIT:
            tree.big(name + "a", lambda name=name: tree.tied(name + "a", own()[0]), lambda v: send(v, "z2"))
            tree.big(name + "b", lambda name=name: tree.tied(name + "b", own()[1]), lambda v: send(v, "z6"))
            tree.ops[name] = lambda name=name: (tree.result(name + "a"), tree.result(name + "b"))
        else:
            tree.big(name, lambda name=name: tree.tied(name, own()), lambda v, name=name: send(v, name))
    for group, members in FXG.items():
        tree.big(
            group,
            lambda g=group, m=members: tree.tied(g, jnp.concatenate([tree.result(n + "h") for n in m])),
            lambda v: send(v, "x2"),
        )
        for i, name in enumerate(members):
            tree.ops[name] = lambda g=group, i=i, name=name: joined(
                6, tree.result(name + "h"), tree.result(g)[2 * i : 2 * i + 2]
            )
    ranks = tree.run()
    rows = [own()] + [tree.result(name) for name in names]
    input_rank, cot_rank = ranks[:, :256], ranks[:, 256:]

    preact = mm(input_rank, up_right, NN)
    grad_hidden = mm(cot_rank, down_left, NT)
    for t in range(terms):
        preact = preact + mm(rows[t][0], up[t], NN)
        grad_hidden = grad_hidden + mm(rows[t][1], down[t], NT)
    hidden_wide, pull = jax.vjp(gelu, preact)
    hidden = hidden_wide.astype(BF)
    grad_preact = pull(grad_hidden)[0].astype(BF)

    partial_back = jnp.concatenate([mm(hidden, down_left, NN), mm(grad_preact, up_right, NT)], axis=1)
    tree = Tree(partial_back, STEPS_C, STARTS_C, ENDS_C)
    pairs = [(hidden, rows[t][1]) for t in range(terms)] + [(hidden, cot_rank)]
    pairs += [(rows[t][0], grad_preact) for t in range(terms)] + [(input_rank, grad_preact)]
    edges = [2 * (terms + 1) * i // PARTS for i in range(PARTS + 1)]
    memo = {}

    def chunk(i):
        if i not in memo:
            found = []
            for left, right in pairs[edges[i] : edges[i + 1]]:
                if WAITS[i] is not None:
                    left, right = after((left, right), tree.history[WAITS[i]])
                found.append(mm(left, right, TN).astype(BF))
            memo[i] = jnp.stack(found)
        return memo[i]

    exchanged = swapped_dp if DMODE == "swap" else lambda v: lax.psum(v, "dp")
    for i in range(PARTS):
        tree.big(f"d{i}", lambda i=i: tree.tied(f"d{i}", chunk(i)), exchanged)

    def term(t):
        step = TERMS_C.get(names[t - 1])
        left, right = (hidden, grad_preact) if step is None else after((hidden, grad_preact), tree.history[step])
        return jnp.stack([mm(left, down[t], NN).astype(BF), mm(right, up[t], NT).astype(BF)])

    for t, name in enumerate(names):
        tree.big(name, lambda t=t, name=name: tree.tied(name, term(t + 1)), lambda v, name=name: send(v, name))

    def quarters(value, which_bit):
        middle = value.shape[2] // 2
        low, high = value[:, :, :middle], value[:, :, middle:]
        first = bit_value(which_bit)
        return pick(first, low, high), pick(first, high, low).astype(BF)

    def sums():
        total = jnp.stack([mm(hidden, down[0], NN), mm(grad_preact, up[0], NT)])
        for name in names:
            total = total + tree.result(name).astype(F32)
        return quarters(total, 6)

    tree.big("q2", lambda: tree.tied("q2", sums()[1]), lambda v: send(v, "x2"))
    halves = lambda: quarters(sums()[0] + tree.result("q2").astype(F32), 5)
    tree.big("q1", lambda: tree.tied("q1", halves()[1]), lambda v: send(v, "z4"))
    back = tree.run()
    mine = halves()[0] + tree.result("q1").astype(F32)
    hidden_rank, back_rank = back[:, :256], back[:, 256:]
    outputs = (mine[0] + mm(hidden_rank, down_right, NN)).astype(BF)
    grad_inputs = (mine[1] + mm(back_rank, up_left, NT)).astype(BF)
    narrow = jnp.stack([mm(inputs, back_rank, TN), mm(cotangent, hidden_rank, TN)]).astype(BF)

    def total(part, other):
        return (part.astype(F32) + other.astype(F32)).astype(BF)

    grads = []
    for i in range(PARTS):
        got = tree.result(f"d{i}")
        grads += list(total(chunk(i), got) if DMODE == "swap" else got)
    narrow = total(narrow, swapped_dp(narrow if DMODE == "psum" and not NTIE else after(narrow, *[tree.result(f"d{i}") for i in range(PARTS)])))
    return (
        outputs,
        grad_inputs,
        jnp.stack(grads[terms + 1 : 2 * terms + 1])[None],
        jnp.stack(grads[:terms])[None],
        narrow[0],
        grads[2 * terms + 1],
        grads[terms],
        narrow[1].T,
    )


def solution(mesh):
    placed = (
        P("dp", "mp"),
        P("dp", "mp"),
        P("mp", None, None, None),
        P("mp", None, None, None),
        P("mp", None),
        P(None, "mp"),
        P("mp", None),
        P(None, "mp"),
    )
    return jax.shard_map(shards, mesh=mesh, in_specs=placed, out_specs=placed, check_vma=False)
```

time: 204 us -> 157 us (0.77)
  waiting for transfers between devices: 122 us -> 49.4 us
  local copies, waits for them, and re-layouts: 2.64 us -> 11.8 us
  starting transfers between devices: 59.5 us -> 67.6 us
  other arithmetic: 3.87 us -> 8.45 us
    ppermute x34 -> x41, waiting for transfers between devices: 101 us -> 47.5 us  [send(): return lax.ppermute(value, 'mp', ROUTES[route])]
    ppermute x2 -> x3, waiting for transfers between devices: 20.2 us -> 1.96 us  [swapped_dp(): return lax.ppermute(value, 'dp', [(0, 1), (1, 0)])]
    ppermute x34 -> x41, starting transfers between devices: 57.9 us -> 66 us  [send(): return lax.ppermute(value, 'mp', ROUTES[route])]
    another operation x6 -> x8, other arithmetic: 0.27 us -> 3.79 us  [the longest x5 3.71 us: term(): jnp.stack([mm(left, down[t], NN).astype(BF), mm(right, up[t], NT).astype(...]
    squeeze x1 -> x5, local copies, waits for them, and re-layouts: 0.71 us -> 3.41 us  [the longest x4 3.38 us: shards(): preact = preact + mm(rows[t][0], up[t], NN)]
    add x0 -> x2, local copies, waits for them, and re-layouts: none -> 2.22 us  [run(): self.value = pick(side, low, high) + send(give, route).astype(F32)]
    add x7 -> x5, other arithmetic: 0.84 us -> 2.94 us  [the longest x1 1.79 us: sums(): total = total + tree.result(name).astype(F32)]
  transfers between devices with their start and end apart: 36 -> 44, of which waited for: 20 -> 19; matrix products, arithmetic and copies ran while one was open for 6% -> 18% of each run, Pallas kernels for 0% -> 0%
where the time goes in v2:
time: 157 us; the launch traced here: 155 us
  starting transfers between devices  67.6 us (43%)
  waiting for transfers between devices  49.4 us (31%)
  matrix products  16.4 us (10%)
  local copies, waits for them, and re-layouts  11.8 us (8%)
  other arithmetic  8.45 us (5%)
  between operations  1.67 us (1%)
    ppermute x41, starting transfers between devices, send(): return lax.ppermute(value, 'mp', ROUTES[route])  66 us
    ppermute x41, waiting for transfers between devices, send(): return lax.ppermute(value, 'mp', ROUTES[route])  47.5 us
    dot_general x48, matrix products, mm(): return lax.dot_general(a, b, (dims, ((), ())), preferred_element_type=F32)  16.4 us
    another operation x5, other arithmetic, term(): jnp.stack([mm(left, down[t], NN).astype(BF), mm(right, up[t], NT).astype(...  3.71 us
    squeeze x4, local copies, waits for them, and re-layouts, shards(): preact = preact + mm(rows[t][0], up[t], NN)  3.38 us
  transfers between devices with their start and end apart: 44, of which 19 were waited for; matrix products, arithmetic and copies ran while one was open for 18% of the time, Pallas kernels for 0%

profile of v2, /device:TPU:32, one launch (start us, length us, event | category | flops | bytes accessed | tf_op | source)
XLA Modules:
  0.0 155.4 jit_solution(6107164325205757100)
XLA Ops:
  3.2 6.4 %collective-permute-start.4 = (bf16[2,512,64]{1,2,0:T(8,128)(2,1)S(1)}, bf16[2,512,64]{1,2,0:T(8,128)(2,1)S(1)}, u32[]{:S(2)}, u32[]{:S(2)}) collective-permute-start(bf16[2,512,64]{1,2,0:T(8,128)(2,1)S(1)} %pad_maximum_fusion.11), channel_id=1, source_target_pairs={{0,32},{1,33},{2,34},{3,35},{4,36},{5,37},{6,38},{7,39},{8,40},{9,... | collective-permute-start | bytes 393224 | tf_op jit(solution)/shard_map/ppermute | solution.py:58
  11.6 2.2 %collective-permute-start.2 = (bf16[64,512]{1,0:T(8,128)(2,1)S(1)}, bf16[64,512]{1,0:T(8,128)(2,1)S(1)}, u32[]{:S(2)}, u32[]{:S(2)}) collective-permute-start(bf16[64,512]{1,0:T(8,128)(2,1)S(1)} %get-tuple-element.57), channel_id=1, source_target_pairs={{0,6},{1,7},{2,4},{3,5},{4,2},{5,3},{6,0},{7,1},{8,14},{9,15},{10,... | collective-permute-start | bytes 196616 | tf_op jit(solution)/shard_map/ppermute | solution.py:58
  14.5 2.1 %collective-permute-done.4 = bf16[2,512,64]{1,2,0:T(8,128)(2,1)S(1)} collective-permute-done((bf16[2,512,64]{1,2,0:T(8,128)(2,1)S(1)}, bf16[2,512,64]{1,2,0:T(8,128)(2,1)S(1)}, u32[]{:S(2)}, u32[]{:S(2)}) %collective-permute-start.4) | collective-permute-done | bytes 131104 | tf_op jit(solution)/shard_map/ppermute | solution.py:58
  16.7 3.1 %collective-permute-start.7 = (bf16[2,512,128]{1,2,0:T(8,128)(2,1)S(1)}, bf16[2,512,128]{1,2,0:T(8,128)(2,1)S(1)}, u32[]{:S(2)}, u32[]{:S(2)}) collective-permute-start(bf16[2,512,128]{1,2,0:T(8,128)(2,1)S(1)} %maximum_select_fusion.2), channel_id=1, source_target_pairs={{0,64},{1,65},{2,66},{3,67},{4,68},{5,69},{6,70},{7,71},{8,72},{9,... | collective-permute-start | bytes 786440 | tf_op jit(solution)/shard_map/ppermute | solution.py:58
  19.8 6.5 %collective-permute-done.7 = bf16[2,512,128]{1,2,0:T(8,128)(2,1)S(1)} collective-permute-done((bf16[2,512,128]{1,2,0:T(8,128)(2,1)S(1)}, bf16[2,512,128]{1,2,0:T(8,128)(2,1)S(1)}, u32[]{:S(2)}, u32[]{:S(2)}) %collective-permute-start.7) | collective-permute-done | bytes 262176 | tf_op jit(solution)/shard_map/ppermute | solution.py:58
  26.5 3.3 %collective-permute-start.13 = (bf16[2,512,256]{1,2,0:T(8,128)(2,1)S(1)}, bf16[2,512,256]{1,2,0:T(8,128)(2,1)S(1)}, u32[]{:S(2)}, u32[]{:S(2)}) collective-permute-start(bf16[2,512,256]{1,2,0:T(8,128)(2,1)S(1)} %maximum_select_fusion), channel_id=1, source_target_pairs={{0,4},{1,5},{2,6},{3,7},{4,0},{5,1},{6,2},{7,3},{8,12},{9,13},{10,... | collective-permute-start | bytes 1572872 | tf_op jit(solution)/shard_map/ppermute | solution.py:58
  30.8 4.0 %collective-permute-done.6 = bf16[64,512]{1,0:T(8,128)(2,1)S(1)} collective-permute-done((bf16[64,512]{1,0:T(8,128)(2,1)S(1)}, bf16[64,512]{1,0:T(8,128)(2,1)S(1)}, u32[]{:S(2)}, u32[]{:S(2)}) %collective-permute-start.6) | collective-permute-done | bytes 65568 | tf_op jit(solution)/shard_map/ppermute | solution.py:58
  34.8 4.1 %collective-permute-start.10 = (bf16[64,512]{1,0:T(8,128)(2,1)S(1)}, bf16[64,512]{1,0:T(8,128)(2,1)S(1)}, u32[]{:S(2)}, u32[]{:S(2)}) collective-permute-start(bf16[64,512]{1,0:T(8,128)(2,1)S(1)} %get-tuple-element.60), channel_id=1, source_target_pairs={{0,40},{1,41},{2,42},{3,43},{4,44},{5,45},{6,46},{7,47},{8,32},{9,... | collective-permute-start | bytes 196616 | tf_op jit(solution)/shard_map/ppermute | solution.py:58
  43.3 3.0 %collective-permute-start.12 = (bf16[2,512,128]{1,2,0:T(8,128)(2,1)S(1)}, bf16[2,512,128]{1,2,0:T(8,128)(2,1)S(1)}, u32[]{:S(2)}, u32[]{:S(2)}) collective-permute-start(bf16[2,512,128]{1,2,0:T(8,128)(2,1)S(1)} %collective-permute-done.5), channel_id=1, source_target_pairs={{0,64},{1,65},{2,66},{3,67},{4,68},{5,69},{6,70},{7,71},{8,72},{9,... | collective-permute-start | bytes 786440 | tf_op jit(solution)/shard_map/ppermute | solution.py:58
  46.5 3.1 %collective-permute-start.11 = (bf16[64,512]{1,0:T(8,128)(2,1)S(1)}, bf16[64,512]{1,0:T(8,128)(2,1)S(1)}, u32[]{:S(2)}, u32[]{:S(2)}) collective-permute-start(bf16[64,512]{1,0:T(8,128)(2,1)S(1)} %fusion.141), channel_id=1, source_target_pairs={{0,64},{1,65},{2,66},{3,67},{4,68},{5,69},{6,70},{7,71},{8,72},{9,... | collective-permute-start | bytes 196616 | tf_op jit(solution)/shard_map/ppermute | solution.py:58
  50.0 2.4 %collective-permute-done.11 = bf16[64,512]{1,0:T(8,128)(2,1)S(1)} collective-permute-done((bf16[64,512]{1,0:T(8,128)(2,1)S(1)}, bf16[64,512]{1,0:T(8,128)(2,1)S(1)}, u32[]{:S(2)}, u32[]{:S(2)}) %collective-permute-start.11) | collective-permute-done | bytes 65568 | tf_op jit(solution)/shard_map/ppermute | solution.py:58
  52.4 2.7 %collective-permute-start.21 = (bf16[512,256]{0,1:T(8,128)(2,1)S(1)}, bf16[512,256]{0,1:T(8,128)(2,1)S(1)}, u32[]{:S(2)}, u32[]{:S(2)}) collective-permute-start(bf16[512,256]{0,1:T(8,128)(2,1)S(1)} %get-tuple-element.74), channel_id=1, source_target_pairs={{0,48},{1,49},{2,50},{3,51},{4,52},{5,53},{6,54},{7,55},{8,56},{9,... | collective-permute-start | bytes 786440 | tf_op jit(solution)/shard_map/ppermute | solution.py:58
  58.6 2.9 %collective-permute-start.16 = (bf16[64,512]{1,0:T(8,128)(2,1)S(1)}, bf16[64,512]{1,0:T(8,128)(2,1)S(1)}, u32[]{:S(2)}, u32[]{:S(2)}) collective-permute-start(bf16[64,512]{1,0:T(8,128)(2,1)S(1)} %add_convert_fusion.4), channel_id=1, source_target_pairs={{0,4},{1,5},{2,6},{3,7},{4,0},{5,1},{6,2},{7,3},{8,12},{9,13},{10,... | collective-permute-start | bytes 196616 | tf_op jit(solution)/shard_map/ppermute | solution.py:58
  74.6 2.2 %collective-permute-start.26 = (bf16[2,512,256]{1,2,0:T(8,128)(2,1)}, bf16[2,512,256]{1,2,0:T(8,128)(2,1)}, u32[]{:S(2)}, u32[]{:S(2)}) collective-permute-start(bf16[2,512,256]{1,2,0:T(8,128)(2,1)} %pad_maximum_fusion.5), channel_id=1, source_target_pairs={{0,8},{1,9},{2,10},{3,11},{4,12},{5,13},{6,14},{7,15},{8,0},{9,1},... | collective-permute-start | bytes 1572872 | tf_op jit(solution)/shard_map/ppermute | solution.py:58
  81.7 2.0 %copy.41 = f32[256,512]{1,0:T(8,128)} copy(f32[256,512]{0,1:T(8,128)} %convert_add_fusion.1) | data formatting | bytes 1048576 | tf_op jit(solution)/shard_map/add | solution.py:141
  86.2 2.9 %collective-permute-start.31 = (bf16[64,512]{1,0:T(8,128)(2,1)S(1)}, bf16[64,512]{1,0:T(8,128)(2,1)S(1)}, u32[]{:S(2)}, u32[]{:S(2)}) collective-permute-start(bf16[64,512]{1,0:T(8,128)(2,1)S(1)} %get-tuple-element.70), channel_id=1, source_target_pairs={{0,6},{1,7},{2,4},{3,5},{4,2},{5,3},{6,0},{7,1},{8,14},{9,15},{10,... | collective-permute-start | bytes 196616 | tf_op jit(solution)/shard_map/ppermute | solution.py:58
  91.6 2.5 %collective-permute-start.25 = (bf16[2,512,256]{1,2,0:T(8,128)(2,1)S(1)}, bf16[2,512,256]{1,2,0:T(8,128)(2,1)S(1)}, u32[]{:S(2)}, u32[]{:S(2)}) collective-permute-start(bf16[2,512,256]{1,2,0:T(8,128)(2,1)S(1)} %pad_maximum_fusion.4), channel_id=1, source_target_pairs={{0,4},{1,5},{2,6},{3,7},{4,0},{5,1},{6,2},{7,3},{8,12},{9,13},{10,... | collective-permute-start | bytes 1572872 | tf_op jit(solution)/shard_map/ppermute | solution.py:58
  95.5 3.0 %collective-permute-start.33 = (bf16[64,512]{1,0:T(8,128)(2,1)S(1)}, bf16[64,512]{1,0:T(8,128)(2,1)S(1)}, u32[]{:S(2)}, u32[]{:S(2)}) collective-permute-start(bf16[64,512]{1,0:T(8,128)(2,1)S(1)} %get-tuple-element.112), channel_id=1, source_target_pairs={{0,64},{1,65},{2,66},{3,67},{4,68},{5,69},{6,70},{7,71},{8,72},{9,... | collective-permute-start | bytes 196616 | tf_op jit(solution)/shard_map/ppermute | solution.py:58
  103.0 2.1 %collective-permute-start.34 = (bf16[64,512]{1,0:T(8,128)(2,1)S(1)}, bf16[64,512]{1,0:T(8,128)(2,1)S(1)}, u32[]{:S(2)}, u32[]{:S(2)}) collective-permute-start(bf16[64,512]{1,0:T(8,128)(2,1)S(1)} %fusion.133), channel_id=1, source_target_pairs={{0,8},{1,9},{2,10},{3,11},{4,12},{5,13},{6,14},{7,15},{8,0},{9,1},... | collective-permute-start | bytes 196616 | tf_op jit(solution)/shard_map/ppermute | solution.py:58
  108.6 7.7 %collective-permute-done.25 = bf16[2,512,256]{1,2,0:T(8,128)(2,1)S(1)} collective-permute-done((bf16[2,512,256]{1,2,0:T(8,128)(2,1)S(1)}, bf16[2,512,256]{1,2,0:T(8,128)(2,1)S(1)}, u32[]{:S(2)}, u32[]{:S(2)}) %collective-permute-start.25) | collective-permute-done | bytes 524320 | tf_op jit(solution)/shard_map/ppermute | solution.py:58
  118.1 2.8 %collective-permute-start.28 = (bf16[2,512,128]{1,2,0:T(8,128)(2,1)S(1)}, bf16[2,512,128]{1,2,0:T(8,128)(2,1)S(1)}, u32[]{:S(2)}, u32[]{:S(2)}) collective-permute-start(bf16[2,512,128]{1,2,0:T(8,128)(2,1)S(1)} %select_convert_fusion), channel_id=1, source_target_pairs={{0,64},{1,65},{2,66},{3,67},{4,68},{5,69},{6,70},{7,71},{8,72},{9,... | collective-permute-start | bytes 786440 | tf_op jit(solution)/shard_map/ppermute | solution.py:58
  122.5 5.4 %collective-permute-done.28 = bf16[2,512,128]{1,2,0:T(8,128)(2,1)S(1)} collective-permute-done((bf16[2,512,128]{1,2,0:T(8,128)(2,1)S(1)}, bf16[2,512,128]{1,2,0:T(8,128)(2,1)S(1)}, u32[]{:S(2)}, u32[]{:S(2)}) %collective-permute-start.28) | collective-permute-done | bytes 262176 | tf_op jit(solution)/shard_map/ppermute | solution.py:58
  130.4 8.0 %collective-permute-done.29 = bf16[2,512,64]{1,2,0:T(8,128)(2,1)S(1)} collective-permute-done((bf16[2,512,64]{1,2,0:T(8,128)(2,1)S(1)}, bf16[2,512,64]{1,2,0:T(8,128)(2,1)S(1)}, u32[]{:S(2)}, u32[]{:S(2)}) %collective-permute-start.29) | collective-permute-done | bytes 131104 | tf_op jit(solution)/shard_map/ppermute | solution.py:58
  141.2 2.0 %collective-permute-start.40 = (bf16[64,512]{1,0:T(8,128)(2,1)S(1)}, bf16[64,512]{1,0:T(8,128)(2,1)S(1)}, u32[]{:S(2)}, u32[]{:S(2)}) collective-permute-start(bf16[64,512]{1,0:T(8,128)(2,1)S(1)} %add_convert_fusion.3), channel_id=1, source_target_pairs={{0,6},{1,7},{2,4},{3,5},{4,2},{5,3},{6,0},{7,1},{8,14},{9,15},{10,... | collective-permute-start | bytes 196616 | tf_op jit(solution)/shard_map/ppermute | solution.py:58
  (236 shorter events, 67.3 us)
Async XLA Ops:
  3.2 13.4 %collective-permute-start.4 = (bf16[2,512,64]{1,2,0:T(8,128)(2,1)S(1)}, bf16[2,512,64]{1,2,0:T(8,128)(2,1)S(1)}, u32[]{:S(2)}, u32[]{:S(2)}) collective-permute-start(bf16[2,512,64]{1,2,0:T(8,128)(2,1)S(1)} %pad_maximum_fusion.11), channel_id=1, source_target_pairs={{0,32},{1,33},{2,34},{3,35},{4,36},{5,37},{6,38},{7,39},{8,40},{9,... | collective-permute-start | bytes 393224 | tf_op jit(solution)/shard_map/ppermute | solution.py:58
  9.9 9.8 %collective-permute-start.1 = (bf16[64,512]{1,0:T(8,128)(2,1)S(1)}, bf16[64,512]{1,0:T(8,128)(2,1)S(1)}, u32[]{:S(2)}, u32[]{:S(2)}) collective-permute-start(bf16[64,512]{1,0:T(8,128)(2,1)S(1)} %get-tuple-element.56), channel_id=1, source_target_pairs={{0,2},{1,3},{2,0},{3,1},{4,6},{5,7},{6,4},{7,5},{8,10},{9,11},{10,... | collective-permute-start | bytes 196616 | tf_op jit(solution)/shard_map/ppermute | solution.py:58
  11.6 8.2 %collective-permute-start.2 = (bf16[64,512]{1,0:T(8,128)(2,1)S(1)}, bf16[64,512]{1,0:T(8,128)(2,1)S(1)}, u32[]{:S(2)}, u32[]{:S(2)}) collective-permute-start(bf16[64,512]{1,0:T(8,128)(2,1)S(1)} %get-tuple-element.57), channel_id=1, source_target_pairs={{0,6},{1,7},{2,4},{3,5},{4,2},{5,3},{6,0},{7,1},{8,14},{9,15},{10,... | collective-permute-start | bytes 196616 | tf_op jit(solution)/shard_map/ppermute | solution.py:58
  16.7 9.7 %collective-permute-start.7 = (bf16[2,512,128]{1,2,0:T(8,128)(2,1)S(1)}, bf16[2,512,128]{1,2,0:T(8,128)(2,1)S(1)}, u32[]{:S(2)}, u32[]{:S(2)}) collective-permute-start(bf16[2,512,128]{1,2,0:T(8,128)(2,1)S(1)} %maximum_select_fusion.2), channel_id=1, source_target_pairs={{0,64},{1,65},{2,66},{3,67},{4,68},{5,69},{6,70},{7,71},{8,72},{9,... | collective-permute-start | bytes 786440 | tf_op jit(solution)/shard_map/ppermute | solution.py:58
  19.8 10.7 %collective-permute-start.5 = (bf16[2,512,128]{1,2,0:T(8,128)(2,1)S(1)}, bf16[2,512,128]{1,2,0:T(8,128)(2,1)S(1)}, u32[]{:S(2)}, u32[]{:S(2)}) collective-permute-start(bf16[2,512,128]{1,2,0:T(8,128)(2,1)S(1)} %maximum_select_fusion.2), channel_id=1, source_target_pairs={{0,8},{1,9},{2,10},{3,11},{4,12},{5,13},{6,14},{7,15},{8,0},{9,1},... | collective-permute-start | bytes 786440 | tf_op jit(solution)/shard_map/ppermute | solution.py:58
  26.5 30.2 %collective-permute-start.13 = (bf16[2,512,256]{1,2,0:T(8,128)(2,1)S(1)}, bf16[2,512,256]{1,2,0:T(8,128)(2,1)S(1)}, u32[]{:S(2)}, u32[]{:S(2)}) collective-permute-start(bf16[2,512,256]{1,2,0:T(8,128)(2,1)S(1)} %maximum_select_fusion), channel_id=1, source_target_pairs={{0,4},{1,5},{2,6},{3,7},{4,0},{5,1},{6,2},{7,3},{8,12},{9,13},{10,... | collective-permute-start | bytes 1572872 | tf_op jit(solution)/shard_map/ppermute | solution.py:58
  29.8 26.9 %collective-permute-start.14 = (bf16[2,512,256]{1,2,0:T(8,128)(2,1)S(1)}, bf16[2,512,256]{1,2,0:T(8,128)(2,1)S(1)}, u32[]{:S(2)}, u32[]{:S(2)}) collective-permute-start(bf16[2,512,256]{1,2,0:T(8,128)(2,1)S(1)} %maximum_select_fusion), channel_id=1, source_target_pairs={{0,2},{1,3},{2,0},{3,1},{4,6},{5,7},{6,4},{7,5},{8,10},{9,11},{10,... | collective-permute-start | bytes 1572872 | tf_op jit(solution)/shard_map/ppermute | solution.py:58
  34.8 8.5 %collective-permute-start.10 = (bf16[64,512]{1,0:T(8,128)(2,1)S(1)}, bf16[64,512]{1,0:T(8,128)(2,1)S(1)}, u32[]{:S(2)}, u32[]{:S(2)}) collective-permute-start(bf16[64,512]{1,0:T(8,128)(2,1)S(1)} %get-tuple-element.60), channel_id=1, source_target_pairs={{0,40},{1,41},{2,42},{3,43},{4,44},{5,45},{6,46},{7,47},{8,32},{9,... | collective-permute-start | bytes 196616 | tf_op jit(solution)/shard_map/ppermute | solution.py:58
  38.9 7.5 %collective-permute-start.8 = (bf16[64,512]{1,0:T(8,128)(2,1)S(1)}, bf16[64,512]{1,0:T(8,128)(2,1)S(1)}, u32[]{:S(2)}, u32[]{:S(2)}) collective-permute-start(bf16[64,512]{1,0:T(8,128)(2,1)S(1)} %get-tuple-element.60), channel_id=1, source_target_pairs={{0,56},{1,57},{2,58},{3,59},{4,60},{5,61},{6,62},{7,63},{8,16},{9,... | collective-permute-start | bytes 196616 | tf_op jit(solution)/shard_map/ppermute | solution.py:58
  43.3 11.8 %collective-permute-start.12 = (bf16[2,512,128]{1,2,0:T(8,128)(2,1)S(1)}, bf16[2,512,128]{1,2,0:T(8,128)(2,1)S(1)}, u32[]{:S(2)}, u32[]{:S(2)}) collective-permute-start(bf16[2,512,128]{1,2,0:T(8,128)(2,1)S(1)} %collective-permute-done.5), channel_id=1, source_target_pairs={{0,64},{1,65},{2,66},{3,67},{4,68},{5,69},{6,70},{7,71},{8,72},{9,... | collective-permute-start | bytes 786440 | tf_op jit(solution)/shard_map/ppermute | solution.py:58
  49.7 18.7 %collective-permute-start.20 = (bf16[512,256]{0,1:T(8,128)(2,1)S(1)}, bf16[512,256]{0,1:T(8,128)(2,1)S(1)}, u32[]{:S(2)}, u32[]{:S(2)}) collective-permute-start(bf16[512,256]{0,1:T(8,128)(2,1)S(1)} %get-tuple-element.88), channel_id=1, source_target_pairs={{0,16},{1,17},{2,18},{3,19},{4,20},{5,21},{6,22},{7,23},{8,24},{9,... | collective-permute-start | bytes 786440 | tf_op jit(solution)/shard_map/ppermute | solution.py:58
  52.4 16.5 %collective-permute-start.21 = (bf16[512,256]{0,1:T(8,128)(2,1)S(1)}, bf16[512,256]{0,1:T(8,128)(2,1)S(1)}, u32[]{:S(2)}, u32[]{:S(2)}) collective-permute-start(bf16[512,256]{0,1:T(8,128)(2,1)S(1)} %get-tuple-element.74), channel_id=1, source_target_pairs={{0,48},{1,49},{2,50},{3,51},{4,52},{5,53},{6,54},{7,55},{8,56},{9,... | collective-permute-start | bytes 786440 | tf_op jit(solution)/shard_map/ppermute | solution.py:58
  73.1 12.4 %collective-permute-start.22 = (bf16[2,512,256]{1,2,0:T(8,128)(2,1)}, bf16[2,512,256]{1,2,0:T(8,128)(2,1)}, u32[]{:S(2)}, u32[]{:S(2)}) collective-permute-start(bf16[2,512,256]{1,2,0:T(8,128)(2,1)} %pad_maximum_fusion.2), channel_id=1, source_target_pairs={{0,1},{1,0},{2,3},{3,2},{4,5},{5,4},{6,7},{7,6},{8,9},{9,8},{10,11... | collective-permute-start | bytes 1572872 | tf_op jit(solution)/shard_map/ppermute | solution.py:58
  74.6 28.4 %collective-permute-start.26 = (bf16[2,512,256]{1,2,0:T(8,128)(2,1)}, bf16[2,512,256]{1,2,0:T(8,128)(2,1)}, u32[]{:S(2)}, u32[]{:S(2)}) collective-permute-start(bf16[2,512,256]{1,2,0:T(8,128)(2,1)} %pad_maximum_fusion.5), channel_id=1, source_target_pairs={{0,8},{1,9},{2,10},{3,11},{4,12},{5,13},{6,14},{7,15},{8,0},{9,1},... | collective-permute-start | bytes 1572872 | tf_op jit(solution)/shard_map/ppermute | solution.py:58
  77.6 25.4 %collective-permute-start.27 = (bf16[2,512,256]{1,2,0:T(8,128)(2,1)}, bf16[2,512,256]{1,2,0:T(8,128)(2,1)}, u32[]{:S(2)}, u32[]{:S(2)}) collective-permute-start(bf16[2,512,256]{1,2,0:T(8,128)(2,1)} %pad_maximum_fusion.6), channel_id=1, source_target_pairs={{0,16},{1,17},{2,18},{3,19},{4,20},{5,21},{6,22},{7,23},{8,24},{9,... | collective-permute-start | bytes 1572872 | tf_op jit(solution)/shard_map/ppermute | solution.py:58
  89.9 18.7 %collective-permute-start.24 = (bf16[2,512,256]{1,2,0:T(8,128)(2,1)S(1)}, bf16[2,512,256]{1,2,0:T(8,128)(2,1)S(1)}, u32[]{:S(2)}, u32[]{:S(2)}) collective-permute-start(bf16[2,512,256]{1,2,0:T(8,128)(2,1)S(1)} %pad_maximum_fusion.3), channel_id=1, source_target_pairs={{0,2},{1,3},{2,0},{3,1},{4,6},{5,7},{6,4},{7,5},{8,10},{9,11},{10,... | collective-permute-start | bytes 1572872 | tf_op jit(solution)/shard_map/ppermute | solution.py:58
  91.6 24.7 %collective-permute-start.25 = (bf16[2,512,256]{1,2,0:T(8,128)(2,1)S(1)}, bf16[2,512,256]{1,2,0:T(8,128)(2,1)S(1)}, u32[]{:S(2)}, u32[]{:S(2)}) collective-permute-start(bf16[2,512,256]{1,2,0:T(8,128)(2,1)S(1)} %pad_maximum_fusion.4), channel_id=1, source_target_pairs={{0,4},{1,5},{2,6},{3,7},{4,0},{5,1},{6,2},{7,3},{8,12},{9,13},{10,... | collective-permute-start | bytes 1572872 | tf_op jit(solution)/shard_map/ppermute | solution.py:58
  95.5 6.7 %collective-permute-start.33 = (bf16[64,512]{1,0:T(8,128)(2,1)S(1)}, bf16[64,512]{1,0:T(8,128)(2,1)S(1)}, u32[]{:S(2)}, u32[]{:S(2)}) collective-permute-start(bf16[64,512]{1,0:T(8,128)(2,1)S(1)} %get-tuple-element.112), channel_id=1, source_target_pairs={{0,64},{1,65},{2,66},{3,67},{4,68},{5,69},{6,70},{7,71},{8,72},{9,... | collective-permute-start | bytes 196616 | tf_op jit(solution)/shard_map/ppermute | solution.py:58
  102.3 36.2 %collective-permute-start.37 = (bf16[7,256,256]{2,1,0:T(8,128)(2,1)S(1)}, bf16[7,256,256]{2,1,0:T(8,128)(2,1)S(1)}, u32[]{:S(2)}, u32[]{:S(2)}) collective-permute-start(bf16[7,256,256]{2,1,0:T(8,128)(2,1)S(1)} %fusion.31), channel_id=1, source_target_pairs={{0,128},{128,0},{1,129},{129,1},{2,130},{130,2},{3,131},{131,3},{4... | collective-permute-start | bytes 2752520 | tf_op jit(solution)/shard_map/ppermute | solution.py:62
  107.4 13.8 %collective-permute-start.35 = (bf16[64,512]{1,0:T(8,128)(2,1)S(1)}, bf16[64,512]{1,0:T(8,128)(2,1)S(1)}, u32[]{:S(2)}, u32[]{:S(2)}) collective-permute-start(bf16[64,512]{1,0:T(8,128)(2,1)S(1)} %fusion.143), channel_id=1, source_target_pairs={{0,56},{1,57},{2,58},{3,59},{4,60},{5,61},{6,62},{7,63},{8,16},{9,... | collective-permute-start | bytes 196616 | tf_op jit(solution)/shard_map/ppermute | solution.py:58
  118.1 9.8 %collective-permute-start.28 = (bf16[2,512,128]{1,2,0:T(8,128)(2,1)S(1)}, bf16[2,512,128]{1,2,0:T(8,128)(2,1)S(1)}, u32[]{:S(2)}, u32[]{:S(2)}) collective-permute-start(bf16[2,512,128]{1,2,0:T(8,128)(2,1)S(1)} %select_convert_fusion), channel_id=1, source_target_pairs={{0,64},{1,65},{2,66},{3,67},{4,68},{5,69},{6,70},{7,71},{8,72},{9,... | collective-permute-start | bytes 786440 | tf_op jit(solution)/shard_map/ppermute | solution.py:58
  121.3 8.7 %collective-permute-start.36 = (bf16[64,512]{1,0:T(8,128)(2,1)S(1)}, bf16[64,512]{1,0:T(8,128)(2,1)S(1)}, u32[]{:S(2)}, u32[]{:S(2)}) collective-permute-start(bf16[64,512]{1,0:T(8,128)(2,1)S(1)} %fusion.134), channel_id=1, source_target_pairs={{0,24},{1,25},{2,26},{3,27},{4,28},{5,29},{6,30},{7,31},{8,48},{9,... | collective-permute-start | bytes 196616 | tf_op jit(solution)/shard_map/ppermute | solution.py:58
  128.1 10.3 %collective-permute-start.29 = (bf16[2,512,64]{1,2,0:T(8,128)(2,1)S(1)}, bf16[2,512,64]{1,2,0:T(8,128)(2,1)S(1)}, u32[]{:S(2)}, u32[]{:S(2)}) collective-permute-start(bf16[2,512,64]{1,2,0:T(8,128)(2,1)S(1)} %select_convert_fusion.3), channel_id=1, source_target_pairs={{0,32},{1,33},{2,34},{3,35},{4,36},{5,37},{6,38},{7,39},{8,40},{9,... | collective-permute-start | bytes 393224 | tf_op jit(solution)/shard_map/ppermute | solution.py:58
  130.0 20.5 %collective-permute-start.42 = (bf16[7,256,256]{2,1,0:T(8,128)(2,1)S(1)}, bf16[7,256,256]{2,1,0:T(8,128)(2,1)S(1)}, u32[]{:S(2)}, u32[]{:S(2)}) collective-permute-start(bf16[7,256,256]{2,1,0:T(8,128)(2,1)S(1)} %fusion.45), channel_id=1, source_target_pairs={{0,128},{128,0},{1,129},{129,1},{2,130},{130,2},{3,131},{131,3},{4... | collective-permute-start | bytes 2752520 | tf_op jit(solution)/shard_map/ppermute | solution.py:62
  (47 other events, 298.2 us)

commit v3 on v2

--- a/solution.py
+++ b/solution.py
@@ -1,8 +1,8 @@
-from functools import partial
-
 import jax
 import jax.numpy as jnp
 from jax import lax
+from jax.experimental import pallas as pl
+from jax.experimental.pallas import tpu as pltpu
 from jax.sharding import PartitionSpec as P
 
 BF = jnp.bfloat16
@@ -13,20 +13,21 @@
 Z_TWO = (6, 3, 0, 5, 2, 7, 4, 1)
 Z_THREE = (5, 4, 7, 6, 1, 0, 3, 2)
 
-STEPS_A = ['h:core', 'y:halve', 'a:z1', 'z:all', 'a:x2', 'y:join', 'j:core']
-STARTS_A = {'z2a': 2, 'z2b': 2, 'core': 'y2'}
-ENDS_A = {'q1': 2, 'z1h': 2, 'q2': 3, 'fx': 5, 'y2': 5, 'y1': 5}
+STEPS_A = ['h:core', 'y:halve', 'a:z1', 'a:zn', 'a:zf', 'a:x2', 'y:join', 'j:core']
+STARTS_A = {'z2a': 3, 'z2b': 3, 'core': 'y2'}
+ENDS_A = {'q1': 2, 'z1h': 2, 'q2': 3, 'fx': 6, 'y2': 6, 'y1': 6}
 FAR = ('z1',)
 FXG = {'fx': ('z1',)}
 SPLIT = ('z2',)
 NTIE = False
+KSTEPS = 2
 STEPS_C = ['h:core', 'y:halve', 'a:x2', 'a:z1', 'a:zn', 'a:zf', 'y:join', 'j:core']
 STARTS_C = {'y1': 0, 'y2': 0, 'd0': 2, 'd1': 'q2'}
 ENDS_C = {'core': 1, 'z1': 3, 'z2': 3, 'y2': 6, 'y1': 6, 'd0': 6}
-PARTS = 2
+EDGES = (0, 7, 14)
 WAITS = (1, 1)
 DMODE = 'swap'
-TERMS_C = {'y1': 0, 'y2': 0}
+REAL = ('narrow',)
 
 
 def by_mask(mask):
@@ -66,6 +67,13 @@
     return lax.optimization_barrier((value,) + others)[0]
 
 
+def bound(value, *others):
+    for other in others:
+        one = other[(0,) * other.ndim].astype(value.dtype)
+        value = value + lax.clamp(jnp.zeros_like(one), one, jnp.zeros_like(one))
+    return value
+
+
 def bit_value(which_bit):
     return lax.axis_index("mp") >> which_bit & 1
 
@@ -102,13 +110,15 @@
         step = self.starts.get(name)
         if step is None:
             return value
-        return after(value, self.result(step) if isinstance(step, str) else self.history[step])
+        hold = bound if name + "s" in REAL else after
+        return hold(value, self.result(step) if isinstance(step, str) else self.history[step])
 
     def direct(self, way, first):
         mine = bit_value(1) + 2 * bit_value(2)
         if way == "halve":
-            parts = self.value.reshape((4, -1) + self.value.shape[1:])
-            take = lambda k: lax.dynamic_index_in_dim(parts, mine ^ k, 0, False)
+            quarter = self.value.shape[0] // 4
+            parts = [self.value[quarter * k : quarter * (k + 1)] for k in range(4)]
+            take = lambda k: lax.select_n(mine ^ k, *parts)
             gives = after(tuple(take(k).astype(BF) for k in (1, 3, 2)), *first)
             self.value = take(0)
             for give, route in zip(gives, ("y1", "y3", "y2")):
@@ -116,16 +126,20 @@
         else:
             own = after(self.value.astype(BF), *first)
             got = {1: send(own, "y1"), 3: send(own, "y3"), 2: send(own, "y2")}
-            stack = jnp.stack([own, got[1], got[2], got[3]])
-            self.value = jnp.concatenate(
-                [lax.dynamic_index_in_dim(stack, mine ^ k, 0, False) for k in range(4)], axis=0
-            )
+            parts = [own, got[1], got[2], got[3]]
+            self.value = jnp.concatenate([lax.select_n(mine ^ k, *parts) for k in range(4)], axis=0)
 
     def run(self):
         self.history = {}
         for index, step in enumerate(self.steps):
             kind, route = step.split(":")
             first = [self.result(name) for name, at in self.ends.items() if at == index]
+            must = [self.result(name) for name, at in self.ends.items() if at == index and name + "e" in REAL]
+            if must:
+                if isinstance(self.value, tuple):
+                    self.value = self.value[0], bound(self.value[1], *must)
+                else:
+                    self.value = bound(self.value, *must)
             if kind == "y":
                 self.direct(route, first)
             elif kind == "z":
@@ -133,6 +147,9 @@
                 got = [send(give, r) for r in (("zn", "zp", "zq") if route == "all" else route.split(","))]
                 for one in got:
                     self.value = self.value + one.astype(F32)
+            elif kind == "h" and isinstance(self.value, tuple):
+                keep, give = self.value
+                self.value = keep + send(after(give, *first), route).astype(F32)
             elif kind == "h":
                 side = self.side(route)
                 half = self.value.shape[0] // 2
@@ -164,6 +181,77 @@
 TN = ((0,), (0,))
 
 
+def middle(core_ref, pre_ref, grad_ref, rank_ref, up_ref, down_ref, up_right_ref, down_left_ref, *outs):
+    act_ref, give_ref, keep_ref, own_ref = outs[:4]
+    width = pre_ref.shape[1]
+    v = pre_ref[...] + mm(rank_ref[:, :width], up_right_ref[...], NN)
+    g = grad_ref[...] + mm(rank_ref[:, width:], down_left_ref[...], NT)
+    scale = 0.7978845608028654
+    square = v * v
+    t = jnp.tanh(scale * (v + 0.044715 * (square * v)))
+    half = 0.5 * (1.0 + t)
+    slope = half + 0.5 * v * (1.0 - t * t) * (scale * (1.0 + 3 * 0.044715 * square))
+    hidden = (v * half).astype(BF)
+    grad = (g * slope).astype(BF)
+    act_ref[0] = hidden
+    act_ref[1] = grad
+    ranks = jnp.concatenate([mm(hidden, down_left_ref[...], NN), mm(grad, up_right_ref[...], NT)], axis=1)
+    step = pl.program_id(0)
+    steps = pl.num_programs(0)
+
+    @pl.when(step < steps // 2)
+    def _():
+        give_ref[...] = ranks.astype(BF)
+
+    @pl.when(step >= steps // 2)
+    def _():
+        keep_ref[...] = ranks
+
+    for t_index, out in enumerate((own_ref,) + outs[4:]):
+        out[0] = mm(hidden, down_ref[t_index], NN).astype(out.dtype)
+        out[1] = mm(grad, up_ref[t_index], NT).astype(out.dtype)
+
+
+def between(pre, grad, ranks, up, down, up_right, down_left):
+    rows, width = pre.shape
+    terms = up.shape[0]
+    steps = KSTEPS
+    block = rows // steps
+    core = (lax.axis_index("mp") & 1).astype(jnp.int32).reshape(1)
+
+    def place(i, core_ref):
+        return lax.rem(i + (steps // 2) * (1 - core_ref[0]), steps)
+
+    by_rows = lambda cols: pl.BlockSpec((block, cols), lambda i, c: (place(i, c), 0))
+    by_pair = pl.BlockSpec((2, block, width), lambda i, c: (0, place(i, c), 0))
+    whole = lambda shape: pl.BlockSpec(shape, lambda i, c: (0,) * len(shape))
+    first = pl.BlockSpec((block, 2 * width), lambda i, c: (jnp.minimum(i, steps // 2 - 1), 0))
+    second = pl.BlockSpec((block, 2 * width), lambda i, c: (jnp.maximum(i - steps // 2, 0), 0))
+    pair = lambda dtype: jax.ShapeDtypeStruct((2, rows, width), dtype)
+    ranks_half = lambda dtype: jax.ShapeDtypeStruct((rows // 2, 2 * width), dtype)
+    return pl.pallas_call(
+        middle,
+        grid_spec=pltpu.PrefetchScalarGridSpec(
+            num_scalar_prefetch=1,
+            grid=(steps,),
+            in_specs=[
+                by_rows(width),
+                by_rows(width),
+                by_rows(2 * width),
+                whole(up.shape),
+                whole(down.shape),
+                whole(up_right.shape),
+                whole(down_left.shape),
+            ],
+            out_specs=[by_pair, first, second] + [by_pair] * terms,
+        ),
+        out_shape=[pair(BF), ranks_half(BF), ranks_half(F32), pair(F32)] + [pair(BF)] * (terms - 1),
+        compiler_params=pltpu.CompilerParams(vmem_limit_bytes=24 << 20),
+        cost_estimate=pl.CostEstimate(flops=2 * 16 * rows * width * width, bytes_accessed=9 << 20, transcendentals=rows * width),
+        name="middle",
+    )(core, pre, grad, ranks, up, down, up_right, down_left)
+
+
 def joined(which_bit, mine, other):
     return pick(
         bit_value(which_bit),
@@ -175,7 +263,6 @@
 def shards(inputs, cotangent, up_blocks, down_blocks, up_left, up_right, down_left, down_right):
     up, down = up_blocks[0], down_blocks[0]
     terms = up.shape[0]
-    gelu = partial(jax.nn.gelu, approximate=True)
     names = ("core", "y1", "y2", "z1", "z2")
 
     pair = jnp.stack([inputs, cotangent])
@@ -208,43 +295,36 @@
     rows = [own()] + [tree.result(name) for name in names]
     input_rank, cot_rank = ranks[:, :256], ranks[:, 256:]
 
-    preact = mm(input_rank, up_right, NN)
-    grad_hidden = mm(cot_rank, down_left, NT)
-    for t in range(terms):
-        preact = preact + mm(rows[t][0], up[t], NN)
-        grad_hidden = grad_hidden + mm(rows[t][1], down[t], NT)
-    hidden_wide, pull = jax.vjp(gelu, preact)
-    hidden = hidden_wide.astype(BF)
-    grad_preact = pull(grad_hidden)[0].astype(BF)
-
-    partial_back = jnp.concatenate([mm(hidden, down_left, NN), mm(grad_preact, up_right, NT)], axis=1)
-    tree = Tree(partial_back, STEPS_C, STARTS_C, ENDS_C)
+    pre = sum(mm(rows[t][0], up[t], NN) for t in range(terms))
+    grad = sum(mm(rows[t][1], down[t], NT) for t in range(terms))
+    act, give, keep, own_sum, *sent = between(pre, grad, ranks, up, down, up_right, down_left)
+    hidden, grad_preact = act[0], act[1]
+    tree = Tree((keep, give), STEPS_C, STARTS_C, ENDS_C)
     pairs = [(hidden, rows[t][1]) for t in range(terms)] + [(hidden, cot_rank)]
     pairs += [(rows[t][0], grad_preact) for t in range(terms)] + [(input_rank, grad_preact)]
-    edges = [2 * (terms + 1) * i // PARTS for i in range(PARTS + 1)]
+    edges = EDGES
     memo = {}
 
     def chunk(i):
         if i not in memo:
             found = []
             for left, right in pairs[edges[i] : edges[i + 1]]:
-                if WAITS[i] is not None:
+                if isinstance(WAITS[i], str):
+                    left = bound(left, tree.result(WAITS[i]))
+                elif isinstance(WAITS[i], float):
+                    left = bound(left, tree.history[int(WAITS[i])])
+                elif WAITS[i] is not None:
                     left, right = after((left, right), tree.history[WAITS[i]])
                 found.append(mm(left, right, TN).astype(BF))
             memo[i] = jnp.stack(found)
         return memo[i]
 
     exchanged = swapped_dp if DMODE == "swap" else lambda v: lax.psum(v, "dp")
-    for i in range(PARTS):
+    for i in range(len(EDGES) - 1):
         tree.big(f"d{i}", lambda i=i: tree.tied(f"d{i}", chunk(i)), exchanged)
 
-    def term(t):
-        step = TERMS_C.get(names[t - 1])
-        left, right = (hidden, grad_preact) if step is None else after((hidden, grad_preact), tree.history[step])
-        return jnp.stack([mm(left, down[t], NN).astype(BF), mm(right, up[t], NT).astype(BF)])
-
     for t, name in enumerate(names):
-        tree.big(name, lambda t=t, name=name: tree.tied(name, term(t + 1)), lambda v, name=name: send(v, name))
+        tree.big(name, lambda t=t, name=name: tree.tied(name, sent[t]), lambda v, name=name: send(v, name))
 
     def quarters(value, which_bit):
         middle = value.shape[2] // 2
@@ -253,7 +333,7 @@
         return pick(first, low, high), pick(first, high, low).astype(BF)
 
     def sums():
-        total = jnp.stack([mm(hidden, down[0], NN), mm(grad_preact, up[0], NT)])
+        total = own_sum
         for name in names:
             total = total + tree.result(name).astype(F32)
         return quarters(total, 6)
@@ -262,20 +342,22 @@
     halves = lambda: quarters(sums()[0] + tree.result("q2").astype(F32), 5)
     tree.big("q1", lambda: tree.tied("q1", halves()[1]), lambda v: send(v, "z4"))
     back = tree.run()
-    mine = halves()[0] + tree.result("q1").astype(F32)
     hidden_rank, back_rank = back[:, :256], back[:, 256:]
+    narrow = jnp.stack([mm(inputs, back_rank, TN), mm(cotangent, hidden_rank, TN)]).astype(BF)
+
+    def total(part, other):
+        return (part.astype(F32) + other.astype(F32)).astype(BF)
+
+    grads = []
+    for i in range(len(EDGES) - 1):
+        got = tree.result(f"d{i}")
+        grads += list(total(chunk(i), got) if DMODE == "swap" else got)
+    other = swapped_dp(narrow if DMODE == "psum" and not NTIE else after(narrow, *[tree.result(f"d{i}") for i in range(len(EDGES) - 1)]))
+    last = tree.result("q1")
+    mine = halves()[0] + (bound(last, other) if "narrow" in REAL else last).astype(F32)
     outputs = (mine[0] + mm(hidden_rank, down_right, NN)).astype(BF)
     grad_inputs = (mine[1] + mm(back_rank, up_left, NT)).astype(BF)
-    narrow = jnp.stack([mm(inputs, back_rank, TN), mm(cotangent, hidden_rank, TN)]).astype(BF)
-
-    def total(part, other):
-        return (part.astype(F32) + other.astype(F32)).astype(BF)
-
-    grads = []
-    for i in range(PARTS):
-        got = tree.result(f"d{i}")
-        grads += list(total(chunk(i), got) if DMODE == "swap" else got)
-    narrow = total(narrow, swapped_dp(narrow if DMODE == "psum" and not NTIE else after(narrow, *[tree.result(f"d{i}") for i in range(PARTS)])))
+    narrow = total(narrow, other)
     return (
         outputs,
         grad_inputs,

time: 157 us -> 151 us (0.962)
  matrix products: 16.4 us -> 9.71 us
  other arithmetic: 8.45 us -> 3.01 us
  waiting for transfers between devices: 49.4 us -> 54.8 us
  local copies, waits for them, and re-layouts: 11.8 us -> 7.93 us
  Pallas kernels: 0 us -> 2.63 us
    ppermute x3, waiting for transfers between devices: 1.96 us -> 9.77 us  [swapped_dp(): return lax.ppermute(value, 'dp', [(0, 1), (1, 0)])]
    dot_general x48 -> x32, matrix products: 16.4 us -> 9.71 us  [mm(): return lax.dot_general(a, b, (dims, ((), ())), preferred_element_type=F32)]
    another operation x7 -> x0, other arithmetic: 3.78 us -> none  [the longest x5 3.71 us: term(): jnp.stack([mm(left, down[t], NN).astype(BF), mm(right, up[t], NT).astype(...]
    squeeze x5 -> x6, local copies, waits for them, and re-layouts: 3.41 us -> 0.21 us  [the longest x4 0.14 us: shards(): pre = sum((mm(rows[t][0], up[t], NN) for t in range(terms)))]
    pallas_call x0 -> x1, Pallas kernels: none -> 2.63 us  [between(): pl.pallas_call(middle, grid_spec=pltpu.PrefetchScalarGridSpec(num_scalar_...]
    ppermute x41 -> x40, waiting for transfers between devices: 47.5 us -> 45 us  [send(): return lax.ppermute(value, 'mp', ROUTES[route])]
    add x2 -> x0, local copies, waits for them, and re-layouts: 2.22 us -> none  [run(): self.value = pick(side, low, high) + send(give, route).astype(F32)]
    unnamed x70 -> x26, local copies, waits for them, and re-layouts: 1.4 us -> 3.34 us
  transfers between devices with their start and end apart: 44 -> 43, of which waited for: 19 -> 24; matrix products, arithmetic and copies ran while one was open for 18% -> 9% of each run, Pallas kernels for 0% -> 0%
where the time goes in v3:
time: 151 us; the launch traced here: 149 us
  starting transfers between devices  68.8 us (46%)
  waiting for transfers between devices  54.8 us (36%)
  matrix products  9.71 us (6%)
  local copies, waits for them, and re-layouts  7.93 us (5%)
  other arithmetic  3.01 us (2%)
  Pallas kernels  2.63 us (2%)
  between operations  2.07 us (1%)
    ppermute x40, starting transfers between devices, send(): return lax.ppermute(value, 'mp', ROUTES[route])  67 us
    ppermute x40, waiting for transfers between devices, send(): return lax.ppermute(value, 'mp', ROUTES[route])  45 us
    ppermute x3, waiting for transfers between devices, swapped_dp(): return lax.ppermute(value, 'dp', [(0, 1), (1, 0)])  9.77 us
    dot_general x32, matrix products, mm(): return lax.dot_general(a, b, (dims, ((), ())), preferred_element_type=F32)  9.71 us
    unnamed x26, local copies, waits for them, and re-layouts  3.34 us
  transfers between devices with their start and end apart: 43, of which 24 were waited for; matrix products, arithmetic and copies ran while one was open for 9% of the time, Pallas kernels for 0%

profile of v3, /device:TPU:32, one launch (start us, length us, event | category | flops | bytes accessed | tf_op | source)
XLA Modules:
  0.0 148.9 jit_solution(15796831618450614289)
XLA Ops:
  3.9 6.4 %collective-permute-start = (bf16[2,512,64]{1,2,0:T(8,128)(2,1)S(1)}, bf16[2,512,64]{1,2,0:T(8,128)(2,1)S(1)}, u32[]{:S(2)}, u32[]{:S(2)}) collective-permute-start(bf16[2,512,64]{1,2,0:T(8,128)(2,1)S(1)} %pad_maximum_fusion.3), channel_id=1, source_target_pairs={{0,32},{1,33},{2,34},{3,35},{4,36},{5,37},{6,38},{7,39},{8,40},{9,... | collective-permute-start | bytes 393224 | tf_op jit(solution)/shard_map/ppermute | solution.py:59
  10.4 3.3 %collective-permute-start.10 = (bf16[64,512]{1,0:T(8,128)(2,1)S(1)}, bf16[64,512]{1,0:T(8,128)(2,1)S(1)}, u32[]{:S(2)}, u32[]{:S(2)}) collective-permute-start(bf16[64,512]{1,0:T(8,128)(2,1)S(1)} %get-tuple-element.66), channel_id=1, source_target_pairs={{0,4},{1,5},{2,6},{3,7},{4,0},{5,1},{6,2},{7,3},{8,12},{9,13},{10,... | collective-permute-start | bytes 196616 | tf_op jit(solution)/shard_map/ppermute | solution.py:59
  14.8 2.5 %collective-permute-done = bf16[2,512,64]{1,2,0:T(8,128)(2,1)S(1)} collective-permute-done((bf16[2,512,64]{1,2,0:T(8,128)(2,1)S(1)}, bf16[2,512,64]{1,2,0:T(8,128)(2,1)S(1)}, u32[]{:S(2)}, u32[]{:S(2)}) %collective-permute-start) | collective-permute-done | bytes 131104 | tf_op jit(solution)/shard_map/ppermute | solution.py:59
  17.4 3.1 %collective-permute-start.1 = (bf16[2,512,128]{1,2,0:T(8,128)(2,1)S(1)}, bf16[2,512,128]{1,2,0:T(8,128)(2,1)S(1)}, u32[]{:S(2)}, u32[]{:S(2)}) collective-permute-start(bf16[2,512,128]{1,2,0:T(8,128)(2,1)S(1)} %maximum_select_fusion.2), channel_id=1, source_target_pairs={{0,64},{1,65},{2,66},{3,67},{4,68},{5,69},{6,70},{7,71},{8,72},{9,... | collective-permute-start | bytes 786440 | tf_op jit(solution)/shard_map/ppermute | solution.py:59
  20.6 4.9 %collective-permute-done.5 = bf16[2,512,128]{1,2,0:T(8,128)(2,1)S(1)} collective-permute-done((bf16[2,512,128]{1,2,0:T(8,128)(2,1)S(1)}, bf16[2,512,128]{1,2,0:T(8,128)(2,1)S(1)}, u32[]{:S(2)}, u32[]{:S(2)}) %collective-permute-start.5) | collective-permute-done | bytes 262176 | tf_op jit(solution)/shard_map/ppermute | solution.py:59
  27.3 3.3 %collective-permute-start.2 = (bf16[2,512,256]{1,2,0:T(8,128)(2,1)S(1)}, bf16[2,512,256]{1,2,0:T(8,128)(2,1)S(1)}, u32[]{:S(2)}, u32[]{:S(2)}) collective-permute-start(bf16[2,512,256]{1,2,0:T(8,128)(2,1)S(1)} %maximum_select_fusion), channel_id=1, source_target_pairs={{0,4},{1,5},{2,6},{3,7},{4,0},{5,1},{6,2},{7,3},{8,12},{9,13},{10,... | collective-permute-start | bytes 1572872 | tf_op jit(solution)/shard_map/ppermute | solution.py:59
  32.7 2.9 %collective-permute-done.12 = bf16[64,512]{1,0:T(8,128)(2,1)S(1)} collective-permute-done((bf16[64,512]{1,0:T(8,128)(2,1)S(1)}, bf16[64,512]{1,0:T(8,128)(2,1)S(1)}, u32[]{:S(2)}, u32[]{:S(2)}) %collective-permute-start.12) | collective-permute-done | bytes 65568 | tf_op jit(solution)/shard_map/ppermute | solution.py:59
  35.7 5.0 %collective-permute-start.15 = (bf16[64,512]{1,0:T(8,128)(2,1)S(1)}, bf16[64,512]{1,0:T(8,128)(2,1)S(1)}, u32[]{:S(2)}, u32[]{:S(2)}) collective-permute-start(bf16[64,512]{1,0:T(8,128)(2,1)S(1)} %get-tuple-element.144), channel_id=1, source_target_pairs={{0,24},{1,25},{2,26},{3,27},{4,28},{5,29},{6,30},{7,31},{8,48},{9,... | collective-permute-start | bytes 196616 | tf_op jit(solution)/shard_map/ppermute | solution.py:59
  40.9 3.1 %collective-permute-start.6 = (bf16[2,512,128]{1,2,0:T(8,128)(2,1)S(1)}, bf16[2,512,128]{1,2,0:T(8,128)(2,1)S(1)}, u32[]{:S(2)}, u32[]{:S(2)}) collective-permute-start(bf16[2,512,128]{1,2,0:T(8,128)(2,1)S(1)} %collective-permute-done.5), channel_id=1, source_target_pairs={{0,64},{1,65},{2,66},{3,67},{4,68},{5,69},{6,70},{7,71},{8,72},{9,... | collective-permute-start | bytes 786440 | tf_op jit(solution)/shard_map/ppermute | solution.py:59
  46.2 3.2 %collective-permute-start.13 = (bf16[512,256]{0,1:T(8,128)(2,1)S(1)}, bf16[512,256]{0,1:T(8,128)(2,1)S(1)}, u32[]{:S(2)}, u32[]{:S(2)}) collective-permute-start(bf16[512,256]{0,1:T(8,128)(2,1)S(1)} %get-tuple-element.102), channel_id=1, source_target_pairs={{0,16},{1,17},{2,18},{3,19},{4,20},{5,21},{6,22},{7,23},{8,24},{9,... | collective-permute-start | bytes 786440 | tf_op jit(solution)/shard_map/ppermute | solution.py:59
  49.9 4.7 %collective-permute-start.14 = (bf16[512,256]{0,1:T(8,128)(2,1)S(1)}, bf16[512,256]{0,1:T(8,128)(2,1)S(1)}, u32[]{:S(2)}, u32[]{:S(2)}) collective-permute-start(bf16[512,256]{0,1:T(8,128)(2,1)S(1)} %get-tuple-element.88), channel_id=1, source_target_pairs={{0,48},{1,49},{2,50},{3,51},{4,52},{5,53},{6,54},{7,55},{8,56},{9,... | collective-permute-start | bytes 786440 | tf_op jit(solution)/shard_map/ppermute | solution.py:59
  68.3 2.6 %middle.1 = (bf16[2,512,256]{2,1,0:T(8,128)(2,1)S(1)}, bf16[256,512]{1,0:T(8,128)(2,1)S(1)}, f32[256,512]{1,0:T(8,128)S(1)}, f32[2,512,256]{2,1,0:T(8,128)S(1)},...) custom-call(s32[1]{0:T(128)} %bitcast.core_ref, ...), custom_call_target="tpu_custom_call" | custom-call | flops 1073741824 | bytes 9437184 | tf_op jit(solution)/shard_map/middle/pallas_call | solution.py:232
  76.2 2.2 %collective-permute-start.30 = (bf16[64,512]{1,0:T(8,128)(2,1)S(1)}, bf16[64,512]{1,0:T(8,128)(2,1)S(1)}, u32[]{:S(2)}, u32[]{:S(2)}) collective-permute-start(bf16[64,512]{1,0:T(8,128)(2,1)S(1)} %select_convert_fusion.4), channel_id=1, source_target_pairs={{0,6},{1,7},{2,4},{3,5},{4,2},{5,3},{6,0},{7,1},{8,14},{9,15},{10,... | collective-permute-start | bytes 196616 | tf_op jit(solution)/shard_map/ppermute | solution.py:59
  79.3 2.7 %collective-permute-done.31 = bf16[64,512]{1,0:T(8,128)(2,1)S(1)} collective-permute-done((bf16[64,512]{1,0:T(8,128)(2,1)S(1)}, bf16[64,512]{1,0:T(8,128)(2,1)S(1)}, u32[]{:S(2)}, u32[]{:S(2)}) %collective-permute-start.31) | collective-permute-done | bytes 65568 | tf_op jit(solution)/shard_map/ppermute | solution.py:59
  83.7 3.6 %collective-permute-start.32 = (bf16[64,512]{1,0:T(8,128)(2,1)S(1)}, bf16[64,512]{1,0:T(8,128)(2,1)S(1)}, u32[]{:S(2)}, u32[]{:S(2)}) collective-permute-start(bf16[64,512]{1,0:T(8,128)(2,1)S(1)} %get-tuple-element.134), channel_id=1, source_target_pairs={{0,64},{1,65},{2,66},{3,67},{4,68},{5,69},{6,70},{7,71},{8,72},{9,... | collective-permute-start | bytes 196616 | tf_op jit(solution)/shard_map/ppermute | solution.py:59
  91.1 3.6 %collective-permute-done.26 = bf16[2,512,256]{2,1,0:T(8,128)(2,1)S(1)} collective-permute-done((bf16[2,512,256]{2,1,0:T(8,128)(2,1)S(1)}, bf16[2,512,256]{2,1,0:T(8,128)(2,1)S(1)}, u32[]{:S(2)}, u32[]{:S(2)}) %collective-permute-start.26) | collective-permute-done | bytes 524320 | tf_op jit(solution)/shard_map/ppermute | solution.py:59
  94.7 2.6 %collective-permute-done.25 = bf16[2,512,256]{2,1,0:T(8,128)(2,1)S(1)} collective-permute-done((bf16[2,512,256]{2,1,0:T(8,128)(2,1)S(1)}, bf16[2,512,256]{2,1,0:T(8,128)(2,1)S(1)}, u32[]{:S(2)}, u32[]{:S(2)}) %collective-permute-start.25) | collective-permute-done | bytes 524320 | tf_op jit(solution)/shard_map/ppermute | solution.py:59
  98.3 3.3 %collective-permute-done.33 = bf16[64,512]{1,0:T(8,128)(2,1)S(1)} collective-permute-done((bf16[64,512]{1,0:T(8,128)(2,1)S(1)}, bf16[64,512]{1,0:T(8,128)(2,1)S(1)}, u32[]{:S(2)}, u32[]{:S(2)}) %collective-permute-start.33) | collective-permute-done | bytes 65568 | tf_op jit(solution)/shard_map/ppermute | solution.py:59
  102.6 3.0 %collective-permute-done.23 = bf16[2,512,256]{2,1,0:T(8,128)(2,1)S(1)} collective-permute-done((bf16[2,512,256]{2,1,0:T(8,128)(2,1)S(1)}, bf16[2,512,256]{2,1,0:T(8,128)(2,1)S(1)}, u32[]{:S(2)}, u32[]{:S(2)}) %collective-permute-start.23) | collective-permute-done | bytes 524320 | tf_op jit(solution)/shard_map/ppermute | solution.py:59
  106.0 3.6 %collective-permute-start.27 = (bf16[2,512,128]{2,1,0:T(8,128)(2,1)S(1)}, bf16[2,512,128]{2,1,0:T(8,128)(2,1)S(1)}, u32[]{:S(2)}, u32[]{:S(2)}) collective-permute-start(bf16[2,512,128]{2,1,0:T(8,128)(2,1)S(1)} %select_convert_fusion.1), channel_id=1, source_target_pairs={{0,64},{1,65},{2,66},{3,67},{4,68},{5,69},{6,70},{7,71},{8,72},{9,... | collective-permute-start | bytes 786440 | tf_op jit(solution)/shard_map/ppermute | solution.py:59
  111.7 6.0 %collective-permute-done.35 = bf16[64,512]{1,0:T(8,128)(2,1)S(1)} collective-permute-done((bf16[64,512]{1,0:T(8,128)(2,1)S(1)}, bf16[64,512]{1,0:T(8,128)(2,1)S(1)}, u32[]{:S(2)}, u32[]{:S(2)}) %collective-permute-start.35) | collective-permute-done | bytes 65568 | tf_op jit(solution)/shard_map/ppermute | solution.py:59
  118.2 2.6 %collective-permute-start.28 = (bf16[2,512,64]{2,1,0:T(8,128)(2,1)S(1)}, bf16[2,512,64]{2,1,0:T(8,128)(2,1)S(1)}, u32[]{:S(2)}, u32[]{:S(2)}) collective-permute-start(bf16[2,512,64]{2,1,0:T(8,128)(2,1)S(1)} %select_convert_fusion), channel_id=1, source_target_pairs={{0,32},{1,33},{2,34},{3,35},{4,36},{5,37},{6,38},{7,39},{8,40},{9,... | collective-permute-start | bytes 393224 | tf_op jit(solution)/shard_map/ppermute | solution.py:59
  121.1 2.4 %collective-permute-start.38 = (bf16[64,512]{1,0:T(8,128)(2,1)S(1)}, bf16[64,512]{1,0:T(8,128)(2,1)S(1)}, u32[]{:S(2)}, u32[]{:S(2)}) collective-permute-start(bf16[64,512]{1,0:T(8,128)(2,1)S(1)} %add_convert_fusion.3), channel_id=1, source_target_pairs={{0,4},{1,5},{2,6},{3,7},{4,0},{5,1},{6,2},{7,3},{8,12},{9,13},{10,... | collective-permute-start | bytes 196616 | tf_op jit(solution)/shard_map/ppermute | solution.py:59
  132.1 8.3 %collective-permute-done.41 = bf16[7,256,256]{2,1,0:T(8,128)(2,1)S(1)} collective-permute-done((bf16[7,256,256]{2,1,0:T(8,128)(2,1)S(1)}, bf16[7,256,256]{2,1,0:T(8,128)(2,1)S(1)}, u32[]{:S(2)}, u32[]{:S(2)}) %collective-permute-start.41) | collective-permute-done | bytes 917536 | tf_op jit(solution)/shard_map/ppermute | solution.py:63
  (178 shorter events, 58.0 us)
Async XLA Ops:
  3.7 6.5 %collective-permute-start.7 = (bf16[256,512]{1,0:T(8,128)(2,1)S(1)}, bf16[256,512]{1,0:T(8,128)(2,1)S(1)}, u32[]{:S(2)}, u32[]{:S(2)}) collective-permute-start(bf16[256,512]{1,0:T(8,128)(2,1)S(1)} %select_convert_fusion.2), channel_id=1, source_target_pairs={{0,1},{1,0},{2,3},{3,2},{4,5},{5,4},{6,7},{7,6},{8,9},{9,8},{10,11... | collective-permute-start | bytes 786440 | tf_op jit(solution)/shard_map/ppermute | solution.py:59
  3.9 13.4 %collective-permute-start = (bf16[2,512,64]{1,2,0:T(8,128)(2,1)S(1)}, bf16[2,512,64]{1,2,0:T(8,128)(2,1)S(1)}, u32[]{:S(2)}, u32[]{:S(2)}) collective-permute-start(bf16[2,512,64]{1,2,0:T(8,128)(2,1)S(1)} %pad_maximum_fusion.3), channel_id=1, source_target_pairs={{0,32},{1,33},{2,34},{3,35},{4,36},{5,37},{6,38},{7,39},{8,40},{9,... | collective-permute-start | bytes 393224 | tf_op jit(solution)/shard_map/ppermute | solution.py:59
  10.4 10.1 %collective-permute-start.10 = (bf16[64,512]{1,0:T(8,128)(2,1)S(1)}, bf16[64,512]{1,0:T(8,128)(2,1)S(1)}, u32[]{:S(2)}, u32[]{:S(2)}) collective-permute-start(bf16[64,512]{1,0:T(8,128)(2,1)S(1)} %get-tuple-element.66), channel_id=1, source_target_pairs={{0,4},{1,5},{2,6},{3,7},{4,0},{5,1},{6,2},{7,3},{8,12},{9,13},{10,... | collective-permute-start | bytes 196616 | tf_op jit(solution)/shard_map/ppermute | solution.py:59
  13.7 6.8 %collective-permute-start.9 = (bf16[64,512]{1,0:T(8,128)(2,1)S(1)}, bf16[64,512]{1,0:T(8,128)(2,1)S(1)}, u32[]{:S(2)}, u32[]{:S(2)}) collective-permute-start(bf16[64,512]{1,0:T(8,128)(2,1)S(1)} %select_convert_fusion.7), channel_id=1, source_target_pairs={{0,6},{1,7},{2,4},{3,5},{4,2},{5,3},{6,0},{7,1},{8,14},{9,15},{10,... | collective-permute-start | bytes 196616 | tf_op jit(solution)/shard_map/ppermute | solution.py:59
  17.3 8.2 %collective-permute-start.5 = (bf16[2,512,128]{1,2,0:T(8,128)(2,1)S(1)}, bf16[2,512,128]{1,2,0:T(8,128)(2,1)S(1)}, u32[]{:S(2)}, u32[]{:S(2)}) collective-permute-start(bf16[2,512,128]{1,2,0:T(8,128)(2,1)S(1)} %maximum_select_fusion.2), channel_id=1, source_target_pairs={{0,8},{1,9},{2,10},{3,11},{4,12},{5,13},{6,14},{7,15},{8,0},{9,1},... | collective-permute-start | bytes 786440 | tf_op jit(solution)/shard_map/ppermute | solution.py:59
  17.4 9.7 %collective-permute-start.1 = (bf16[2,512,128]{1,2,0:T(8,128)(2,1)S(1)}, bf16[2,512,128]{1,2,0:T(8,128)(2,1)S(1)}, u32[]{:S(2)}, u32[]{:S(2)}) collective-permute-start(bf16[2,512,128]{1,2,0:T(8,128)(2,1)S(1)} %maximum_select_fusion.2), channel_id=1, source_target_pairs={{0,64},{1,65},{2,66},{3,67},{4,68},{5,69},{6,70},{7,71},{8,72},{9,... | collective-permute-start | bytes 786440 | tf_op jit(solution)/shard_map/ppermute | solution.py:59
  27.3 28.2 %collective-permute-start.2 = (bf16[2,512,256]{1,2,0:T(8,128)(2,1)S(1)}, bf16[2,512,256]{1,2,0:T(8,128)(2,1)S(1)}, u32[]{:S(2)}, u32[]{:S(2)}) collective-permute-start(bf16[2,512,256]{1,2,0:T(8,128)(2,1)S(1)} %maximum_select_fusion), channel_id=1, source_target_pairs={{0,4},{1,5},{2,6},{3,7},{4,0},{5,1},{6,2},{7,3},{8,12},{9,13},{10,... | collective-permute-start | bytes 1572872 | tf_op jit(solution)/shard_map/ppermute | solution.py:59
  30.6 24.9 %collective-permute-start.4 = (bf16[2,512,256]{1,2,0:T(8,128)(2,1)S(1)}, bf16[2,512,256]{1,2,0:T(8,128)(2,1)S(1)}, u32[]{:S(2)}, u32[]{:S(2)}) collective-permute-start(bf16[2,512,256]{1,2,0:T(8,128)(2,1)S(1)} %maximum_select_fusion), channel_id=1, source_target_pairs={{0,2},{1,3},{2,0},{3,1},{4,6},{5,7},{6,4},{7,5},{8,10},{9,11},{10,... | collective-permute-start | bytes 1572872 | tf_op jit(solution)/shard_map/ppermute | solution.py:59
  35.7 8.4 %collective-permute-start.15 = (bf16[64,512]{1,0:T(8,128)(2,1)S(1)}, bf16[64,512]{1,0:T(8,128)(2,1)S(1)}, u32[]{:S(2)}, u32[]{:S(2)}) collective-permute-start(bf16[64,512]{1,0:T(8,128)(2,1)S(1)} %get-tuple-element.144), channel_id=1, source_target_pairs={{0,24},{1,25},{2,26},{3,27},{4,28},{5,29},{6,30},{7,31},{8,48},{9,... | collective-permute-start | bytes 196616 | tf_op jit(solution)/shard_map/ppermute | solution.py:59
  40.9 13.8 %collective-permute-start.6 = (bf16[2,512,128]{1,2,0:T(8,128)(2,1)S(1)}, bf16[2,512,128]{1,2,0:T(8,128)(2,1)S(1)}, u32[]{:S(2)}, u32[]{:S(2)}) collective-permute-start(bf16[2,512,128]{1,2,0:T(8,128)(2,1)S(1)} %collective-permute-done.5), channel_id=1, source_target_pairs={{0,64},{1,65},{2,66},{3,67},{4,68},{5,69},{6,70},{7,71},{8,72},{9,... | collective-permute-start | bytes 786440 | tf_op jit(solution)/shard_map/ppermute | solution.py:59
  46.2 20.9 %collective-permute-start.13 = (bf16[512,256]{0,1:T(8,128)(2,1)S(1)}, bf16[512,256]{0,1:T(8,128)(2,1)S(1)}, u32[]{:S(2)}, u32[]{:S(2)}) collective-permute-start(bf16[512,256]{0,1:T(8,128)(2,1)S(1)} %get-tuple-element.102), channel_id=1, source_target_pairs={{0,16},{1,17},{2,18},{3,19},{4,20},{5,21},{6,22},{7,23},{8,24},{9,... | collective-permute-start | bytes 786440 | tf_op jit(solution)/shard_map/ppermute | solution.py:59
  49.9 17.4 %collective-permute-start.14 = (bf16[512,256]{0,1:T(8,128)(2,1)S(1)}, bf16[512,256]{0,1:T(8,128)(2,1)S(1)}, u32[]{:S(2)}, u32[]{:S(2)}) collective-permute-start(bf16[512,256]{0,1:T(8,128)(2,1)S(1)} %get-tuple-element.88), channel_id=1, source_target_pairs={{0,48},{1,49},{2,50},{3,51},{4,52},{5,53},{6,54},{7,55},{8,56},{9,... | collective-permute-start | bytes 786440 | tf_op jit(solution)/shard_map/ppermute | solution.py:59
  71.2 23.5 %collective-permute-start.26 = (bf16[2,512,256]{2,1,0:T(8,128)(2,1)S(1)}, bf16[2,512,256]{2,1,0:T(8,128)(2,1)S(1)}, u32[]{:S(2)}, u32[]{:S(2)}) collective-permute-start(bf16[2,512,256]{2,1,0:T(8,128)(2,1)S(1)} %get-tuple-element.81), channel_id=1, source_target_pairs={{0,16},{1,17},{2,18},{3,19},{4,20},{5,21},{6,22},{7,23},{8,24},{9,... | collective-permute-start | bytes 1572872 | tf_op jit(solution)/shard_map/ppermute | solution.py:59
  71.7 25.6 %collective-permute-start.25 = (bf16[2,512,256]{2,1,0:T(8,128)(2,1)S(1)}, bf16[2,512,256]{2,1,0:T(8,128)(2,1)S(1)}, u32[]{:S(2)}, u32[]{:S(2)}) collective-permute-start(bf16[2,512,256]{2,1,0:T(8,128)(2,1)S(1)} %get-tuple-element.80), channel_id=1, source_target_pairs={{0,8},{1,9},{2,10},{3,11},{4,12},{5,13},{6,14},{7,15},{8,0},{9,1},... | collective-permute-start | bytes 1572872 | tf_op jit(solution)/shard_map/ppermute | solution.py:59
  76.2 6.5 %collective-permute-start.30 = (bf16[64,512]{1,0:T(8,128)(2,1)S(1)}, bf16[64,512]{1,0:T(8,128)(2,1)S(1)}, u32[]{:S(2)}, u32[]{:S(2)}) collective-permute-start(bf16[64,512]{1,0:T(8,128)(2,1)S(1)} %select_convert_fusion.4), channel_id=1, source_target_pairs={{0,6},{1,7},{2,4},{3,5},{4,2},{5,3},{6,0},{7,1},{8,14},{9,15},{10,... | collective-permute-start | bytes 196616 | tf_op jit(solution)/shard_map/ppermute | solution.py:59
  82.0 20.7 %collective-permute-start.24 = (bf16[2,512,256]{2,1,0:T(8,128)(2,1)S(1)}, bf16[2,512,256]{2,1,0:T(8,128)(2,1)S(1)}, u32[]{:S(2)}, u32[]{:S(2)}) collective-permute-start(bf16[2,512,256]{2,1,0:T(8,128)(2,1)S(1)} %get-tuple-element.79), channel_id=1, source_target_pairs={{0,4},{1,5},{2,6},{3,7},{4,0},{5,1},{6,2},{7,3},{8,12},{9,13},{10,... | collective-permute-start | bytes 1572872 | tf_op jit(solution)/shard_map/ppermute | solution.py:59
  82.7 22.9 %collective-permute-start.23 = (bf16[2,512,256]{2,1,0:T(8,128)(2,1)S(1)}, bf16[2,512,256]{2,1,0:T(8,128)(2,1)S(1)}, u32[]{:S(2)}, u32[]{:S(2)}) collective-permute-start(bf16[2,512,256]{2,1,0:T(8,128)(2,1)S(1)} %get-tuple-element.77), channel_id=1, source_target_pairs={{0,2},{1,3},{2,0},{3,1},{4,6},{5,7},{6,4},{7,5},{8,10},{9,11},{10,... | collective-permute-start | bytes 1572872 | tf_op jit(solution)/shard_map/ppermute | solution.py:59
  83.7 6.7 %collective-permute-start.32 = (bf16[64,512]{1,0:T(8,128)(2,1)S(1)}, bf16[64,512]{1,0:T(8,128)(2,1)S(1)}, u32[]{:S(2)}, u32[]{:S(2)}) collective-permute-start(bf16[64,512]{1,0:T(8,128)(2,1)S(1)} %get-tuple-element.134), channel_id=1, source_target_pairs={{0,64},{1,65},{2,66},{3,67},{4,68},{5,69},{6,70},{7,71},{8,72},{9,... | collective-permute-start | bytes 196616 | tf_op jit(solution)/shard_map/ppermute | solution.py:59
  90.4 30.6 %collective-permute-start.36 = (bf16[7,256,256]{2,1,0:T(8,128)(2,1)S(1)}, bf16[7,256,256]{2,1,0:T(8,128)(2,1)S(1)}, u32[]{:S(2)}, u32[]{:S(2)}) collective-permute-start(bf16[7,256,256]{2,1,0:T(8,128)(2,1)S(1)} %fusion.17), channel_id=1, source_target_pairs={{0,128},{128,0},{1,129},{129,1},{2,130},{130,2},{3,131},{131,3},{4... | collective-permute-start | bytes 2752520 | tf_op jit(solution)/shard_map/ppermute | solution.py:63
  101.6 8.1 %collective-permute-start.34 = (bf16[64,512]{1,0:T(8,128)(2,1)S(1)}, bf16[64,512]{1,0:T(8,128)(2,1)S(1)}, u32[]{:S(2)}, u32[]{:S(2)}) collective-permute-start(bf16[64,512]{1,0:T(8,128)(2,1)S(1)} %fusion.83), channel_id=1, source_target_pairs={{0,56},{1,57},{2,58},{3,59},{4,60},{5,61},{6,62},{7,63},{8,16},{9,... | collective-permute-start | bytes 196616 | tf_op jit(solution)/shard_map/ppermute | solution.py:59
  106.0 11.9 %collective-permute-start.27 = (bf16[2,512,128]{2,1,0:T(8,128)(2,1)S(1)}, bf16[2,512,128]{2,1,0:T(8,128)(2,1)S(1)}, u32[]{:S(2)}, u32[]{:S(2)}) collective-permute-start(bf16[2,512,128]{2,1,0:T(8,128)(2,1)S(1)} %select_convert_fusion.1), channel_id=1, source_target_pairs={{0,64},{1,65},{2,66},{3,67},{4,68},{5,69},{6,70},{7,71},{8,72},{9,... | collective-permute-start | bytes 786440 | tf_op jit(solution)/shard_map/ppermute | solution.py:59
  109.7 8.1 %collective-permute-start.35 = (bf16[64,512]{1,0:T(8,128)(2,1)S(1)}, bf16[64,512]{1,0:T(8,128)(2,1)S(1)}, u32[]{:S(2)}, u32[]{:S(2)}) collective-permute-start(bf16[64,512]{1,0:T(8,128)(2,1)S(1)} %fusion.82), channel_id=1, source_target_pairs={{0,24},{1,25},{2,26},{3,27},{4,28},{5,29},{6,30},{7,31},{8,48},{9,... | collective-permute-start | bytes 196616 | tf_op jit(solution)/shard_map/ppermute | solution.py:59
  118.2 27.6 %collective-permute-start.28 = (bf16[2,512,64]{2,1,0:T(8,128)(2,1)S(1)}, bf16[2,512,64]{2,1,0:T(8,128)(2,1)S(1)}, u32[]{:S(2)}, u32[]{:S(2)}) collective-permute-start(bf16[2,512,64]{2,1,0:T(8,128)(2,1)S(1)} %select_convert_fusion), channel_id=1, source_target_pairs={{0,32},{1,33},{2,34},{3,35},{4,36},{5,37},{6,38},{7,39},{8,40},{9,... | collective-permute-start | bytes 393224 | tf_op jit(solution)/shard_map/ppermute | solution.py:59
  120.8 19.5 %collective-permute-start.41 = (bf16[7,256,256]{2,1,0:T(8,128)(2,1)S(1)}, bf16[7,256,256]{2,1,0:T(8,128)(2,1)S(1)}, u32[]{:S(2)}, u32[]{:S(2)}) collective-permute-start(bf16[7,256,256]{2,1,0:T(8,128)(2,1)S(1)} %fusion.31), channel_id=1, source_target_pairs={{0,128},{128,0},{1,129},{129,1},{2,130},{130,2},{3,131},{131,3},{4... | collective-permute-start | bytes 2752520 | tf_op jit(solution)/shard_map/ppermute | solution.py:63
  (27 other events, 116.9 us)

commit v4 on v3

--- a/solution.py
+++ b/solution.py
@@ -1,3 +1,5 @@
+from functools import partial
+
 import jax
 import jax.numpy as jnp
 from jax import lax
@@ -21,13 +23,15 @@
 SPLIT = ('z2',)
 NTIE = False
 KSTEPS = 2
-STEPS_C = ['h:core', 'y:halve', 'a:x2', 'a:z1', 'a:zn', 'a:zf', 'y:join', 'j:core']
-STARTS_C = {'y1': 0, 'y2': 0, 'd0': 2, 'd1': 'q2'}
-ENDS_C = {'core': 1, 'z1': 3, 'z2': 3, 'y2': 6, 'y1': 6, 'd0': 6}
-EDGES = (0, 7, 14)
-WAITS = (1, 1)
+LATE = ()
+OUTT = False
+STEPS_C = ['h:core', 'h:y1', 'h:y3', 'a:x2', 'a:z1', 'a:zn', 'a:zf', 'y:rejoin', 'j:core']
+STARTS_C = {'y1': 2, 'y2': 2, 'd1': 3, 'd2': 'q2'}
+ENDS_C = {'core': 1, 'z1': 4, 'z2': 7, 'y2': 7, 'y1': 7, 'd0': 3, 'd1': 7}
+EDGES = (0, 3, 10, 14)
+WAITS = (None, 2, 2)
 DMODE = 'swap'
-REAL = ('narrow',)
+REAL = ('narrow', 'q1s')
 
 
 def by_mask(mask):
@@ -111,7 +115,7 @@
         if step is None:
             return value
         hold = bound if name + "s" in REAL else after
-        return hold(value, self.result(step) if isinstance(step, str) else self.history[step])
+        return hold(value, self.history[step] if step in self.history else self.result(step))
 
     def direct(self, way, first):
         mine = bit_value(1) + 2 * bit_value(2)
@@ -126,8 +130,11 @@
         else:
             own = after(self.value.astype(BF), *first)
             got = {1: send(own, "y1"), 3: send(own, "y3"), 2: send(own, "y2")}
+            self.history["y2"] = got[2]
+            self.history["y3"] = got[3]
             parts = [own, got[1], got[2], got[3]]
-            self.value = jnp.concatenate([lax.select_n(mine ^ k, *parts) for k in range(4)], axis=0)
+            order = (0, 3, 1, 2) if way == "rejoin" else range(4)
+            self.value = jnp.concatenate([lax.select_n(mine ^ k, *parts) for k in order], axis=0)
 
     def run(self):
         self.history = {}
@@ -181,11 +188,15 @@
 TN = ((0,), (0,))
 
 
-def middle(core_ref, pre_ref, grad_ref, rank_ref, up_ref, down_ref, up_right_ref, down_left_ref, *outs):
+def middle(late, core_ref, pre_ref, grad_ref, rank_ref, up_ref, down_ref, up_right_ref, down_left_ref, *outs):
+    rows_refs, outs = outs[: 2 * len(late)], outs[2 * len(late) :]
     act_ref, give_ref, keep_ref, own_ref = outs[:4]
     width = pre_ref.shape[1]
     v = pre_ref[...] + mm(rank_ref[:, :width], up_right_ref[...], NN)
     g = grad_ref[...] + mm(rank_ref[:, width:], down_left_ref[...], NT)
+    for i, term in enumerate(late):
+        v = v + mm(rows_refs[2 * i][...], up_ref[term], NN)
+        g = g + mm(rows_refs[2 * i + 1][...], down_ref[term], NT)
     scale = 0.7978845608028654
     square = v * v
     t = jnp.tanh(scale * (v + 0.044715 * (square * v)))
@@ -212,7 +223,7 @@
         out[1] = mm(grad, up_ref[t_index], NT).astype(out.dtype)
 
 
-def between(pre, grad, ranks, up, down, up_right, down_left):
+def between(pre, grad, ranks, up, down, up_right, down_left, late):
     rows, width = pre.shape
     terms = up.shape[0]
     steps = KSTEPS
@@ -230,7 +241,7 @@
     pair = lambda dtype: jax.ShapeDtypeStruct((2, rows, width), dtype)
     ranks_half = lambda dtype: jax.ShapeDtypeStruct((rows // 2, 2 * width), dtype)
     return pl.pallas_call(
-        middle,
+        partial(middle, tuple(late)),
         grid_spec=pltpu.PrefetchScalarGridSpec(
             num_scalar_prefetch=1,
             grid=(steps,),
@@ -242,14 +253,15 @@
                 whole(down.shape),
                 whole(up_right.shape),
                 whole(down_left.shape),
-            ],
+            ]
+            + [by_rows(width)] * (2 * len(late)),
             out_specs=[by_pair, first, second] + [by_pair] * terms,
         ),
         out_shape=[pair(BF), ranks_half(BF), ranks_half(F32), pair(F32)] + [pair(BF)] * (terms - 1),
         compiler_params=pltpu.CompilerParams(vmem_limit_bytes=24 << 20),
         cost_estimate=pl.CostEstimate(flops=2 * 16 * rows * width * width, bytes_accessed=9 << 20, transcendentals=rows * width),
         name="middle",
-    )(core, pre, grad, ranks, up, down, up_right, down_left)
+    )(core, pre, grad, ranks, up, down, up_right, down_left, *[one for pair in late.values() for one in pair])
 
 
 def joined(which_bit, mine, other):
@@ -295,9 +307,10 @@
     rows = [own()] + [tree.result(name) for name in names]
     input_rank, cot_rank = ranks[:, :256], ranks[:, 256:]
 
-    pre = sum(mm(rows[t][0], up[t], NN) for t in range(terms))
-    grad = sum(mm(rows[t][1], down[t], NT) for t in range(terms))
-    act, give, keep, own_sum, *sent = between(pre, grad, ranks, up, down, up_right, down_left)
+    late = {t: (rows[t][0], rows[t][1]) for t in LATE}
+    pre = sum(mm(rows[t][0], up[t], NN) for t in range(terms) if t not in late)
+    grad = sum(mm(rows[t][1], down[t], NT) for t in range(terms) if t not in late)
+    act, give, keep, own_sum, *sent = between(pre, grad, ranks, up, down, up_right, down_left, late)
     hidden, grad_preact = act[0], act[1]
     tree = Tree((keep, give), STEPS_C, STARTS_C, ENDS_C)
     pairs = [(hidden, rows[t][1]) for t in range(terms)] + [(hidden, cot_rank)]
@@ -355,8 +368,12 @@
     other = swapped_dp(narrow if DMODE == "psum" and not NTIE else after(narrow, *[tree.result(f"d{i}") for i in range(len(EDGES) - 1)]))
     last = tree.result("q1")
     mine = halves()[0] + (bound(last, other) if "narrow" in REAL else last).astype(F32)
-    outputs = (mine[0] + mm(hidden_rank, down_right, NN)).astype(BF)
-    grad_inputs = (mine[1] + mm(back_rank, up_left, NT)).astype(BF)
+    if OUTT:
+        outputs = (mine[0].T + mm(down_right, hidden_rank, ((0,), (1,)))).astype(BF).T
+        grad_inputs = (mine[1].T + mm(up_left, back_rank, NT)).astype(BF).T
+    else:
+        outputs = (mine[0] + mm(hidden_rank, down_right, NN)).astype(BF)
+        grad_inputs = (mine[1] + mm(back_rank, up_left, NT)).astype(BF)
     narrow = total(narrow, other)
     return (
         outputs,

time: 151 us -> 148 us (0.980)
  waiting for transfers between devices: 54.8 us -> 49.6 us
  other arithmetic: 3.01 us -> 5.05 us
  local copies, waits for them, and re-layouts: 7.93 us -> 6.11 us
  starting transfers between devices: 68.8 us -> 70.5 us
    ppermute x3 -> x4, waiting for transfers between devices: 9.77 us -> 4.86 us  [swapped_dp(): return lax.ppermute(value, 'dp', [(0, 1), (1, 0)])]
    ppermute x3 -> x4, starting transfers between devices: 1.77 us -> 4.46 us  [swapped_dp(): return lax.ppermute(value, 'dp', [(0, 1), (1, 0)])]
    broadcast_in_dim x0 -> x2, other arithmetic: none -> 1.9 us  [the longest x1 0.95 us: shards(): jnp.stack(grads[:terms])[None]]
    broadcast_in_dim x2 -> x0, local copies, waits for them, and re-layouts: 1.86 us -> none  [the longest x1 0.93 us: shards(): jnp.stack(grads[:terms])[None]]
    ppermute x40 -> x39, starting transfers between devices: 67 us -> 66 us  [send(): return lax.ppermute(value, 'mp', ROUTES[route])]
    ppermute x40 -> x39, waiting for transfers between devices: 45 us -> 44.7 us  [send(): return lax.ppermute(value, 'mp', ROUTES[route])]
  transfers between devices with their start and end apart: 43 -> 43, of which waited for: 24 -> 22; matrix products, arithmetic and copies ran while one was open for 9% -> 9% of each run, Pallas kernels for 0% -> 0%
where the time goes in v4:
time: 148 us; the launch traced here: 146 us
  starting transfers between devices  70.5 us (48%)
  waiting for transfers between devices  49.6 us (34%)
  matrix products  9.69 us (7%)
  local copies, waits for them, and re-layouts  6.11 us (4%)
  other arithmetic  5.05 us (3%)
  Pallas kernels  2.63 us (2%)
  between operations  2.14 us (1%)
    ppermute x39, starting transfers between devices, send(): return lax.ppermute(value, 'mp', ROUTES[route])  66 us
    ppermute x39, waiting for transfers between devices, send(): return lax.ppermute(value, 'mp', ROUTES[route])  44.7 us
    dot_general x32, matrix products, mm(): return lax.dot_general(a, b, (dims, ((), ())), preferred_element_type=F32)  9.69 us
    ppermute x4, waiting for transfers between devices, swapped_dp(): return lax.ppermute(value, 'dp', [(0, 1), (1, 0)])  4.86 us
    ppermute x4, starting transfers between devices, swapped_dp(): return lax.ppermute(value, 'dp', [(0, 1), (1, 0)])  4.46 us
    unnamed x26, local copies, waits for them, and re-layouts  3.33 us
  transfers between devices with their start and end apart: 43, of which 22 were waited for; matrix products, arithmetic and copies ran while one was open for 9% of the time, Pallas kernels for 0%

profile of v4, /device:TPU:32, one launch (start us, length us, event | category | flops | bytes accessed | tf_op | source)
XLA Modules:
  0.0 145.7 jit_solution(16501056521666775696)
XLA Ops:
  3.9 6.4 %collective-permute-start = (bf16[2,512,64]{1,2,0:T(8,128)(2,1)S(1)}, bf16[2,512,64]{1,2,0:T(8,128)(2,1)S(1)}, u32[]{:S(2)}, u32[]{:S(2)}) collective-permute-start(bf16[2,512,64]{1,2,0:T(8,128)(2,1)S(1)} %pad_maximum_fusion.5), channel_id=1, source_target_pairs={{0,32},{1,33},{2,34},{3,35},{4,36},{5,37},{6,38},{7,39},{8,40},{9,... | collective-permute-start | bytes 393224 | tf_op jit(solution)/shard_map/ppermute | solution.py:63
  10.4 3.3 %collective-permute-start.5 = (bf16[64,512]{1,0:T(8,128)(2,1)S(1)}, bf16[64,512]{1,0:T(8,128)(2,1)S(1)}, u32[]{:S(2)}, u32[]{:S(2)}) collective-permute-start(bf16[64,512]{1,0:T(8,128)(2,1)S(1)} %get-tuple-element.58), channel_id=1, source_target_pairs={{0,4},{1,5},{2,6},{3,7},{4,0},{5,1},{6,2},{7,3},{8,12},{9,13},{10,... | collective-permute-start | bytes 196616 | tf_op jit(solution)/shard_map/ppermute | solution.py:63
  14.8 2.5 %collective-permute-done = bf16[2,512,64]{1,2,0:T(8,128)(2,1)S(1)} collective-permute-done((bf16[2,512,64]{1,2,0:T(8,128)(2,1)S(1)}, bf16[2,512,64]{1,2,0:T(8,128)(2,1)S(1)}, u32[]{:S(2)}, u32[]{:S(2)}) %collective-permute-start) | collective-permute-done | bytes 131104 | tf_op jit(solution)/shard_map/ppermute | solution.py:63
  17.4 3.1 %collective-permute-start.1 = (bf16[2,512,128]{1,2,0:T(8,128)(2,1)S(1)}, bf16[2,512,128]{1,2,0:T(8,128)(2,1)S(1)}, u32[]{:S(2)}, u32[]{:S(2)}) collective-permute-start(bf16[2,512,128]{1,2,0:T(8,128)(2,1)S(1)} %maximum_select_fusion.2), channel_id=1, source_target_pairs={{0,64},{1,65},{2,66},{3,67},{4,68},{5,69},{6,70},{7,71},{8,72},{9,... | collective-permute-start | bytes 786440 | tf_op jit(solution)/shard_map/ppermute | solution.py:63
  20.6 4.9 %collective-permute-done.6 = bf16[2,512,128]{1,2,0:T(8,128)(2,1)S(1)} collective-permute-done((bf16[2,512,128]{1,2,0:T(8,128)(2,1)S(1)}, bf16[2,512,128]{1,2,0:T(8,128)(2,1)S(1)}, u32[]{:S(2)}, u32[]{:S(2)}) %collective-permute-start.6) | collective-permute-done | bytes 262176 | tf_op jit(solution)/shard_map/ppermute | solution.py:63
  27.3 3.3 %collective-permute-start.12 = (bf16[2,512,256]{1,2,0:T(8,128)(2,1)S(1)}, bf16[2,512,256]{1,2,0:T(8,128)(2,1)S(1)}, u32[]{:S(2)}, u32[]{:S(2)}) collective-permute-start(bf16[2,512,256]{1,2,0:T(8,128)(2,1)S(1)} %maximum_select_fusion), channel_id=1, source_target_pairs={{0,4},{1,5},{2,6},{3,7},{4,0},{5,1},{6,2},{7,3},{8,12},{9,13},{10,... | collective-permute-start | bytes 1572872 | tf_op jit(solution)/shard_map/ppermute | solution.py:63
  32.7 2.9 %collective-permute-done.8 = bf16[64,512]{1,0:T(8,128)(2,1)S(1)} collective-permute-done((bf16[64,512]{1,0:T(8,128)(2,1)S(1)}, bf16[64,512]{1,0:T(8,128)(2,1)S(1)}, u32[]{:S(2)}, u32[]{:S(2)}) %collective-permute-start.8) | collective-permute-done | bytes 65568 | tf_op jit(solution)/shard_map/ppermute | solution.py:63
  35.7 5.0 %collective-permute-start.9 = (bf16[64,512]{1,0:T(8,128)(2,1)S(1)}, bf16[64,512]{1,0:T(8,128)(2,1)S(1)}, u32[]{:S(2)}, u32[]{:S(2)}) collective-permute-start(bf16[64,512]{1,0:T(8,128)(2,1)S(1)} %get-tuple-element.130), channel_id=1, source_target_pairs={{0,24},{1,25},{2,26},{3,27},{4,28},{5,29},{6,30},{7,31},{8,48},{9,... | collective-permute-start | bytes 196616 | tf_op jit(solution)/shard_map/ppermute | solution.py:63
  40.9 3.1 %collective-permute-start.11 = (bf16[2,512,128]{1,2,0:T(8,128)(2,1)S(1)}, bf16[2,512,128]{1,2,0:T(8,128)(2,1)S(1)}, u32[]{:S(2)}, u32[]{:S(2)}) collective-permute-start(bf16[2,512,128]{1,2,0:T(8,128)(2,1)S(1)} %collective-permute-done.6), channel_id=1, source_target_pairs={{0,64},{1,65},{2,66},{3,67},{4,68},{5,69},{6,70},{7,71},{8,72},{9,... | collective-permute-start | bytes 786440 | tf_op jit(solution)/shard_map/ppermute | solution.py:63
  46.2 3.2 %collective-permute-start.16 = (bf16[512,256]{0,1:T(8,128)(2,1)S(1)}, bf16[512,256]{0,1:T(8,128)(2,1)S(1)}, u32[]{:S(2)}, u32[]{:S(2)}) collective-permute-start(bf16[512,256]{0,1:T(8,128)(2,1)S(1)} %get-tuple-element.87), channel_id=1, source_target_pairs={{0,16},{1,17},{2,18},{3,19},{4,20},{5,21},{6,22},{7,23},{8,24},{9,... | collective-permute-start | bytes 786440 | tf_op jit(solution)/shard_map/ppermute | solution.py:63
  49.9 4.7 %collective-permute-start.17 = (bf16[512,256]{0,1:T(8,128)(2,1)S(1)}, bf16[512,256]{0,1:T(8,128)(2,1)S(1)}, u32[]{:S(2)}, u32[]{:S(2)}) collective-permute-start(bf16[512,256]{0,1:T(8,128)(2,1)S(1)} %get-tuple-element.64), channel_id=1, source_target_pairs={{0,48},{1,49},{2,50},{3,51},{4,52},{5,53},{6,54},{7,55},{8,56},{9,... | collective-permute-start | bytes 786440 | tf_op jit(solution)/shard_map/ppermute | solution.py:63
  69.0 2.6 %middle.1 = (bf16[2,512,256]{2,1,0:T(8,128)(2,1)S(1)}, bf16[256,512]{1,0:T(8,128)(2,1)S(1)}, f32[256,512]{1,0:T(8,128)S(1)}, f32[2,512,256]{2,1,0:T(8,128)S(1)},...) custom-call(s32[1]{0:T(128)} %bitcast.core_ref, ...), custom_call_target="tpu_custom_call" | custom-call | flops 1073741824 | bytes 9437184 | tf_op jit(solution)/shard_map/middle/pallas_call | solution.py:243
  77.6 5.1 %collective-permute-done.23 = bf16[128,512]{1,0:T(8,128)(2,1)S(1)} collective-permute-done((bf16[128,512]{1,0:T(8,128)(2,1)S(1)}, bf16[128,512]{1,0:T(8,128)(2,1)S(1)}, u32[]{:S(2)}, u32[]{:S(2)}) %collective-permute-start.23) | collective-permute-done | bytes 131104 | tf_op jit(solution)/shard_map/ppermute | solution.py:63
  84.0 2.8 %collective-permute-done.31 = bf16[3,256,256]{2,1,0:T(8,128)(2,1)S(1)} collective-permute-done((bf16[3,256,256]{2,1,0:T(8,128)(2,1)S(1)}, bf16[3,256,256]{2,1,0:T(8,128)(2,1)S(1)}, u32[]{:S(2)}, u32[]{:S(2)}) %collective-permute-start.31) | collective-permute-done | bytes 393248 | tf_op jit(solution)/shard_map/ppermute | solution.py:67
  90.5 3.3 %collective-permute-start.32 = (bf16[64,512]{1,0:T(8,128)(2,1)S(1)}, bf16[64,512]{1,0:T(8,128)(2,1)S(1)}, u32[]{:S(2)}, u32[]{:S(2)}) collective-permute-start(bf16[64,512]{1,0:T(8,128)(2,1)S(1)} %get-tuple-element.77), channel_id=1, source_target_pairs={{0,64},{1,65},{2,66},{3,67},{4,68},{5,69},{6,70},{7,71},{8,72},{9,... | collective-permute-start | bytes 196616 | tf_op jit(solution)/shard_map/ppermute | solution.py:63
  98.3 4.0 %collective-permute-done.33 = bf16[64,512]{1,0:T(8,128)(2,1)S(1)} collective-permute-done((bf16[64,512]{1,0:T(8,128)(2,1)S(1)}, bf16[64,512]{1,0:T(8,128)(2,1)S(1)}, u32[]{:S(2)}, u32[]{:S(2)}) %collective-permute-start.33) | collective-permute-done | bytes 65568 | tf_op jit(solution)/shard_map/ppermute | solution.py:63
  103.6 3.1 %collective-permute-done.34 = bf16[64,512]{1,0:T(8,128)(2,1)S(1)} collective-permute-done((bf16[64,512]{1,0:T(8,128)(2,1)S(1)}, bf16[64,512]{1,0:T(8,128)(2,1)S(1)}, u32[]{:S(2)}, u32[]{:S(2)}) %collective-permute-start.34) | collective-permute-done | bytes 65568 | tf_op jit(solution)/shard_map/ppermute | solution.py:63
  106.7 2.2 %collective-permute-start.35 = (bf16[64,512]{1,0:T(8,128)(2,1)S(1)}, bf16[64,512]{1,0:T(8,128)(2,1)S(1)}, u32[]{:S(2)}, u32[]{:S(2)}) collective-permute-start(bf16[64,512]{1,0:T(8,128)(2,1)S(1)} %fusion.75), channel_id=1, source_target_pairs={{0,24},{1,25},{2,26},{3,27},{4,28},{5,29},{6,30},{7,31},{8,48},{9,... | collective-permute-start | bytes 196616 | tf_op jit(solution)/shard_map/ppermute | solution.py:63
  109.0 2.4 %collective-permute-done.25 = bf16[2,512,256]{2,1,0:T(8,128)(2,1)S(1)} collective-permute-done((bf16[2,512,256]{2,1,0:T(8,128)(2,1)S(1)}, bf16[2,512,256]{2,1,0:T(8,128)(2,1)S(1)}, u32[]{:S(2)}, u32[]{:S(2)}) %collective-permute-start.25) | collective-permute-done | bytes 524320 | tf_op jit(solution)/shard_map/ppermute | solution.py:63
  111.8 3.8 %collective-permute-start.29 = (bf16[2,512,128]{2,1,0:T(8,128)(2,1)S(1)}, bf16[2,512,128]{2,1,0:T(8,128)(2,1)S(1)}, u32[]{:S(2)}, u32[]{:S(2)}) collective-permute-start(bf16[2,512,128]{2,1,0:T(8,128)(2,1)S(1)} %select_convert_fusion.1), channel_id=1, source_target_pairs={{0,64},{1,65},{2,66},{3,67},{4,68},{5,69},{6,70},{7,71},{8,72},{9,... | collective-permute-start | bytes 786440 | tf_op jit(solution)/shard_map/ppermute | solution.py:63
  115.8 6.8 %collective-permute-done.29 = bf16[2,512,128]{2,1,0:T(8,128)(2,1)S(1)} collective-permute-done((bf16[2,512,128]{2,1,0:T(8,128)(2,1)S(1)}, bf16[2,512,128]{2,1,0:T(8,128)(2,1)S(1)}, u32[]{:S(2)}, u32[]{:S(2)}) %collective-permute-start.29) | collective-permute-done | bytes 262176 | tf_op jit(solution)/shard_map/ppermute | solution.py:63
  122.8 3.0 %collective-permute-start.30 = (bf16[2,512,64]{2,1,0:T(8,128)(2,1)S(1)}, bf16[2,512,64]{2,1,0:T(8,128)(2,1)S(1)}, u32[]{:S(2)}, u32[]{:S(2)}) collective-permute-start(bf16[2,512,64]{2,1,0:T(8,128)(2,1)S(1)} %select_convert_fusion), channel_id=1, source_target_pairs={{0,32},{1,33},{2,34},{3,35},{4,36},{5,37},{6,38},{7,39},{8,40},{9,... | collective-permute-start | bytes 393224 | tf_op jit(solution)/shard_map/ppermute | solution.py:63
  125.9 2.2 %collective-permute-start.38 = (bf16[64,512]{1,0:T(8,128)(2,1)S(1)}, bf16[64,512]{1,0:T(8,128)(2,1)S(1)}, u32[]{:S(2)}, u32[]{:S(2)}) collective-permute-start(bf16[64,512]{1,0:T(8,128)(2,1)S(1)} %add_convert_fusion.4), channel_id=1, source_target_pairs={{0,4},{1,5},{2,6},{3,7},{4,0},{5,1},{6,2},{7,3},{8,12},{9,13},{10,... | collective-permute-start | bytes 196616 | tf_op jit(solution)/shard_map/ppermute | solution.py:63
  129.7 2.3 %collective-permute-done.38 = bf16[64,512]{1,0:T(8,128)(2,1)S(1)} collective-permute-done((bf16[64,512]{1,0:T(8,128)(2,1)S(1)}, bf16[64,512]{1,0:T(8,128)(2,1)S(1)}, u32[]{:S(2)}, u32[]{:S(2)}) %collective-permute-start.38) | collective-permute-done | bytes 65568 | tf_op jit(solution)/shard_map/ppermute | solution.py:63
  (184 shorter events, 57.5 us)
Async XLA Ops:
  3.7 6.5 %collective-permute-start.2 = (bf16[256,512]{1,0:T(8,128)(2,1)S(1)}, bf16[256,512]{1,0:T(8,128)(2,1)S(1)}, u32[]{:S(2)}, u32[]{:S(2)}) collective-permute-start(bf16[256,512]{1,0:T(8,128)(2,1)S(1)} %select_convert_fusion.2), channel_id=1, source_target_pairs={{0,1},{1,0},{2,3},{3,2},{4,5},{5,4},{6,7},{7,6},{8,9},{9,8},{10,11... | collective-permute-start | bytes 786440 | tf_op jit(solution)/shard_map/ppermute | solution.py:63
  3.9 13.4 %collective-permute-start = (bf16[2,512,64]{1,2,0:T(8,128)(2,1)S(1)}, bf16[2,512,64]{1,2,0:T(8,128)(2,1)S(1)}, u32[]{:S(2)}, u32[]{:S(2)}) collective-permute-start(bf16[2,512,64]{1,2,0:T(8,128)(2,1)S(1)} %pad_maximum_fusion.5), channel_id=1, source_target_pairs={{0,32},{1,33},{2,34},{3,35},{4,36},{5,37},{6,38},{7,39},{8,40},{9,... | collective-permute-start | bytes 393224 | tf_op jit(solution)/shard_map/ppermute | solution.py:63
  10.4 10.1 %collective-permute-start.5 = (bf16[64,512]{1,0:T(8,128)(2,1)S(1)}, bf16[64,512]{1,0:T(8,128)(2,1)S(1)}, u32[]{:S(2)}, u32[]{:S(2)}) collective-permute-start(bf16[64,512]{1,0:T(8,128)(2,1)S(1)} %get-tuple-element.58), channel_id=1, source_target_pairs={{0,4},{1,5},{2,6},{3,7},{4,0},{5,1},{6,2},{7,3},{8,12},{9,13},{10,... | collective-permute-start | bytes 196616 | tf_op jit(solution)/shard_map/ppermute | solution.py:63
  13.7 6.8 %collective-permute-start.4 = (bf16[64,512]{1,0:T(8,128)(2,1)S(1)}, bf16[64,512]{1,0:T(8,128)(2,1)S(1)}, u32[]{:S(2)}, u32[]{:S(2)}) collective-permute-start(bf16[64,512]{1,0:T(8,128)(2,1)S(1)} %select_convert_fusion.6), channel_id=1, source_target_pairs={{0,6},{1,7},{2,4},{3,5},{4,2},{5,3},{6,0},{7,1},{8,14},{9,15},{10,... | collective-permute-start | bytes 196616 | tf_op jit(solution)/shard_map/ppermute | solution.py:63
  17.3 8.2 %collective-permute-start.6 = (bf16[2,512,128]{1,2,0:T(8,128)(2,1)S(1)}, bf16[2,512,128]{1,2,0:T(8,128)(2,1)S(1)}, u32[]{:S(2)}, u32[]{:S(2)}) collective-permute-start(bf16[2,512,128]{1,2,0:T(8,128)(2,1)S(1)} %maximum_select_fusion.2), channel_id=1, source_target_pairs={{0,8},{1,9},{2,10},{3,11},{4,12},{5,13},{6,14},{7,15},{8,0},{9,1},... | collective-permute-start | bytes 786440 | tf_op jit(solution)/shard_map/ppermute | solution.py:63
  17.4 9.7 %collective-permute-start.1 = (bf16[2,512,128]{1,2,0:T(8,128)(2,1)S(1)}, bf16[2,512,128]{1,2,0:T(8,128)(2,1)S(1)}, u32[]{:S(2)}, u32[]{:S(2)}) collective-permute-start(bf16[2,512,128]{1,2,0:T(8,128)(2,1)S(1)} %maximum_select_fusion.2), channel_id=1, source_target_pairs={{0,64},{1,65},{2,66},{3,67},{4,68},{5,69},{6,70},{7,71},{8,72},{9,... | collective-permute-start | bytes 786440 | tf_op jit(solution)/shard_map/ppermute | solution.py:63
  27.3 28.2 %collective-permute-start.12 = (bf16[2,512,256]{1,2,0:T(8,128)(2,1)S(1)}, bf16[2,512,256]{1,2,0:T(8,128)(2,1)S(1)}, u32[]{:S(2)}, u32[]{:S(2)}) collective-permute-start(bf16[2,512,256]{1,2,0:T(8,128)(2,1)S(1)} %maximum_select_fusion), channel_id=1, source_target_pairs={{0,4},{1,5},{2,6},{3,7},{4,0},{5,1},{6,2},{7,3},{8,12},{9,13},{10,... | collective-permute-start | bytes 1572872 | tf_op jit(solution)/shard_map/ppermute | solution.py:63
  30.6 24.9 %collective-permute-start.13 = (bf16[2,512,256]{1,2,0:T(8,128)(2,1)S(1)}, bf16[2,512,256]{1,2,0:T(8,128)(2,1)S(1)}, u32[]{:S(2)}, u32[]{:S(2)}) collective-permute-start(bf16[2,512,256]{1,2,0:T(8,128)(2,1)S(1)} %maximum_select_fusion), channel_id=1, source_target_pairs={{0,2},{1,3},{2,0},{3,1},{4,6},{5,7},{6,4},{7,5},{8,10},{9,11},{10,... | collective-permute-start | bytes 1572872 | tf_op jit(solution)/shard_map/ppermute | solution.py:63
  35.7 8.4 %collective-permute-start.9 = (bf16[64,512]{1,0:T(8,128)(2,1)S(1)}, bf16[64,512]{1,0:T(8,128)(2,1)S(1)}, u32[]{:S(2)}, u32[]{:S(2)}) collective-permute-start(bf16[64,512]{1,0:T(8,128)(2,1)S(1)} %get-tuple-element.130), channel_id=1, source_target_pairs={{0,24},{1,25},{2,26},{3,27},{4,28},{5,29},{6,30},{7,31},{8,48},{9,... | collective-permute-start | bytes 196616 | tf_op jit(solution)/shard_map/ppermute | solution.py:63
  40.9 13.8 %collective-permute-start.11 = (bf16[2,512,128]{1,2,0:T(8,128)(2,1)S(1)}, bf16[2,512,128]{1,2,0:T(8,128)(2,1)S(1)}, u32[]{:S(2)}, u32[]{:S(2)}) collective-permute-start(bf16[2,512,128]{1,2,0:T(8,128)(2,1)S(1)} %collective-permute-done.6), channel_id=1, source_target_pairs={{0,64},{1,65},{2,66},{3,67},{4,68},{5,69},{6,70},{7,71},{8,72},{9,... | collective-permute-start | bytes 786440 | tf_op jit(solution)/shard_map/ppermute | solution.py:63
  44.1 5.9 %collective-permute-start.10 = (bf16[64,512]{1,0:T(8,128)(2,1)S(1)}, bf16[64,512]{1,0:T(8,128)(2,1)S(1)}, u32[]{:S(2)}, u32[]{:S(2)}) collective-permute-start(bf16[64,512]{1,0:T(8,128)(2,1)S(1)} %fusion.73), channel_id=1, source_target_pairs={{0,64},{1,65},{2,66},{3,67},{4,68},{5,69},{6,70},{7,71},{8,72},{9,... | collective-permute-start | bytes 196616 | tf_op jit(solution)/shard_map/ppermute | solution.py:63
  46.2 21.6 %collective-permute-start.16 = (bf16[512,256]{0,1:T(8,128)(2,1)S(1)}, bf16[512,256]{0,1:T(8,128)(2,1)S(1)}, u32[]{:S(2)}, u32[]{:S(2)}) collective-permute-start(bf16[512,256]{0,1:T(8,128)(2,1)S(1)} %get-tuple-element.87), channel_id=1, source_target_pairs={{0,16},{1,17},{2,18},{3,19},{4,20},{5,21},{6,22},{7,23},{8,24},{9,... | collective-permute-start | bytes 786440 | tf_op jit(solution)/shard_map/ppermute | solution.py:63
  49.9 18.1 %collective-permute-start.17 = (bf16[512,256]{0,1:T(8,128)(2,1)S(1)}, bf16[512,256]{0,1:T(8,128)(2,1)S(1)}, u32[]{:S(2)}, u32[]{:S(2)}) collective-permute-start(bf16[512,256]{0,1:T(8,128)(2,1)S(1)} %get-tuple-element.64), channel_id=1, source_target_pairs={{0,48},{1,49},{2,50},{3,51},{4,52},{5,53},{6,54},{7,55},{8,56},{9,... | collective-permute-start | bytes 786440 | tf_op jit(solution)/shard_map/ppermute | solution.py:63
  72.0 37.0 %collective-permute-start.28 = (bf16[2,512,256]{2,1,0:T(8,128)(2,1)S(1)}, bf16[2,512,256]{2,1,0:T(8,128)(2,1)S(1)}, u32[]{:S(2)}, u32[]{:S(2)}) collective-permute-start(bf16[2,512,256]{2,1,0:T(8,128)(2,1)S(1)} %get-tuple-element.75), channel_id=1, source_target_pairs={{0,16},{1,17},{2,18},{3,19},{4,20},{5,21},{6,22},{7,23},{8,24},{9,... | collective-permute-start | bytes 1572872 | tf_op jit(solution)/shard_map/ppermute | solution.py:63
  72.5 25.6 %collective-permute-start.27 = (bf16[2,512,256]{2,1,0:T(8,128)(2,1)S(1)}, bf16[2,512,256]{2,1,0:T(8,128)(2,1)S(1)}, u32[]{:S(2)}, u32[]{:S(2)}) collective-permute-start(bf16[2,512,256]{2,1,0:T(8,128)(2,1)S(1)} %get-tuple-element.74), channel_id=1, source_target_pairs={{0,8},{1,9},{2,10},{3,11},{4,12},{5,13},{6,14},{7,15},{8,0},{9,1},... | collective-permute-start | bytes 1572872 | tf_op jit(solution)/shard_map/ppermute | solution.py:63
  75.7 11.1 %collective-permute-start.31 = (bf16[3,256,256]{2,1,0:T(8,128)(2,1)S(1)}, bf16[3,256,256]{2,1,0:T(8,128)(2,1)S(1)}, u32[]{:S(2)}, u32[]{:S(2)}) collective-permute-start(bf16[3,256,256]{2,1,0:T(8,128)(2,1)S(1)} %pad_maximum_fusion.2), channel_id=1, source_target_pairs={{0,128},{128,0},{1,129},{129,1},{2,130},{130,2},{3,131},{131,3},{4... | collective-permute-start | bytes 1179656 | tf_op jit(solution)/shard_map/ppermute | solution.py:67
  88.3 20.7 %collective-permute-start.26 = (bf16[2,512,256]{2,1,0:T(8,128)(2,1)S(1)}, bf16[2,512,256]{2,1,0:T(8,128)(2,1)S(1)}, u32[]{:S(2)}, u32[]{:S(2)}) collective-permute-start(bf16[2,512,256]{2,1,0:T(8,128)(2,1)S(1)} %get-tuple-element.73), channel_id=1, source_target_pairs={{0,4},{1,5},{2,6},{3,7},{4,0},{5,1},{6,2},{7,3},{8,12},{9,13},{10,... | collective-permute-start | bytes 1572872 | tf_op jit(solution)/shard_map/ppermute | solution.py:63
  88.4 22.9 %collective-permute-start.25 = (bf16[2,512,256]{2,1,0:T(8,128)(2,1)S(1)}, bf16[2,512,256]{2,1,0:T(8,128)(2,1)S(1)}, u32[]{:S(2)}, u32[]{:S(2)}) collective-permute-start(bf16[2,512,256]{2,1,0:T(8,128)(2,1)S(1)} %get-tuple-element.71), channel_id=1, source_target_pairs={{0,2},{1,3},{2,0},{3,1},{4,6},{5,7},{6,4},{7,5},{8,10},{9,11},{10,... | collective-permute-start | bytes 1572872 | tf_op jit(solution)/shard_map/ppermute | solution.py:63
  96.2 29.6 %collective-permute-start.36 = (bf16[7,256,256]{2,1,0:T(8,128)(2,1)S(1)}, bf16[7,256,256]{2,1,0:T(8,128)(2,1)S(1)}, u32[]{:S(2)}, u32[]{:S(2)}) collective-permute-start(bf16[7,256,256]{2,1,0:T(8,128)(2,1)S(1)} %fusion.20), channel_id=1, source_target_pairs={{0,128},{128,0},{1,129},{129,1},{2,130},{130,2},{3,131},{131,3},{4... | collective-permute-start | bytes 2752520 | tf_op jit(solution)/shard_map/ppermute | solution.py:67
  106.7 9.0 %collective-permute-start.35 = (bf16[64,512]{1,0:T(8,128)(2,1)S(1)}, bf16[64,512]{1,0:T(8,128)(2,1)S(1)}, u32[]{:S(2)}, u32[]{:S(2)}) collective-permute-start(bf16[64,512]{1,0:T(8,128)(2,1)S(1)} %fusion.75), channel_id=1, source_target_pairs={{0,24},{1,25},{2,26},{3,27},{4,28},{5,29},{6,30},{7,31},{8,48},{9,... | collective-permute-start | bytes 196616 | tf_op jit(solution)/shard_map/ppermute | solution.py:63
  111.8 10.7 %collective-permute-start.29 = (bf16[2,512,128]{2,1,0:T(8,128)(2,1)S(1)}, bf16[2,512,128]{2,1,0:T(8,128)(2,1)S(1)}, u32[]{:S(2)}, u32[]{:S(2)}) collective-permute-start(bf16[2,512,128]{2,1,0:T(8,128)(2,1)S(1)} %select_convert_fusion.1), channel_id=1, source_target_pairs={{0,64},{1,65},{2,66},{3,67},{4,68},{5,69},{6,70},{7,71},{8,72},{9,... | collective-permute-start | bytes 786440 | tf_op jit(solution)/shard_map/ppermute | solution.py:63
  122.8 19.8 %collective-permute-start.30 = (bf16[2,512,64]{2,1,0:T(8,128)(2,1)S(1)}, bf16[2,512,64]{2,1,0:T(8,128)(2,1)S(1)}, u32[]{:S(2)}, u32[]{:S(2)}) collective-permute-start(bf16[2,512,64]{2,1,0:T(8,128)(2,1)S(1)} %select_convert_fusion), channel_id=1, source_target_pairs={{0,32},{1,33},{2,34},{3,35},{4,36},{5,37},{6,38},{7,39},{8,40},{9,... | collective-permute-start | bytes 393224 | tf_op jit(solution)/shard_map/ppermute | solution.py:63
  125.8 10.3 %collective-permute-start.41 = (bf16[4,256,256]{2,1,0:T(8,128)(2,1)S(1)}, bf16[4,256,256]{2,1,0:T(8,128)(2,1)S(1)}, u32[]{:S(2)}, u32[]{:S(2)}) collective-permute-start(bf16[4,256,256]{2,1,0:T(8,128)(2,1)S(1)} %pad_maximum_fusion.1), channel_id=1, source_target_pairs={{0,128},{128,0},{1,129},{129,1},{2,130},{130,2},{3,131},{131,3},{4... | collective-permute-start | bytes 1572872 | tf_op jit(solution)/shard_map/ppermute | solution.py:67
  125.9 6.1 %collective-permute-start.38 = (bf16[64,512]{1,0:T(8,128)(2,1)S(1)}, bf16[64,512]{1,0:T(8,128)(2,1)S(1)}, u32[]{:S(2)}, u32[]{:S(2)}) collective-permute-start(bf16[64,512]{1,0:T(8,128)(2,1)S(1)} %add_convert_fusion.4), channel_id=1, source_target_pairs={{0,4},{1,5},{2,6},{3,7},{4,0},{5,1},{6,2},{7,3},{8,12},{9,13},{10,... | collective-permute-start | bytes 196616 | tf_op jit(solution)/shard_map/ppermute | solution.py:63
  (27 other events, 113.4 us)

commit v5 on v4

--- a/solution.py
+++ b/solution.py
@@ -27,8 +27,8 @@
 OUTT = False
 STEPS_C = ['h:core', 'h:y1', 'h:y3', 'a:x2', 'a:z1', 'a:zn', 'a:zf', 'y:rejoin', 'j:core']
 STARTS_C = {'y1': 2, 'y2': 2, 'd1': 3, 'd2': 'q2'}
-ENDS_C = {'core': 1, 'z1': 4, 'z2': 7, 'y2': 7, 'y1': 7, 'd0': 3, 'd1': 7}
-EDGES = (0, 3, 10, 14)
+ENDS_C = {'core': 1, 'z1': 4, 'z2': 7, 'y2': 7, 'y1': 7, 'd0': 4, 'd1': 7}
+EDGES = (0, 4, 10, 14)
 WAITS = (None, 2, 2)
 DMODE = 'swap'
 REAL = ('narrow', 'q1s')

time: 148 us -> 149 us (level)
    ppermute x4, waiting for transfers between devices: 4.86 us -> 14.5 us  [swapped_dp(): return lax.ppermute(value, 'dp', [(0, 1), (1, 0)])]
    ppermute x39, waiting for transfers between devices: 44.7 us -> 36.2 us  [send(): return lax.ppermute(value, 'mp', ROUTES[route])]
    unnamed x26 -> x30, local copies, waits for them, and re-layouts: 3.33 us -> 3.39 us
  transfers between devices with their start and end apart: 43 -> 43, of which waited for: 22 -> 19; matrix products, arithmetic and copies ran while one was open for 9% -> 9% of each run, Pallas kernels for 0% -> 0%
where the time goes in v5:
time: 149 us; the launch traced here: 147 us
  starting transfers between devices  70.5 us (47%)
  waiting for transfers between devices  50.7 us (34%)
  matrix products  9.67 us (6%)
  local copies, waits for them, and re-layouts  6.11 us (4%)
  other arithmetic  5.03 us (3%)
  Pallas kernels  2.63 us (2%)
  between operations  2.21 us (1%)
    ppermute x39, starting transfers between devices, send(): return lax.ppermute(value, 'mp', ROUTES[route])  65.4 us
    ppermute x39, waiting for transfers between devices, send(): return lax.ppermute(value, 'mp', ROUTES[route])  36.2 us
    ppermute x4, waiting for transfers between devices, swapped_dp(): return lax.ppermute(value, 'dp', [(0, 1), (1, 0)])  14.5 us
    dot_general x32, matrix products, mm(): return lax.dot_general(a, b, (dims, ((), ())), preferred_element_type=F32)  9.67 us
    ppermute x4, starting transfers between devices, swapped_dp(): return lax.ppermute(value, 'dp', [(0, 1), (1, 0)])  5.03 us
    unnamed x30, local copies, waits for them, and re-layouts  3.39 us
  transfers between devices with their start and end apart: 43, of which 19 were waited for; matrix products, arithmetic and copies ran while one was open for 9% of the time, Pallas kernels for 0%

profile of v5, /device:TPU:32, one launch (start us, length us, event | category | flops | bytes accessed | tf_op | source)
XLA Modules:
  0.0 146.8 jit_solution(5780485231476435115)
XLA Ops:
  3.9 6.4 %collective-permute-start = (bf16[2,512,64]{1,2,0:T(8,128)(2,1)S(1)}, bf16[2,512,64]{1,2,0:T(8,128)(2,1)S(1)}, u32[]{:S(2)}, u32[]{:S(2)}) collective-permute-start(bf16[2,512,64]{1,2,0:T(8,128)(2,1)S(1)} %pad_maximum_fusion.5), channel_id=1, source_target_pairs={{0,32},{1,33},{2,34},{3,35},{4,36},{5,37},{6,38},{7,39},{8,40},{9,... | collective-permute-start | bytes 393224 | tf_op jit(solution)/shard_map/ppermute | solution.py:63
  10.4 3.3 %collective-permute-start.5 = (bf16[64,512]{1,0:T(8,128)(2,1)S(1)}, bf16[64,512]{1,0:T(8,128)(2,1)S(1)}, u32[]{:S(2)}, u32[]{:S(2)}) collective-permute-start(bf16[64,512]{1,0:T(8,128)(2,1)S(1)} %get-tuple-element.55), channel_id=1, source_target_pairs={{0,4},{1,5},{2,6},{3,7},{4,0},{5,1},{6,2},{7,3},{8,12},{9,13},{10,... | collective-permute-start | bytes 196616 | tf_op jit(solution)/shard_map/ppermute | solution.py:63
  14.8 2.5 %collective-permute-done = bf16[2,512,64]{1,2,0:T(8,128)(2,1)S(1)} collective-permute-done((bf16[2,512,64]{1,2,0:T(8,128)(2,1)S(1)}, bf16[2,512,64]{1,2,0:T(8,128)(2,1)S(1)}, u32[]{:S(2)}, u32[]{:S(2)}) %collective-permute-start) | collective-permute-done | bytes 131104 | tf_op jit(solution)/shard_map/ppermute | solution.py:63
  17.4 3.1 %collective-permute-start.1 = (bf16[2,512,128]{1,2,0:T(8,128)(2,1)S(1)}, bf16[2,512,128]{1,2,0:T(8,128)(2,1)S(1)}, u32[]{:S(2)}, u32[]{:S(2)}) collective-permute-start(bf16[2,512,128]{1,2,0:T(8,128)(2,1)S(1)} %maximum_select_fusion.2), channel_id=1, source_target_pairs={{0,64},{1,65},{2,66},{3,67},{4,68},{5,69},{6,70},{7,71},{8,72},{9,... | collective-permute-start | bytes 786440 | tf_op jit(solution)/shard_map/ppermute | solution.py:63
  20.6 4.9 %collective-permute-done.6 = bf16[2,512,128]{1,2,0:T(8,128)(2,1)S(1)} collective-permute-done((bf16[2,512,128]{1,2,0:T(8,128)(2,1)S(1)}, bf16[2,512,128]{1,2,0:T(8,128)(2,1)S(1)}, u32[]{:S(2)}, u32[]{:S(2)}) %collective-permute-start.6) | collective-permute-done | bytes 262176 | tf_op jit(solution)/shard_map/ppermute | solution.py:63
  27.3 3.3 %collective-permute-start.12 = (bf16[2,512,256]{1,2,0:T(8,128)(2,1)S(1)}, bf16[2,512,256]{1,2,0:T(8,128)(2,1)S(1)}, u32[]{:S(2)}, u32[]{:S(2)}) collective-permute-start(bf16[2,512,256]{1,2,0:T(8,128)(2,1)S(1)} %maximum_select_fusion), channel_id=1, source_target_pairs={{0,4},{1,5},{2,6},{3,7},{4,0},{5,1},{6,2},{7,3},{8,12},{9,13},{10,... | collective-permute-start | bytes 1572872 | tf_op jit(solution)/shard_map/ppermute | solution.py:63
  32.7 2.9 %collective-permute-done.8 = bf16[64,512]{1,0:T(8,128)(2,1)S(1)} collective-permute-done((bf16[64,512]{1,0:T(8,128)(2,1)S(1)}, bf16[64,512]{1,0:T(8,128)(2,1)S(1)}, u32[]{:S(2)}, u32[]{:S(2)}) %collective-permute-start.8) | collective-permute-done | bytes 65568 | tf_op jit(solution)/shard_map/ppermute | solution.py:63
  35.7 5.0 %collective-permute-start.9 = (bf16[64,512]{1,0:T(8,128)(2,1)S(1)}, bf16[64,512]{1,0:T(8,128)(2,1)S(1)}, u32[]{:S(2)}, u32[]{:S(2)}) collective-permute-start(bf16[64,512]{1,0:T(8,128)(2,1)S(1)} %get-tuple-element.124), channel_id=1, source_target_pairs={{0,24},{1,25},{2,26},{3,27},{4,28},{5,29},{6,30},{7,31},{8,48},{9,... | collective-permute-start | bytes 196616 | tf_op jit(solution)/shard_map/ppermute | solution.py:63
  40.9 3.1 %collective-permute-start.11 = (bf16[2,512,128]{1,2,0:T(8,128)(2,1)S(1)}, bf16[2,512,128]{1,2,0:T(8,128)(2,1)S(1)}, u32[]{:S(2)}, u32[]{:S(2)}) collective-permute-start(bf16[2,512,128]{1,2,0:T(8,128)(2,1)S(1)} %collective-permute-done.6), channel_id=1, source_target_pairs={{0,64},{1,65},{2,66},{3,67},{4,68},{5,69},{6,70},{7,71},{8,72},{9,... | collective-permute-start | bytes 786440 | tf_op jit(solution)/shard_map/ppermute | solution.py:63
  46.2 3.2 %collective-permute-start.16 = (bf16[512,256]{0,1:T(8,128)(2,1)S(1)}, bf16[512,256]{0,1:T(8,128)(2,1)S(1)}, u32[]{:S(2)}, u32[]{:S(2)}) collective-permute-start(bf16[512,256]{0,1:T(8,128)(2,1)S(1)} %get-tuple-element.81), channel_id=1, source_target_pairs={{0,16},{1,17},{2,18},{3,19},{4,20},{5,21},{6,22},{7,23},{8,24},{9,... | collective-permute-start | bytes 786440 | tf_op jit(solution)/shard_map/ppermute | solution.py:63
  49.9 4.7 %collective-permute-start.17 = (bf16[512,256]{0,1:T(8,128)(2,1)S(1)}, bf16[512,256]{0,1:T(8,128)(2,1)S(1)}, u32[]{:S(2)}, u32[]{:S(2)}) collective-permute-start(bf16[512,256]{0,1:T(8,128)(2,1)S(1)} %get-tuple-element.61), channel_id=1, source_target_pairs={{0,48},{1,49},{2,50},{3,51},{4,52},{5,53},{6,54},{7,55},{8,56},{9,... | collective-permute-start | bytes 786440 | tf_op jit(solution)/shard_map/ppermute | solution.py:63
  57.5 2.2 %collective-permute-start.19 = (bf16[64,512]{1,0:T(8,128)(2,1)S(1)}, bf16[64,512]{1,0:T(8,128)(2,1)S(1)}, u32[]{:S(2)}, u32[]{:S(2)}) collective-permute-start(bf16[64,512]{1,0:T(8,128)(2,1)S(1)} %add_convert_fusion.5), channel_id=1, source_target_pairs={{0,6},{1,7},{2,4},{3,5},{4,2},{5,3},{6,0},{7,1},{8,14},{9,15},{10,... | collective-permute-start | bytes 196616 | tf_op jit(solution)/shard_map/ppermute | solution.py:63
  69.0 2.6 %middle.1 = (bf16[2,512,256]{2,1,0:T(8,128)(2,1)S(1)}, bf16[256,512]{1,0:T(8,128)(2,1)S(1)}, f32[256,512]{1,0:T(8,128)S(1)}, f32[2,512,256]{2,1,0:T(8,128)S(1)},...) custom-call(s32[1]{0:T(128)} %bitcast.core_ref, ...), custom_call_target="tpu_custom_call" | custom-call | flops 1073741824 | bytes 9437184 | tf_op jit(solution)/shard_map/middle/pallas_call | solution.py:243
  77.9 5.1 %collective-permute-done.23 = bf16[128,512]{1,0:T(8,128)(2,1)S(1)} collective-permute-done((bf16[128,512]{1,0:T(8,128)(2,1)S(1)}, bf16[128,512]{1,0:T(8,128)(2,1)S(1)}, u32[]{:S(2)}, u32[]{:S(2)}) %collective-permute-start.23) | collective-permute-done | bytes 131104 | tf_op jit(solution)/shard_map/ppermute | solution.py:63
  84.3 5.6 %collective-permute-done.32 = bf16[4,256,256]{2,1,0:T(8,128)(2,1)S(1)} collective-permute-done((bf16[4,256,256]{2,1,0:T(8,128)(2,1)S(1)}, bf16[4,256,256]{2,1,0:T(8,128)(2,1)S(1)}, u32[]{:S(2)}, u32[]{:S(2)}) %collective-permute-start.32) | collective-permute-done | bytes 524320 | tf_op jit(solution)/shard_map/ppermute | solution.py:67
  92.3 3.5 %collective-permute-start.31 = (bf16[64,512]{1,0:T(8,128)(2,1)S(1)}, bf16[64,512]{1,0:T(8,128)(2,1)S(1)}, u32[]{:S(2)}, u32[]{:S(2)}) collective-permute-start(bf16[64,512]{1,0:T(8,128)(2,1)S(1)} %get-tuple-element.114), channel_id=1, source_target_pairs={{0,64},{1,65},{2,66},{3,67},{4,68},{5,69},{6,70},{7,71},{8,72},{9,... | collective-permute-start | bytes 196616 | tf_op jit(solution)/shard_map/ppermute | solution.py:63
  100.0 4.0 %collective-permute-done.33 = bf16[64,512]{1,0:T(8,128)(2,1)S(1)} collective-permute-done((bf16[64,512]{1,0:T(8,128)(2,1)S(1)}, bf16[64,512]{1,0:T(8,128)(2,1)S(1)}, u32[]{:S(2)}, u32[]{:S(2)}) %collective-permute-start.33) | collective-permute-done | bytes 65568 | tf_op jit(solution)/shard_map/ppermute | solution.py:63
  105.2 3.1 %collective-permute-done.34 = bf16[64,512]{1,0:T(8,128)(2,1)S(1)} collective-permute-done((bf16[64,512]{1,0:T(8,128)(2,1)S(1)}, bf16[64,512]{1,0:T(8,128)(2,1)S(1)}, u32[]{:S(2)}, u32[]{:S(2)}) %collective-permute-start.34) | collective-permute-done | bytes 65568 | tf_op jit(solution)/shard_map/ppermute | solution.py:63
  108.3 2.2 %collective-permute-start.35 = (bf16[64,512]{1,0:T(8,128)(2,1)S(1)}, bf16[64,512]{1,0:T(8,128)(2,1)S(1)}, u32[]{:S(2)}, u32[]{:S(2)}) collective-permute-start(bf16[64,512]{1,0:T(8,128)(2,1)S(1)} %fusion.74), channel_id=1, source_target_pairs={{0,24},{1,25},{2,26},{3,27},{4,28},{5,29},{6,30},{7,31},{8,48},{9,... | collective-permute-start | bytes 196616 | tf_op jit(solution)/shard_map/ppermute | solution.py:63
  110.6 5.1 %collective-permute-done.35 = bf16[64,512]{1,0:T(8,128)(2,1)S(1)} collective-permute-done((bf16[64,512]{1,0:T(8,128)(2,1)S(1)}, bf16[64,512]{1,0:T(8,128)(2,1)S(1)}, u32[]{:S(2)}, u32[]{:S(2)}) %collective-permute-start.35) | collective-permute-done | bytes 65568 | tf_op jit(solution)/shard_map/ppermute | solution.py:63
  116.2 2.9 %collective-permute-start.29 = (bf16[2,512,128]{2,1,0:T(8,128)(2,1)S(1)}, bf16[2,512,128]{2,1,0:T(8,128)(2,1)S(1)}, u32[]{:S(2)}, u32[]{:S(2)}) collective-permute-start(bf16[2,512,128]{2,1,0:T(8,128)(2,1)S(1)} %select_convert_fusion.1), channel_id=1, source_target_pairs={{0,64},{1,65},{2,66},{3,67},{4,68},{5,69},{6,70},{7,71},{8,72},{9,... | collective-permute-start | bytes 786440 | tf_op jit(solution)/shard_map/ppermute | solution.py:63
  119.2 2.8 %collective-permute-start.38 = (bf16[64,512]{1,0:T(8,128)(2,1)S(1)}, bf16[64,512]{1,0:T(8,128)(2,1)S(1)}, u32[]{:S(2)}, u32[]{:S(2)}) collective-permute-start(bf16[64,512]{1,0:T(8,128)(2,1)S(1)} %add_convert_fusion.4), channel_id=1, source_target_pairs={{0,4},{1,5},{2,6},{3,7},{4,0},{5,1},{6,2},{7,3},{8,12},{9,13},{10,... | collective-permute-start | bytes 196616 | tf_op jit(solution)/shard_map/ppermute | solution.py:63
  124.4 2.9 %collective-permute-start.30 = (bf16[2,512,64]{2,1,0:T(8,128)(2,1)S(1)}, bf16[2,512,64]{2,1,0:T(8,128)(2,1)S(1)}, u32[]{:S(2)}, u32[]{:S(2)}) collective-permute-start(bf16[2,512,64]{2,1,0:T(8,128)(2,1)S(1)} %select_convert_fusion), channel_id=1, source_target_pairs={{0,32},{1,33},{2,34},{3,35},{4,36},{5,37},{6,38},{7,39},{8,40},{9,... | collective-permute-start | bytes 393224 | tf_op jit(solution)/shard_map/ppermute | solution.py:63
  130.5 7.0 %collective-permute-done.41 = bf16[4,256,256]{2,1,0:T(8,128)(2,1)S(1)} collective-permute-done((bf16[4,256,256]{2,1,0:T(8,128)(2,1)S(1)}, bf16[4,256,256]{2,1,0:T(8,128)(2,1)S(1)}, u32[]{:S(2)}, u32[]{:S(2)}) %collective-permute-start.41) | collective-permute-done | bytes 524320 | tf_op jit(solution)/shard_map/ppermute | solution.py:67
  (191 shorter events, 53.3 us)
Async XLA Ops:
  3.7 6.5 %collective-permute-start.2 = (bf16[256,512]{1,0:T(8,128)(2,1)S(1)}, bf16[256,512]{1,0:T(8,128)(2,1)S(1)}, u32[]{:S(2)}, u32[]{:S(2)}) collective-permute-start(bf16[256,512]{1,0:T(8,128)(2,1)S(1)} %select_convert_fusion.2), channel_id=1, source_target_pairs={{0,1},{1,0},{2,3},{3,2},{4,5},{5,4},{6,7},{7,6},{8,9},{9,8},{10,11... | collective-permute-start | bytes 786440 | tf_op jit(solution)/shard_map/ppermute | solution.py:63
  3.9 13.4 %collective-permute-start = (bf16[2,512,64]{1,2,0:T(8,128)(2,1)S(1)}, bf16[2,512,64]{1,2,0:T(8,128)(2,1)S(1)}, u32[]{:S(2)}, u32[]{:S(2)}) collective-permute-start(bf16[2,512,64]{1,2,0:T(8,128)(2,1)S(1)} %pad_maximum_fusion.5), channel_id=1, source_target_pairs={{0,32},{1,33},{2,34},{3,35},{4,36},{5,37},{6,38},{7,39},{8,40},{9,... | collective-permute-start | bytes 393224 | tf_op jit(solution)/shard_map/ppermute | solution.py:63
  10.4 10.1 %collective-permute-start.5 = (bf16[64,512]{1,0:T(8,128)(2,1)S(1)}, bf16[64,512]{1,0:T(8,128)(2,1)S(1)}, u32[]{:S(2)}, u32[]{:S(2)}) collective-permute-start(bf16[64,512]{1,0:T(8,128)(2,1)S(1)} %get-tuple-element.55), channel_id=1, source_target_pairs={{0,4},{1,5},{2,6},{3,7},{4,0},{5,1},{6,2},{7,3},{8,12},{9,13},{10,... | collective-permute-start | bytes 196616 | tf_op jit(solution)/shard_map/ppermute | solution.py:63
  13.7 6.8 %collective-permute-start.4 = (bf16[64,512]{1,0:T(8,128)(2,1)S(1)}, bf16[64,512]{1,0:T(8,128)(2,1)S(1)}, u32[]{:S(2)}, u32[]{:S(2)}) collective-permute-start(bf16[64,512]{1,0:T(8,128)(2,1)S(1)} %select_convert_fusion.6), channel_id=1, source_target_pairs={{0,6},{1,7},{2,4},{3,5},{4,2},{5,3},{6,0},{7,1},{8,14},{9,15},{10,... | collective-permute-start | bytes 196616 | tf_op jit(solution)/shard_map/ppermute | solution.py:63
  17.3 8.2 %collective-permute-start.6 = (bf16[2,512,128]{1,2,0:T(8,128)(2,1)S(1)}, bf16[2,512,128]{1,2,0:T(8,128)(2,1)S(1)}, u32[]{:S(2)}, u32[]{:S(2)}) collective-permute-start(bf16[2,512,128]{1,2,0:T(8,128)(2,1)S(1)} %maximum_select_fusion.2), channel_id=1, source_target_pairs={{0,8},{1,9},{2,10},{3,11},{4,12},{5,13},{6,14},{7,15},{8,0},{9,1},... | collective-permute-start | bytes 786440 | tf_op jit(solution)/shard_map/ppermute | solution.py:63
  17.4 9.7 %collective-permute-start.1 = (bf16[2,512,128]{1,2,0:T(8,128)(2,1)S(1)}, bf16[2,512,128]{1,2,0:T(8,128)(2,1)S(1)}, u32[]{:S(2)}, u32[]{:S(2)}) collective-permute-start(bf16[2,512,128]{1,2,0:T(8,128)(2,1)S(1)} %maximum_select_fusion.2), channel_id=1, source_target_pairs={{0,64},{1,65},{2,66},{3,67},{4,68},{5,69},{6,70},{7,71},{8,72},{9,... | collective-permute-start | bytes 786440 | tf_op jit(solution)/shard_map/ppermute | solution.py:63
  27.3 28.2 %collective-permute-start.12 = (bf16[2,512,256]{1,2,0:T(8,128)(2,1)S(1)}, bf16[2,512,256]{1,2,0:T(8,128)(2,1)S(1)}, u32[]{:S(2)}, u32[]{:S(2)}) collective-permute-start(bf16[2,512,256]{1,2,0:T(8,128)(2,1)S(1)} %maximum_select_fusion), channel_id=1, source_target_pairs={{0,4},{1,5},{2,6},{3,7},{4,0},{5,1},{6,2},{7,3},{8,12},{9,13},{10,... | collective-permute-start | bytes 1572872 | tf_op jit(solution)/shard_map/ppermute | solution.py:63
  30.6 24.9 %collective-permute-start.13 = (bf16[2,512,256]{1,2,0:T(8,128)(2,1)S(1)}, bf16[2,512,256]{1,2,0:T(8,128)(2,1)S(1)}, u32[]{:S(2)}, u32[]{:S(2)}) collective-permute-start(bf16[2,512,256]{1,2,0:T(8,128)(2,1)S(1)} %maximum_select_fusion), channel_id=1, source_target_pairs={{0,2},{1,3},{2,0},{3,1},{4,6},{5,7},{6,4},{7,5},{8,10},{9,11},{10,... | collective-permute-start | bytes 1572872 | tf_op jit(solution)/shard_map/ppermute | solution.py:63
  35.7 8.4 %collective-permute-start.9 = (bf16[64,512]{1,0:T(8,128)(2,1)S(1)}, bf16[64,512]{1,0:T(8,128)(2,1)S(1)}, u32[]{:S(2)}, u32[]{:S(2)}) collective-permute-start(bf16[64,512]{1,0:T(8,128)(2,1)S(1)} %get-tuple-element.124), channel_id=1, source_target_pairs={{0,24},{1,25},{2,26},{3,27},{4,28},{5,29},{6,30},{7,31},{8,48},{9,... | collective-permute-start | bytes 196616 | tf_op jit(solution)/shard_map/ppermute | solution.py:63
  40.9 13.8 %collective-permute-start.11 = (bf16[2,512,128]{1,2,0:T(8,128)(2,1)S(1)}, bf16[2,512,128]{1,2,0:T(8,128)(2,1)S(1)}, u32[]{:S(2)}, u32[]{:S(2)}) collective-permute-start(bf16[2,512,128]{1,2,0:T(8,128)(2,1)S(1)} %collective-permute-done.6), channel_id=1, source_target_pairs={{0,64},{1,65},{2,66},{3,67},{4,68},{5,69},{6,70},{7,71},{8,72},{9,... | collective-permute-start | bytes 786440 | tf_op jit(solution)/shard_map/ppermute | solution.py:63
  46.2 21.6 %collective-permute-start.16 = (bf16[512,256]{0,1:T(8,128)(2,1)S(1)}, bf16[512,256]{0,1:T(8,128)(2,1)S(1)}, u32[]{:S(2)}, u32[]{:S(2)}) collective-permute-start(bf16[512,256]{0,1:T(8,128)(2,1)S(1)} %get-tuple-element.81), channel_id=1, source_target_pairs={{0,16},{1,17},{2,18},{3,19},{4,20},{5,21},{6,22},{7,23},{8,24},{9,... | collective-permute-start | bytes 786440 | tf_op jit(solution)/shard_map/ppermute | solution.py:63
  49.9 18.1 %collective-permute-start.17 = (bf16[512,256]{0,1:T(8,128)(2,1)S(1)}, bf16[512,256]{0,1:T(8,128)(2,1)S(1)}, u32[]{:S(2)}, u32[]{:S(2)}) collective-permute-start(bf16[512,256]{0,1:T(8,128)(2,1)S(1)} %get-tuple-element.61), channel_id=1, source_target_pairs={{0,48},{1,49},{2,50},{3,51},{4,52},{5,53},{6,54},{7,55},{8,56},{9,... | collective-permute-start | bytes 786440 | tf_op jit(solution)/shard_map/ppermute | solution.py:63
  72.0 43.8 %collective-permute-start.28 = (bf16[2,512,256]{2,1,0:T(8,128)(2,1)S(1)}, bf16[2,512,256]{2,1,0:T(8,128)(2,1)S(1)}, u32[]{:S(2)}, u32[]{:S(2)}) collective-permute-start(bf16[2,512,256]{2,1,0:T(8,128)(2,1)S(1)} %get-tuple-element.72), channel_id=1, source_target_pairs={{0,16},{1,17},{2,18},{3,19},{4,20},{5,21},{6,22},{7,23},{8,24},{9,... | collective-permute-start | bytes 1572872 | tf_op jit(solution)/shard_map/ppermute | solution.py:63
  72.5 27.1 %collective-permute-start.27 = (bf16[2,512,256]{2,1,0:T(8,128)(2,1)S(1)}, bf16[2,512,256]{2,1,0:T(8,128)(2,1)S(1)}, u32[]{:S(2)}, u32[]{:S(2)}) collective-permute-start(bf16[2,512,256]{2,1,0:T(8,128)(2,1)S(1)} %get-tuple-element.71), channel_id=1, source_target_pairs={{0,8},{1,9},{2,10},{3,11},{4,12},{5,13},{6,14},{7,15},{8,0},{9,1},... | collective-permute-start | bytes 1572872 | tf_op jit(solution)/shard_map/ppermute | solution.py:63
  76.0 13.9 %collective-permute-start.32 = (bf16[4,256,256]{2,1,0:T(8,128)(2,1)S(1)}, bf16[4,256,256]{2,1,0:T(8,128)(2,1)S(1)}, u32[]{:S(2)}, u32[]{:S(2)}) collective-permute-start(bf16[4,256,256]{2,1,0:T(8,128)(2,1)S(1)} %pad_maximum_fusion.1), channel_id=1, source_target_pairs={{0,128},{128,0},{1,129},{129,1},{2,130},{130,2},{3,131},{131,3},{4... | collective-permute-start | bytes 1572872 | tf_op jit(solution)/shard_map/ppermute | solution.py:67
  83.0 7.1 %collective-permute-start.24 = (bf16[64,512]{1,0:T(8,128)(2,1)S(1)}, bf16[64,512]{1,0:T(8,128)(2,1)S(1)}, u32[]{:S(2)}, u32[]{:S(2)}) collective-permute-start(bf16[64,512]{1,0:T(8,128)(2,1)S(1)} %select_convert_fusion.4), channel_id=1, source_target_pairs={{0,6},{1,7},{2,4},{3,5},{4,2},{5,3},{6,0},{7,1},{8,14},{9,15},{10,... | collective-permute-start | bytes 196616 | tf_op jit(solution)/shard_map/ppermute | solution.py:63
  90.1 25.6 %collective-permute-start.26 = (bf16[2,512,256]{2,1,0:T(8,128)(2,1)S(1)}, bf16[2,512,256]{2,1,0:T(8,128)(2,1)S(1)}, u32[]{:S(2)}, u32[]{:S(2)}) collective-permute-start(bf16[2,512,256]{2,1,0:T(8,128)(2,1)S(1)} %get-tuple-element.70), channel_id=1, source_target_pairs={{0,4},{1,5},{2,6},{3,7},{4,0},{5,1},{6,2},{7,3},{8,12},{9,13},{10,... | collective-permute-start | bytes 1572872 | tf_op jit(solution)/shard_map/ppermute | solution.py:63
  90.7 25.1 %collective-permute-start.25 = (bf16[2,512,256]{2,1,0:T(8,128)(2,1)S(1)}, bf16[2,512,256]{2,1,0:T(8,128)(2,1)S(1)}, u32[]{:S(2)}, u32[]{:S(2)}) collective-permute-start(bf16[2,512,256]{2,1,0:T(8,128)(2,1)S(1)} %get-tuple-element.68), channel_id=1, source_target_pairs={{0,2},{1,3},{2,0},{3,1},{4,6},{5,7},{6,4},{7,5},{8,10},{9,11},{10,... | collective-permute-start | bytes 1572872 | tf_op jit(solution)/shard_map/ppermute | solution.py:63
  98.1 21.1 %collective-permute-start.36 = (bf16[6,256,256]{2,1,0:T(8,128)(2,1)S(1)}, bf16[6,256,256]{2,1,0:T(8,128)(2,1)S(1)}, u32[]{:S(2)}, u32[]{:S(2)}) collective-permute-start(bf16[6,256,256]{2,1,0:T(8,128)(2,1)S(1)} %fusion.19), channel_id=1, source_target_pairs={{0,128},{128,0},{1,129},{129,1},{2,130},{130,2},{3,131},{131,3},{4... | collective-permute-start | bytes 2359304 | tf_op jit(solution)/shard_map/ppermute | solution.py:67
  108.3 7.4 %collective-permute-start.35 = (bf16[64,512]{1,0:T(8,128)(2,1)S(1)}, bf16[64,512]{1,0:T(8,128)(2,1)S(1)}, u32[]{:S(2)}, u32[]{:S(2)}) collective-permute-start(bf16[64,512]{1,0:T(8,128)(2,1)S(1)} %fusion.74), channel_id=1, source_target_pairs={{0,24},{1,25},{2,26},{3,27},{4,28},{5,29},{6,30},{7,31},{8,48},{9,... | collective-permute-start | bytes 196616 | tf_op jit(solution)/shard_map/ppermute | solution.py:63
  116.2 8.0 %collective-permute-start.29 = (bf16[2,512,128]{2,1,0:T(8,128)(2,1)S(1)}, bf16[2,512,128]{2,1,0:T(8,128)(2,1)S(1)}, u32[]{:S(2)}, u32[]{:S(2)}) collective-permute-start(bf16[2,512,128]{2,1,0:T(8,128)(2,1)S(1)} %select_convert_fusion.1), channel_id=1, source_target_pairs={{0,64},{1,65},{2,66},{3,67},{4,68},{5,69},{6,70},{7,71},{8,72},{9,... | collective-permute-start | bytes 786440 | tf_op jit(solution)/shard_map/ppermute | solution.py:63
  119.2 8.8 %collective-permute-start.38 = (bf16[64,512]{1,0:T(8,128)(2,1)S(1)}, bf16[64,512]{1,0:T(8,128)(2,1)S(1)}, u32[]{:S(2)}, u32[]{:S(2)}) collective-permute-start(bf16[64,512]{1,0:T(8,128)(2,1)S(1)} %add_convert_fusion.4), channel_id=1, source_target_pairs={{0,4},{1,5},{2,6},{3,7},{4,0},{5,1},{6,2},{7,3},{8,12},{9,13},{10,... | collective-permute-start | bytes 196616 | tf_op jit(solution)/shard_map/ppermute | solution.py:63
  124.4 19.3 %collective-permute-start.30 = (bf16[2,512,64]{2,1,0:T(8,128)(2,1)S(1)}, bf16[2,512,64]{2,1,0:T(8,128)(2,1)S(1)}, u32[]{:S(2)}, u32[]{:S(2)}) collective-permute-start(bf16[2,512,64]{2,1,0:T(8,128)(2,1)S(1)} %select_convert_fusion), channel_id=1, source_target_pairs={{0,32},{1,33},{2,34},{3,35},{4,36},{5,37},{6,38},{7,39},{8,40},{9,... | collective-permute-start | bytes 393224 | tf_op jit(solution)/shard_map/ppermute | solution.py:63
  127.4 10.1 %collective-permute-start.41 = (bf16[4,256,256]{2,1,0:T(8,128)(2,1)S(1)}, bf16[4,256,256]{2,1,0:T(8,128)(2,1)S(1)}, u32[]{:S(2)}, u32[]{:S(2)}) collective-permute-start(bf16[4,256,256]{2,1,0:T(8,128)(2,1)S(1)} %pad_maximum_fusion.2), channel_id=1, source_target_pairs={{0,128},{128,0},{1,129},{129,1},{2,130},{130,2},{3,131},{131,3},{4... | collective-permute-start | bytes 1572872 | tf_op jit(solution)/shard_map/ppermute | solution.py:67
  (31 other events, 131.7 us)
